TPU v7x, 256 devices: a whole 4x4x8 slice. The times are simulated.
256 devices in a mesh: seq: 32 (over x, y, core), head: 8 (over z).
Axes of the slice: x: 4, y: 4, z: 8, core: 2. Of those that a mesh axis runs over, the one named last changes fastest.
Arguments:
- queries: bfloat16 [16384, 4096], P('seq', 'head'), may hold values from -6 to 6
- keys: bfloat16 [16384, 4096], P('seq', 'head'), may hold values from -6 to 6
- values: bfloat16 [16384, 4096], P('seq', 'head'), may hold values from -6 to 6
- w_out: bfloat16 [4096, 4096], P(None, 'head'), may hold values from -0.125 to 0.125
- grad_out: bfloat16 [16384, 4096], P('seq', 'head'), may hold values from -6 to 6
Outputs:
- layer_out: bfloat16 [16384, 4096], P('seq', 'head')
- grad_queries: bfloat16 [16384, 4096], P('seq', 'head')
- grad_keys: bfloat16 [16384, 4096], P('seq', 'head')
- grad_values: bfloat16 [16384, 4096], P('seq', 'head')
- grad_w_out: float32 [4096, 4096], P('seq', 'head')
All inputs are finite; a program needn't handle non-finite values.
Results may differ from a plain program's by a relative error of at most 0.0051.
Values may be sent and summed in bfloat16 or wider, within the bound.
No kernel may reach another device: no remote copies, remote signals or barrier semaphores. Data moves between devices by JAX's collectives and lax.ppermute only.
A program may use at most 128 MiB of HBM per device.

v0:
```python
import jax
import jax.numpy as jnp
from jax import lax
from jax.sharding import PartitionSpec as P

DH = 128


epsilon = 1e-06


def prefix_2(part, axis, combine, identity, reverse):
    count = lax.axis_size(axis)
    place = lax.axis_index(axis)
    ahead = count - 1 - place if reverse else place
    gathered = lax.all_gather(part, axis)
    state = jnp.zeros_like(part) + jnp.asarray(identity, part.dtype)

    def one(hop, state):
        source = count - 1 - hop if reverse else hop
        return combine(state, lax.dynamic_index_in_dim(gathered, source, 0, False))

    return lax.fori_loop(0, ahead, one, state)


def product(form, left, right):
    return jnp.einsum(form, left, right, precision=lax.Precision.HIGHEST)


def plain_product(form, left, right):
    return jnp.einsum(form, left, right, preferred_element_type=jnp.float32)


def combine_sum(earlier, later_part):
    return earlier + later_part


def per_device(queries, keys, values, w_out, grad_out):
    length = queries.shape[0]
    feature_count = queries.shape[1]
    heads_dev = feature_count // DH
    query_half = queries.reshape(length, heads_dev, DH)
    key_half = keys.reshape(length, heads_dev, DH)
    value_half = values.reshape(length, heads_dev, DH)
    query_rows = query_half.astype(jnp.float32)
    key_rows = key_half.astype(jnp.float32)
    value_rows = value_half.astype(jnp.float32)
    causal = jnp.tril(jnp.ones((length, length), jnp.float32))
    zero_state = jnp.zeros((heads_dev, DH, DH), jnp.float32)
    local_state = plain_product("shd,she->hde", key_half, value_half)
    prefix = prefix_2(local_state, "seq", combine_sum, zero_state, False)
    scores = plain_product("thd,shd->hts", query_half, key_half) * causal
    mixed = product("hts,she->the", scores, value_rows) + product(
        "thd,hde->the", query_rows, prefix
    )
    inverse = lax.rsqrt(jnp.mean(mixed * mixed, axis=-1, keepdims=True) + epsilon)
    normed = mixed * inverse
    attn = normed.reshape(length, feature_count).astype(jnp.bfloat16)
    partial_terms = lax.dot_general(
        attn, w_out, (((1,), (1,)), ((), ())), preferred_element_type=jnp.float32
    )
    layer_out = lax.psum_scatter(partial_terms, "head", scatter_dimension=1, tiled=True).astype(
        jnp.bfloat16
    )
    grad_full = lax.all_gather(grad_out, "head", axis=1, tiled=True)
    d_attn = jnp.dot(grad_full, w_out, preferred_element_type=jnp.float32).reshape(
        length, heads_dev, DH
    )
    d_mixed = inverse * (d_attn - normed * jnp.mean(d_attn * normed, axis=-1, keepdims=True))
    grad_half = d_mixed.astype(jnp.bfloat16)
    grad_mixed = grad_half.astype(jnp.float32)
    local_grads = plain_product("thd,the->hde", query_half, grad_half)
    later_grads = prefix_2(local_grads, "seq", combine_sum, zero_state, True)
    grad_scores = plain_product("the,she->hts", grad_half, value_half) * causal
    grad_query = product("hts,shd->thd", grad_scores, key_rows) + product(
        "the,hde->thd", grad_mixed, prefix
    )
    grad_key = product("hts,thd->shd", grad_scores, query_rows) + product(
        "she,hde->shd", value_rows, later_grads
    )
    grad_value = product("hts,the->she", scores, grad_mixed) + product(
        "shd,hde->she", key_rows, later_grads
    )
    grad_w_out = lax.psum_scatter(
        lax.dot_general(
            grad_full, attn, (((0,), (0,)), ((), ())), preferred_element_type=jnp.float32
        ),
        "seq",
        scatter_dimension=0,
        tiled=True,
    )
    return (
        layer_out,
        grad_query.reshape(length, feature_count).astype(jnp.bfloat16),
        grad_key.reshape(length, feature_count).astype(jnp.bfloat16),
        grad_value.reshape(length, feature_count).astype(jnp.bfloat16),
        grad_w_out,
    )


def solution(mesh):
    return jax.shard_map(
        per_device,
        mesh=mesh,
        in_specs=(
            P("seq", "head"),
            P("seq", "head"),
            P("seq", "head"),
            P(None, "head"),
            P("seq", "head"),
        ),
        out_specs=(
            P("seq", "head"),
            P("seq", "head"),
            P("seq", "head"),
            P("seq", "head"),
            P("seq", "head"),
        ),
        check_vma=False,
    )
```

profile of v0, /device:TPU:1, one launch (start us, length us, event | category | flops | bytes accessed | tf_op | source)
XLA Modules:
  0.0 407.5 jit_solution(6903677644800149251)
XLA Ops:
  7.3 1.4 copy.99
  10.6 2.7 fusion.51
  13.3 60.0 %all-gather.8.cloned.1.call-done = f32[128,128,128]{2,1,0:T(8,128)} async-done(((f32[4,128,128]{2,1,0:T(8,128)}), f32[128,128,128]{2,1,0:T(8,128)}) %all-gather.8.cloned.1.call-update) | async-done | bytes 8388624 | tf_op jit(solution)/shard_map/all_gather | solution.py:16
  73.4 1.0 while.22
  75.0 4.8 %multiply_reduce_fusion.1 = (f32[512,4]{0,1:T(4,128)S(1)}, f32[512,4,128]{0,2,1:T(8,128)S(1)}) fusion(f32[512,4,128]{0,2,1:T(8,128)S(1)} %convolution_bitcast_fusion.3, f32[4,512,512]{2,1,0:T(8,128)} %fusion.51, f32[512,512]{1,0:T(8,128)S(1)} %fusion.42, bf16[512,512]{1,0:T(8,128)(2,1)S(1)} %copy-done), kind=kOutput, calls=%fused_computation.31 | convolution fusion | flops 1612445696 | bytes 7872512 | tf_op jit(solution)/shard_map/hts,she->the/dot_general | solution.py:27
  79.9 49.3 %all-gather.6.cloned.1.call-done = bf16[512,4096]{1,0:T(8,128)(2,1)} async-done(((bf16[512,512]{1,0:T(8,128)(2,1)}), bf16[512,4096]{1,0:T(8,128)(2,1)}) %all-gather.6.cloned.1.call-update) | async-done | bytes 4194320 | tf_op jit(solution)/shard_map/all_gather | solution.py:65
  129.2 6.0 %multiply_reduce_fusion = (f32[512,4]{0,1:T(4,128)S(1)}, f32[512,512]{0,1:T(8,128)S(1)}) fusion(f32[512,4,128]{0,2,1:T(8,128)S(1)} %get-tuple-element.119, f32[512,4]{0,1:T(4,128)S(1)} %add_rsqrt_fusion, bf16[512,4096]{1,0:T(8,128)(2,1)} %all-gather.6.cloned.1.call-done, bf16[4096,512]{1,0:T(8,128)(2,1)} %param.12), kind=kOutput, calls=%fused_computation.30 | convolution fusion | flops 2148268032 | bytes 10502144 | tf_op jit(solution)/shard_map/dot_general | solution.py:66
  136.3 5.6 %convolution_bitcast_fusion = f32[4096,512]{0,1:T(8,128)} fusion(bf16[512,512]{0,1:T(8,128)(2,1)S(1)} %bitcast.122, bf16[512,4096]{1,0:T(8,128)(2,1)S(1)} %copy-done.2), kind=kOutput, calls=%fused_computation.2 | convolution fusion | flops 2147483648 | bytes 13107200 | tf_op jit(solution)/shard_map/dot_general | solution.py:85
  143.9 1.8 copy.44
  146.0 7.8 %fusion.67 = f32[512,4096]{1,0:T(8,128)} fusion(bf16[512,512]{0,1:T(8,128)(2,1)S(1)} %bitcast.123, bf16[4096,512]{1,0:T(8,128)(2,1)} %param.12), kind=kOutput, calls=%fused_computation.61 | convolution fusion | flops 2147483648 | bytes 13107200 | tf_op jit(solution)/shard_map/dot_general | solution.py:59
  155.2 1.9 copy-done.1
  157.2 3.5 fusion.36
  160.6 2.1 copy.48
  162.8 76.6 %reduce-scatter.5.cloned.1.call-done = f32[128,512]{0,1:T(8,128)} async-done(((f32[4096,512]{0,1:T(8,128)}), f32[128,512]{0,1:T(8,128)}) %reduce-scatter.5.cloned.1.call-update) | async-done | bytes 262160 | tf_op jit(solution)/shard_map/reduce_scatter | solution.py:84
  239.3 1.8 copy.51
  241.1 61.0 %all-gather.10.cloned.1.call-done = f32[128,128,128]{2,1,0:T(8,128)} async-done(((f32[4,128,128]{2,1,0:T(8,128)}), f32[128,128,128]{2,1,0:T(8,128)}) %all-gather.10.cloned.1.call-update) | async-done | bytes 8388624 | tf_op jit(solution)/shard_map/all_gather | solution.py:16
  302.1 31.1 %while.23 = (s32[]{:T(128)}, f32[4,128,128]{2,1,0:T(8,128)S(1)}, s32[]{:T(128)}, f32[32,4,128,128]{3,2,1,0:T(8,128)}, s32[]{:T(128)}, /*index=5*/s32[]{:T(128)}, s32[]{:T(128)}, s32[]{:T(128)}) while((s32[]{:T(128)}, f32[4,128,128]{2,1,0:T(8,128)S(1)}, s32[]{:T(128)}, f32[32,4,128,128]{3,2,1,0:T(8,128)}, s32[]{:T(128)}, /*index=5*/s32[]{:T(128)}, ...), condition=%wide.region_6.7_spmd, body=%wide.region_5.6_spmd.sunk | while | flops 65542 | bytes 786575 | solution.py:23
  314.5 1.1 bitcast_add_fusion.5
  315.6 1.1 bitcast_add_fusion.5
  322.9 1.0 bitcast_add_fusion.5
  333.9 4.0 fusion.39
  339.5 4.1 %fusion.33 = bf16[512,4,128]{0,2,1:T(8,128)(2,1)S(1)} fusion(f32[512,4,128]{0,2,1:T(8,128)S(1)} %convolution_bitcast_fusion.1, f32[4,512,512]{2,1,0:T(8,128)} %copy-done.1, f32[512,512]{1,0:T(8,128)S(1)} %fusion.42, bf16[512,512]{1,0:T(8,128)(2,1)S(1)} %copy-done.4), kind=kOutput, calls=%fused_computation.25 | convolution fusion | flops 1612185600 | bytes 7340032 | tf_op jit(solution)/shard_map/hts,thd->shd/dot_general | solution.py:27
  344.6 54.3 %reduce-scatter.3.cloned.1.call-done = f32[512,512]{1,0:T(8,128)} async-done(((f32[512,4096]{1,0:T(8,128)}), f32[512,512]{1,0:T(8,128)}) %reduce-scatter.3.cloned.1.call-update) | async-done | bytes 1048592 | tf_op jit(solution)/shard_map/reduce_scatter | solution.py:62
  398.9 2.1 convert_element_type.39
  (74 shorter events, 38.9 us)
Async XLA Ops:
  7.2 1.5 copy-start
  7.2 3.4 copy-start.7
  7.2 3.4 copy-start.3
  7.2 66.1 %all-gather.8.cloned.1.call-start = ((), (), s32[]{:S(2)}) async-start(), calls=%async_computation.5 | async-start | bytes 8650752 | tf_op jit(solution)/shard_map/all_gather | solution.py:16
  8.6 1.9 copy-start.5
  9.7 119.6 %all-gather.6.cloned.1.call-start = ((), (), s32[]{:S(2)}) async-start(), calls=%async_computation.3 | async-start | bytes 4718592 | tf_op jit(solution)/shard_map/all_gather | solution.py:65
  10.4 228.9 %reduce-scatter.5.cloned.1.call-start = ((), (), s32[]{:S(2)}) async-start(), calls=%async_computation.4 | async-start | bytes 8650752 | tf_op jit(solution)/shard_map/reduce_scatter | solution.py:84
  129.2 7.1 %copy-start.2 = (bf16[512,4096]{1,0:T(8,128)(2,1)S(1)}, bf16[512,4096]{1,0:T(8,128)(2,1)}, u32[]{:S(2)}) copy-start(bf16[512,4096]{1,0:T(8,128)(2,1)} %all-gather.6.cloned.1.call-done) | copy-start | bytes 12582916
  135.5 0.8 copy-start.9
  141.9 1.0 copy-start.4
  141.9 4.1 %copy-start.10 = (bf16[512,4,128]{0,2,1:T(8,128)(2,1)S(1)}, bf16[512,4,128]{0,2,1:T(8,128)(2,1)}, u32[]{:S(2)}) copy-start(bf16[512,4,128]{0,2,1:T(8,128)(2,1)} %copy-done.9) | copy-start | bytes 1572868
  141.9 160.2 %all-gather.10.cloned.1.call-start = ((), (), s32[]{:S(2)}) async-start(), calls=%async_computation.6 | async-start | bytes 8650752 | tf_op jit(solution)/shard_map/all_gather | solution.py:16
  145.8 253.1 %reduce-scatter.3.cloned.1.call-start = ((), (), s32[]{:S(2)}) async-start(), calls=%async_computation.2 | async-start | bytes 9437184 | tf_op jit(solution)/shard_map/reduce_scatter | solution.py:62
  153.9 3.3 copy-start.6
  155.2 1.9 copy-start.1
  160.6 172.6 %copy-start.8 = (bf16[512,512]{1,0:T(8,128)(2,1)S(1)}, bf16[512,512]{1,0:T(8,128)(2,1)}, u32[]{:S(2)}) copy-start(bf16[512,512]{1,0:T(8,128)(2,1)} %param.10) | copy-start | bytes 1572868
Sparse Core Ops, SparseCore 0:
  11.2 62.1 all-gather.7
  75.1 54.0 all-gather.5
  142.1 97.2 reduce-scatter.4
  242.6 59.4 all-gather.9
  304.7 94.1 reduce-scatter.2
where the time goes:
time: 409 us; the launch traced here: 407 us
  waiting for transfers between devices  302 us (74%)
  matrix products  43.6 us (11%)
  other arithmetic  34 us (8%)
  between operations  14 us (3%)
  local copies, waits for them, and re-layouts  12.8 us (3%)
    all_gather x2, waiting for transfers between devices, prefix_2(): gathered = lax.all_gather(part, axis)  121 us
    reduce_scatter x1, waiting for transfers between devices, per_device(): lax.psum_scatter(lax.dot_general(grad_full, attn, (((0,), (0,)), ((), ())...  76.6 us
    reduce_scatter x1, waiting for transfers between devices, per_device(): lax.psum_scatter(partial_terms, 'head', scatter_dimension=1, tiled=True)  54.3 us
    all_gather x1, waiting for transfers between devices, per_device(): grad_full = lax.all_gather(grad_out, 'head', axis=1, tiled=True)  49.3 us
    add x31, other arithmetic, combine_sum(): return earlier + later_part  31.5 us
    dot_general x8, matrix products, product(): return jnp.einsum(form, left, right, precision=lax.Precision.HIGHEST)  18.7 us
    unnamed x26, local copies, waits for them, and re-layouts  9.66 us
  transfers between devices with their start and end apart: 5, of which 5 were waited for; matrix products, arithmetic and copies ran while one was open for 17% of the time, Pallas kernels for 0%

commit v1 on v0

v1 whole, which is shorter than its diff:
```python
import functools

import jax
import jax.numpy as jnp
from jax import lax
from jax.experimental import pallas as pl
from jax.experimental.pallas import tpu as pltpu
from jax.sharding import PartitionSpec as P

DH = 128
epsilon = 1e-06
MIB = 1 << 20
bf16, f32 = jnp.bfloat16, jnp.float32


def dot(a, b, left, right):
    return lax.dot_general(a, b, (((left,), (right,)), ((), ())), preferred_element_type=f32)


def split(x):
    high = x.astype(bf16)
    return high, (x - high.astype(f32)).astype(bf16)


def dot2(parts, b, left, right):
    return dot(parts[0], b, left, right) + dot(parts[1], b, left, right)


def dot2r(a, parts, left, right):
    return dot(a, parts[0], left, right) + dot(a, parts[1], left, right)


def shape(dims, dtype):
    return jax.ShapeDtypeStruct(dims, dtype)


def call(body, outs, args, name, flops, scalars=0, vmem=40):
    in_specs = [pl.BlockSpec(memory_space=pltpu.SMEM)] * scalars
    in_specs += [pl.BlockSpec(memory_space=pltpu.VMEM)] * (len(args) - scalars)
    size = sum(a.size * a.dtype.itemsize for a in list(args) + list(outs))
    return pl.pallas_call(
        body,
        out_shape=tuple(outs),
        in_specs=in_specs,
        out_specs=tuple([pl.BlockSpec(memory_space=pltpu.VMEM)] * len(outs)),
        compiler_params=pltpu.CompilerParams(vmem_limit_bytes=vmem * MIB),
        cost_estimate=pl.CostEstimate(flops=flops, bytes_accessed=size, transcendentals=0),
        name=name,
    )(*args)


def head(i):
    return slice(i * DH, (i + 1) * DH)


def state_body(left, right, out):
    for h in range(out.shape[0]):
        out[h] = dot(left[:, head(h)], right[:, head(h)], 0, 0)


def prefix_body(reverse, parts, out):
    count = parts.shape[0]
    state = jnp.zeros(parts.shape[1:], f32)
    for step in range(count):
        i = count - 1 - step if reverse else step
        out[i] = state
        state = state + parts[i]


def lower_mask(rows):
    return lax.broadcasted_iota(jnp.int32, (rows, rows), 0) >= lax.broadcasted_iota(
        jnp.int32, (rows, rows), 1
    )


def forward_body(q, k, v, prefix, attn, attn_t, mixed_out):
    rows = q.shape[0]
    mask = lower_mask(rows)
    for h in range(prefix.shape[0]):
        qh, kh, vh = q[:, head(h)], k[:, head(h)], v[:, head(h)]
        scores = split(jnp.where(mask, dot(qh, kh, 1, 1), 0.0))
        mixed = dot2(scores, vh, 1, 0) + dot2r(qh, split(prefix[h]), 1, 0)
        inverse = lax.rsqrt(jnp.mean(mixed * mixed, axis=-1, keepdims=True) + epsilon)
        normed = mixed * inverse
        mixed_out[:, head(h)] = mixed
        attn[:, head(h)] = normed.astype(bf16)
        attn_t[head(h), :] = normed.T.astype(bf16)


def project_body(offsets, me, w, mixed, q, *rest):
    blocks, (d_mixed, grads) = rest[:-2], rest[-2:]
    ring = w.shape[0] // w.shape[1]
    wide = w.shape[1]
    half = q.shape[0] // 2
    top = bottom = None
    for block, (offset, part) in zip(blocks, offsets):
        source = lax.rem(me[0] + offset, ring)
        weight = w[pl.ds(pl.multiple_of(source * wide, wide), wide), :]
        if part != 1:
            term = dot(block[0:half, :], weight, 1, 0)
            top = term if top is None else top + term
        if part != 0:
            rows = block[half:, :] if part == 2 else block[...]
            term = dot(rows, weight, 1, 0)
            bottom = term if bottom is None else bottom + term
    for h in range(grads.shape[0]):
        total = None
        for place, d_part in ((slice(0, half), top), (slice(half, 2 * half), bottom)):
            d_attn = d_part[:, head(h)]
            m = mixed[place, head(h)]
            inverse = lax.rsqrt(jnp.mean(m * m, axis=-1, keepdims=True) + epsilon)
            normed = m * inverse
            d_m = inverse * (d_attn - normed * jnp.mean(d_attn * normed, axis=-1, keepdims=True))
            d_m = d_m.astype(bf16)
            d_mixed[place, head(h)] = d_m
            term = dot(q[place, head(h)], d_m, 0, 0)
            total = term if total is None else total + term
        grads[h] = total


def backward_body(q, k, v, d_mixed, prefix, later, grad_q, grad_k, grad_v):
    rows = q.shape[0]
    low = lower_mask(rows)
    high = lax.broadcasted_iota(jnp.int32, (rows, rows), 0) <= lax.broadcasted_iota(
        jnp.int32, (rows, rows), 1
    )
    for h in range(prefix.shape[0]):
        qh, kh, vh, dh = q[:, head(h)], k[:, head(h)], v[:, head(h)], d_mixed[:, head(h)]
        before, after = split(prefix[h]), split(later[h])
        d_scores = split(jnp.where(low, dot(dh, vh, 1, 1), 0.0))
        grad_q[:, head(h)] = (dot2(d_scores, kh, 1, 0) + dot2r(dh, before, 1, 1)).astype(bf16)
        d_scores_t = split(jnp.where(high, dot(vh, dh, 1, 1), 0.0))
        grad_k[:, head(h)] = (dot2(d_scores_t, qh, 1, 0) + dot2r(vh, after, 1, 1)).astype(bf16)
        scores_t = split(jnp.where(high, dot(kh, qh, 1, 1), 0.0))
        grad_v[:, head(h)] = (dot2(scores_t, dh, 1, 0) + dot2r(kh, after, 1, 0)).astype(bf16)


def weight_body(offsets, ring, me, attn_t, *rest):
    blocks, (keep, send) = rest[:-2], rest[-2:]
    half = attn_t.shape[1] // 2
    wide = 128
    first = me[1] == 0
    for blocks_of, offset in offsets:
        source = lax.rem(me[0] + offset, ring)
        if len(blocks_of) == 1:
            terms = dot(attn_t[...], blocks[blocks_of[0]][...], 1, 0)
        else:
            terms = dot(attn_t[:, 0:half], blocks[blocks_of[0]][...], 1, 0) + dot(
                attn_t[:, half:], blocks[blocks_of[1]][...], 1, 0
            )
        for j in range(terms.shape[1] // (2 * wide)):
            even = terms[:, 2 * j * wide : (2 * j + 1) * wide]
            odd = terms[:, (2 * j + 1) * wide : (2 * j + 2) * wide]
            place = source * (terms.shape[1] // (2 * wide)) + j
            keep[place] = jnp.where(first, even, odd)
            send[place] = jnp.where(first, odd, even).astype(bf16)


def sum_body(parts, out):
    total = parts[0].astype(f32)
    for i in range(1, parts.shape[0]):
        total = total + parts[i].astype(f32)
    out[...] = total.T


def first_body(me, attn, w, top, bottom):
    half = attn.shape[0] // 2
    terms = dot(attn[...], w[...], 1, 1).astype(bf16)
    top[...] = terms[0:half]
    bottom[...] = terms[half:]


def step_body(me, attn, w, from_left, from_right, to_right, to_left):
    half = attn.shape[0] // 2
    terms = dot(attn[...], w[...], 1, 1)

    def put(source, target, top):
        if source.shape[0] == target.shape[0]:
            target[...] = (terms + source[...].astype(f32)).astype(bf16)
        else:
            place, other = slice(0, half), slice(half, 2 * half)
            if not top:
                place, other = other, place
            target[place, :] = (terms[place] + source[...].astype(f32)).astype(bf16)
            target[other, :] = terms[other].astype(bf16)

    @pl.when(pl.program_id(0) == 0)
    def _():
        put(from_left, to_right, True)

    @pl.when(pl.program_id(0) == 1)
    def _():
        put(from_right, to_left, False)


def last_body(me, attn, w, from_left, from_right, out):
    terms = dot(attn[...], w[...], 1, 1)
    out[...] = (terms + from_left[...].astype(f32) + from_right[...].astype(f32)).astype(bf16)


def ring_call(body, outs, me, attn, w, rest, offsets, name):
    ring = w.shape[0] // attn.shape[0]
    wide = w.shape[0] // ring

    def whole(a):
        return pl.BlockSpec(a.shape, lambda i, me: (0,) * len(a.shape))

    def weight(i, me):
        offset = offsets[0] if len(offsets) == 1 else jnp.where(i == 0, offsets[0], offsets[1])
        return (lax.rem(me[0] + offset, ring), 0)

    size = attn.size * (len(rest) + len(outs) + len(offsets) + 1) * 2
    return pl.pallas_call(
        body,
        grid_spec=pltpu.PrefetchScalarGridSpec(
            num_scalar_prefetch=1,
            grid=(len(offsets),),
            in_specs=[whole(attn), pl.BlockSpec((wide, w.shape[1]), weight)]
            + [whole(a) for a in rest],
            out_specs=tuple(whole(o) for o in outs),
        ),
        out_shape=tuple(outs),
        compiler_params=pltpu.CompilerParams(vmem_limit_bytes=24 * MIB),
        cost_estimate=pl.CostEstimate(
            flops=2 * attn.size * wide * len(offsets), bytes_accessed=size, transcendentals=0
        ),
        name=name,
    )(me, attn, w, *rest)


def shift(x, axis, amount):
    count = lax.axis_size(axis)
    return lax.ppermute(x, axis, [(i, (i + amount) % count) for i in range(count)])


def across(state, reverse, name):
    count = lax.axis_size("seq")
    dims = state.shape
    parts = state.reshape(count, -1, dims[-1])
    parts = lax.all_to_all(parts, "seq", 0, 0, tiled=True)
    (sums,) = call(
        functools.partial(prefix_body, reverse), [shape(parts.shape, f32)], [parts], name, parts.size
    )
    sums = lax.all_to_all(sums, "seq", 0, 0, tiled=True)
    return sums.reshape(dims)


def per_device(queries, keys, values, w_out, grad_out):
    length, features = queries.shape
    heads = features // DH
    half = length // 2
    ring = lax.axis_size("head")
    count = lax.axis_size("seq")
    me = jnp.stack([lax.axis_index("head"), lax.rem(lax.axis_index("seq"), 2)]).astype(jnp.int32)
    block = shape((length, features), bf16)
    half_block = shape((half, features), bf16)
    states = shape((heads, DH, DH), f32)
    pair_flops = 2 * length * features * DH

    right = left = grad_out
    blocks, offsets = [grad_out], [(0, 2)]
    for hop in range(1, ring // 2):
        right, left = shift(right, "head", 1), shift(left, "head", -1)
        blocks += [right, left]
        offsets += [(ring - hop, 2), (hop, 2)]
    top, bottom = shift(right[:half], "head", 1), shift(left[half:], "head", -1)
    blocks += [top, bottom]
    offsets += [(ring // 2, 0), (ring // 2, 1)]

    (local_state,) = call(state_body, [states], [keys, values], "state", pair_flops)
    prefix = across(local_state, False, "prefix")
    attn, attn_t, mixed = call(
        forward_body,
        [block, shape((features, length), bf16), shape((length, features), f32)],
        [queries, keys, values, prefix],
        "forward",
        12 * pair_flops,
    )

    to_right, to_left = ring_call(
        first_body, [half_block, half_block], me, attn, w_out, [], [ring // 2], "out_first"
    )
    for hop in range(ring // 2 - 1, 0, -1):
        from_left, from_right = shift(to_right, "head", 1), shift(to_left, "head", -1)
        to_right, to_left = ring_call(
            step_body,
            [block, block],
            me,
            attn,
            w_out,
            [from_left, from_right],
            [hop, ring - hop],
            "out_step",
        )
    from_left, from_right = shift(to_right, "head", 1), shift(to_left, "head", -1)
    (layer_out,) = ring_call(
        last_body, [block], me, attn, w_out, [from_left, from_right], [0], "out_last"
    )

    d_mixed, local_grads = call(
        functools.partial(project_body, offsets),
        [block, states],
        [me, w_out, mixed, queries] + blocks,
        "project",
        2 * length * features * features * ring,
        scalars=1,
    )
    later = across(local_grads, True, "suffix")
    grad_q, grad_k, grad_v = call(
        backward_body,
        [block, block, block],
        [queries, keys, values, d_mixed, prefix, later],
        "backward",
        36 * pair_flops,
    )

    grouped = [([i], offsets[i][0]) for i in range(ring - 1)] + [([ring - 1, ring], ring // 2)]
    pieces = (count // 2, features, w_out.shape[0] // count)
    keep, send = call(
        functools.partial(weight_body, grouped, ring),
        [shape(pieces, f32), shape(pieces, bf16)],
        [me, attn_t] + blocks,
        "weight",
        2 * length * features * features * ring,
        scalars=1,
    )
    received = lax.ppermute(send, "seq", [(i, i ^ 1) for i in range(count)])
    both = (keep + received.astype(f32)).astype(bf16)
    groups = [[2 * chip + core for chip in range(count // 2)] for core in range(2)]
    terms = lax.all_to_all(both, "seq", 0, 0, axis_index_groups=groups, tiled=True)
    (grad_w_out,) = call(
        sum_body, [shape((pieces[2], pieces[1]), f32)], [terms], "weight_sum", terms.size
    )
    return layer_out, grad_q, grad_k, grad_v, grad_w_out


def solution(mesh):
    return jax.shard_map(
        per_device,
        mesh=mesh,
        in_specs=(
            P("seq", "head"),
            P("seq", "head"),
            P("seq", "head"),
            P(None, "head"),
            P("seq", "head"),
        ),
        out_specs=(
            P("seq", "head"),
            P("seq", "head"),
            P("seq", "head"),
            P("seq", "head"),
            P("seq", "head"),
        ),
        check_vma=False,
    )
```

time: 409 us -> 178 us (0.44)
  waiting for transfers between devices: 302 us -> 56 us
  starting transfers between devices: 0.38 us -> 48.1 us
  matrix products: 43.6 us -> 0 us
  Pallas kernels: 0 us -> 33 us
  other arithmetic: 34 us -> 4.87 us
  blocking collectives: 0 us -> 18.6 us
  between operations: 14 us -> 0.91 us
    all_gather x3 -> x0, waiting for transfers between devices: 170 us -> none  [the longest x2 121 us: prefix_2(): gathered = lax.all_gather(part, axis)]
    reduce_scatter x2 -> x0, waiting for transfers between devices: 131 us -> none  [the longest x1 76.6 us: per_device(): lax.psum_scatter(lax.dot_general(grad_full, attn, (((0,), (0,)), ((), ())...]
    ppermute x0 -> x17, waiting for transfers between devices: none -> 44.8 us  [the longest x16 44.8 us: shift(): lax.ppermute(x, axis, [(i, (i + amount) % count) for i in range(count)])]
    dot_general x15 -> x0, matrix products: 43.6 us -> none  [the longest x8 18.7 us: product(): return jnp.einsum(form, left, right, precision=lax.Precision.HIGHEST)]
    pallas_call x0 -> x13, Pallas kernels: none -> 33 us  [the longest x8 23.3 us: call(): pl.pallas_call(body, out_shape=tuple(outs), in_specs=in_specs, out_specs=...]
    add x31 -> x0, other arithmetic: 31.5 us -> none  [combine_sum(): return earlier + later_part]
    ppermute x0 -> x17, starting transfers between devices: none -> 27.3 us  [the longest x16 27.1 us: shift(): lax.ppermute(x, axis, [(i, (i + amount) % count) for i in range(count)])]
    all_to_all x0 -> x4, starting transfers between devices: none -> 20.8 us  [the longest x2 9.96 us: across(): sums = lax.all_to_all(sums, 'seq', 0, 0, tiled=True)]
  transfers between devices with their start and end apart: 5 -> 21, of which waited for: 5 -> 8; matrix products, arithmetic and copies ran while one was open for 17% -> 4% of each run, Pallas kernels for 0% -> 15%
where the time goes in v1:
time: 178 us; the launch traced here: 177 us
  waiting for transfers between devices  56 us (31%)
  starting transfers between devices  48.1 us (27%)
  Pallas kernels  33 us (19%)
  blocking collectives  18.6 us (10%)
  local copies, waits for them, and re-layouts  15.3 us (9%)
  other arithmetic  4.87 us (3%)
    ppermute x16, waiting for transfers between devices, shift(): lax.ppermute(x, axis, [(i, (i + amount) % count) for i in range(count)])  44.8 us
    ppermute x16, starting transfers between devices, shift(): lax.ppermute(x, axis, [(i, (i + amount) % count) for i in range(count)])  27.1 us
    pallas_call x8, Pallas kernels, call(): pl.pallas_call(body, out_shape=tuple(outs), in_specs=in_specs, out_specs=...  23.3 us
    all_to_all x1, blocking collectives, across(): parts = lax.all_to_all(parts, 'seq', 0, 0, tiled=True)  18.6 us
    unnamed x40, local copies, waits for them, and re-layouts  13.9 us
    all_to_all x2, starting transfers between devices, across(): sums = lax.all_to_all(sums, 'seq', 0, 0, tiled=True)  9.96 us
    pallas_call x5, Pallas kernels, ring_call(): pl.pallas_call(body, grid_spec=pltpu.PrefetchScalarGridSpec(num_scalar_pr...  9.69 us
    all_to_all x2, waiting for transfers between devices, across(): sums = lax.all_to_all(sums, 'seq', 0, 0, tiled=True)  8.8 us
  transfers between devices with their start and end apart: 21, of which 8 were waited for; matrix products, arithmetic and copies ran while one was open for 4% of the time, Pallas kernels for 15%

profile of v1, /device:TPU:1, one launch (start us, length us, event | category | flops | bytes accessed | tf_op | source)
XLA Modules:
  0.0 176.8 jit_solution(12499627097546918556)
XLA Ops:
  0.6 6.5 %collective-permute-start.9 = (bf16[512,512]{1,0:T(8,128)(2,1)}, bf16[512,512]{1,0:T(8,128)(2,1)S(1)}, u32[]{:S(2)}, u32[]{:S(2)}) collective-permute-start(bf16[512,512]{1,0:T(8,128)(2,1)} %rest_0_.3), channel_id=1, source_target_pairs={{0,7},{1,0},{2,1},{3,2},{4,3},{5,4},{6,5},{7,6},{8,15},{9,8},{10,9... | collective-permute-start | bytes 1572872 | tf_op jit(solution)/shard_map/ppermute | solution.py:233
  7.1 10.9 %collective-permute-done.9.rest_2_ = bf16[512,512]{1,0:T(8,128)(2,1)S(1)} collective-permute-done((bf16[512,512]{1,0:T(8,128)(2,1)}, bf16[512,512]{1,0:T(8,128)(2,1)S(1)}, u32[]{:S(2)}, u32[]{:S(2)}) %collective-permute-start.9) | collective-permute-done | bytes 524320 | tf_op jit(solution)/shard_map/ppermute | solution.py:233
  18.0 3.3 %collective-permute-start.11 = (bf16[512,512]{1,0:T(8,128)(2,1)S(1)}, bf16[512,512]{1,0:T(8,128)(2,1)S(1)}, u32[]{:S(2)}, u32[]{:S(2)}) collective-permute-start(bf16[512,512]{1,0:T(8,128)(2,1)S(1)} %collective-permute-done.9.rest_2_), channel_id=1, source_target_pairs={{0,7},{1,0},{2,1},{3,2},{4,3},{5,4},{6,5},{7,6},{8,15},{9,8},{10,9... | collective-permute-start | bytes 1572872 | tf_op jit(solution)/shard_map/ppermute | solution.py:233
  22.1 8.9 %collective-permute-done.11.rest_4_ = bf16[512,512]{1,0:T(8,128)(2,1)S(1)} collective-permute-done((bf16[512,512]{1,0:T(8,128)(2,1)S(1)}, bf16[512,512]{1,0:T(8,128)(2,1)S(1)}, u32[]{:S(2)}, u32[]{:S(2)}) %collective-permute-start.11) | collective-permute-done | bytes 524320 | tf_op jit(solution)/shard_map/ppermute | solution.py:233
  31.0 3.4 %collective-permute-start.13 = (bf16[512,512]{1,0:T(8,128)(2,1)S(1)}, bf16[512,512]{1,0:T(8,128)(2,1)S(1)}, u32[]{:S(2)}, u32[]{:S(2)}) collective-permute-start(bf16[512,512]{1,0:T(8,128)(2,1)S(1)} %collective-permute-done.11.rest_4_), channel_id=1, source_target_pairs={{0,7},{1,0},{2,1},{3,2},{4,3},{5,4},{6,5},{7,6},{8,15},{9,8},{10,9... | collective-permute-start | bytes 1572872 | tf_op jit(solution)/shard_map/ppermute | solution.py:233
  36.9 18.6 %all_to_all.25.parts = f32[32,16,128]{2,1,0:T(8,128)S(1)} all-to-all(f32[32,16,128]{2,1,0:T(8,128)S(1)} %bitcast.6), channel_id=1, replica_groups=mesh['seq'=32,'head'=8] {'seq'}, dimensions={0} | all-to-all | bytes 524288 | tf_op jit(solution)/shard_map/all_to_all | solution.py:240
  56.2 4.4 %all-to-all-start.1 = ((f32[32,16,128]{2,1,0:T(8,128)}), f32[32,16,128]{2,1,0:T(8,128)}, u32[]{:S(2)}, u32[]{:S(2)}) async-start(f32[32,16,128]{2,1,0:T(8,128)} %prefix.1), calls=%async_computation.1 | async-start | bytes 524288 | tf_op jit(solution)/shard_map/all_to_all | solution.py:244
  61.4 3.0 %collective-permute-start.15 = (bf16[256,512]{1,0:T(8,128)(2,1)}, bf16[256,512]{1,0:T(8,128)(2,1)S(1)}, u32[]{:S(2)}, u32[]{:S(2)}) collective-permute-start(bf16[256,512]{1,0:T(8,128)(2,1)} %slice.9), channel_id=1, source_target_pairs={{0,7},{1,0},{2,1},{3,2},{4,3},{5,4},{6,5},{7,6},{8,15},{9,8},{10,9... | collective-permute-start | bytes 786440 | tf_op jit(solution)/shard_map/ppermute | solution.py:233
  65.1 4.6 %all-to-all-done.1 = f32[32,16,128]{2,1,0:T(8,128)} async-done(((f32[32,16,128]{2,1,0:T(8,128)}), f32[32,16,128]{2,1,0:T(8,128)}, u32[]{:S(2)}, u32[]{:S(2)}) %all-to-all-start.1) | async-done | bytes 262176 | tf_op jit(solution)/shard_map/all_to_all | solution.py:244
  71.8 3.3 %forward.1 = (bf16[512,512]{1,0:T(8,128)(2,1)S(1)}, bf16[512,512]{1,0:T(8,128)(2,1)S(1)}, f32[512,512]{1,0:T(8,128)S(1)}) custom-call(bf16[512,512]{1,0:T(8,128)(2,1)S(1)} %copy-done.6, bf16[512,512]{1,0:T(8,128)(2,1)S(1)} %copy-done.12, bf16[512,512]{1,0:T(8,128)(2,1)S(1)} %copy-done.15, f32[4,128,128]{2,1,0:T(8,128)} %bitcast.3.prefix), custom_call_target="tpu_custom_call" | custom-call | flops 805306368 | bytes 3932160 | tf_op jit(solution)/shard_map/forward/pallas_call | solution.py:41
  76.2 5.0 %weight.1 = (f32[16,512,128]{2,1,0:T(8,128)S(1)}, bf16[16,512,128]{2,1,0:T(8,128)(2,1)}) custom-call(s32[2]{0:T(128)S(1)} %pad_add_fusion.me, bf16[512,512]{1,0:T(8,128)(2,1)S(1)} %get-tuple-element.38.attn_t, bf16[512,512]{1,0:T(8,128)(2,1)S(1)} %copy-done.5, bf16[512,512]{1,0:T(8,128)(2,1)S(1)} %copy-done.8, ...), custom_call_target="tpu_custom_call" | custom-call | flops 2147483648 | bytes 11010056 | tf_op jit(solution)/shard_map/weight/pallas_call | solution.py:41
  83.4 4.3 %project.1 = (bf16[512,512]{1,0:T(8,128)(2,1)S(1)}, f32[4,128,128]{2,1,0:T(8,128)S(1)}) custom-call(s32[2]{0:T(128)S(1)} %pad_add_fusion.me, bf16[4096,512]{1,0:T(8,128)(2,1)S(1)} %copy-done, f32[512,512]{1,0:T(8,128)S(1)} %get-tuple-element.32.mixed, bf16[512,512]{1,0:T(8,128)(2,1)S(1)} %copy-done.6, bf16[512,512]{1,0:T(8,128)(2,1)S(1)} %copy-done.5, ...), custom_call_target="tpu_custom_call" | custom-call | flops 2147483648 | bytes 10747912 | tf_op jit(solution)/shard_map/project/pallas_call | solution.py:41
  89.3 7.1 %all-to-all-start.2 = ((f32[32,16,128]{2,1,0:T(8,128)}), f32[32,16,128]{2,1,0:T(8,128)S(1)}, u32[]{:S(2)}, u32[]{:S(2)}) async-start(f32[32,16,128]{2,1,0:T(8,128)} %bitcast.8), calls=%async_computation.2 | async-start | bytes 524288 | tf_op jit(solution)/shard_map/all_to_all | solution.py:240
  100.3 2.7 %collective-permute-start.1 = (bf16[256,512]{1,0:T(8,128)(2,1)}, bf16[256,512]{1,0:T(8,128)(2,1)}, u32[]{:S(2)}, u32[]{:S(2)}) collective-permute-start(bf16[256,512]{1,0:T(8,128)(2,1)} %get-tuple-element.25), channel_id=1, source_target_pairs={{0,7},{1,0},{2,1},{3,2},{4,3},{5,4},{6,5},{7,6},{8,15},{9,8},{10,9... | collective-permute-start | bytes 786440 | tf_op jit(solution)/shard_map/ppermute | solution.py:233
  106.1 5.6 %all-to-all-start.3 = ((f32[32,16,128]{2,1,0:T(8,128)}), f32[32,16,128]{2,1,0:T(8,128)S(1)}, u32[]{:S(2)}, u32[]{:S(2)}) async-start(f32[32,16,128]{2,1,0:T(8,128)} %suffix.1), calls=%async_computation.3 | async-start | bytes 524288 | tf_op jit(solution)/shard_map/all_to_all | solution.py:244
  111.7 4.8 %add_convert_fusion = bf16[16,512,128]{2,1,0:T(8,128)(2,1)} fusion(f32[16,512,128]{2,1,0:T(8,128)} %copy-done.4, bf16[16,512,128]{2,1,0:T(8,128)(2,1)} %collective-permute-done.16), kind=kLoop, calls=%fused_computation | loop fusion | flops 3145728 | bytes 8388608 | tf_op jit(solution)/shard_map/convert_element_type | solution.py:328
  116.5 4.2 %all-to-all-done.3 = f32[32,16,128]{2,1,0:T(8,128)S(1)} async-done(((f32[32,16,128]{2,1,0:T(8,128)}), f32[32,16,128]{2,1,0:T(8,128)S(1)}, u32[]{:S(2)}, u32[]{:S(2)}) %all-to-all-start.3) | async-done | bytes 262176 | tf_op jit(solution)/shard_map/all_to_all | solution.py:244
  120.7 3.7 %all-to-all-start.4 = ((bf16[16,512,128]{2,1,0:T(8,128)(2,1)}), bf16[16,512,128]{2,1,0:T(8,128)(2,1)S(1)}, u32[]{:S(2)}, u32[]{:S(2)}) async-start(bf16[16,512,128]{2,1,0:T(8,128)(2,1)} %add_convert_fusion), calls=%async_computation.4 | async-start | bytes 4194304 | tf_op jit(solution)/shard_map/all_to_all | solution.py:330
  126.6 2.7 %out_step.3 = (bf16[512,512]{1,0:T(8,128)(2,1)S(1)}, bf16[512,512]{1,0:T(8,128)(2,1)S(1)}) custom-call(s32[2]{0:T(128)S(1)} %pad_add_fusion.me, bf16[512,512]{1,0:T(8,128)(2,1)S(1)} %get-tuple-element.23.attn, bf16[4096,512]{1,0:T(8,128)(2,1)S(1)} %copy-done.2, bf16[256,512]{1,0:T(8,128)(2,1)} %collective-permute-done.from_left, ...), custom_call_target="tpu_custom_call" | custom-call | flops 536870912 | bytes 3670016 | tf_op jit(solution)/shard_map/out_step/pallas_call | solution.py:213
  129.4 2.7 %collective-permute-start.3 = (bf16[512,512]{1,0:T(8,128)(2,1)S(1)}, bf16[512,512]{1,0:T(8,128)(2,1)S(1)}, u32[]{:S(2)}, u32[]{:S(2)}) collective-permute-start(bf16[512,512]{1,0:T(8,128)(2,1)S(1)} %get-tuple-element.27), channel_id=1, source_target_pairs={{0,7},{1,0},{2,1},{3,2},{4,3},{5,4},{6,5},{7,6},{8,15},{9,8},{10,9... | collective-permute-start | bytes 1572872 | tf_op jit(solution)/shard_map/ppermute | solution.py:233
  132.1 11.9 %collective-permute-done.2.from_left = bf16[512,512]{1,0:T(8,128)(2,1)S(1)} collective-permute-done((bf16[512,512]{1,0:T(8,128)(2,1)S(1)}, bf16[512,512]{1,0:T(8,128)(2,1)S(1)}, u32[]{:S(2)}, u32[]{:S(2)}) %collective-permute-start.2) | collective-permute-done | bytes 524320 | tf_op jit(solution)/shard_map/ppermute | solution.py:233
  148.4 10.9 %collective-permute-done.4.from_left = bf16[512,512]{1,0:T(8,128)(2,1)S(1)} collective-permute-done((bf16[512,512]{1,0:T(8,128)(2,1)S(1)}, bf16[512,512]{1,0:T(8,128)(2,1)S(1)}, u32[]{:S(2)}, u32[]{:S(2)}) %collective-permute-start.4) | collective-permute-done | bytes 524320 | tf_op jit(solution)/shard_map/ppermute | solution.py:233
  161.2 2.7 %collective-permute-start.7 = (bf16[512,512]{1,0:T(8,128)(2,1)S(1)}, bf16[512,512]{1,0:T(8,128)(2,1)S(1)}, u32[]{:S(2)}, u32[]{:S(2)}) collective-permute-start(bf16[512,512]{1,0:T(8,128)(2,1)S(1)} %get-tuple-element.31), channel_id=1, source_target_pairs={{0,7},{1,0},{2,1},{3,2},{4,3},{5,4},{6,5},{7,6},{8,15},{9,8},{10,9... | collective-permute-start | bytes 1572872 | tf_op jit(solution)/shard_map/ppermute | solution.py:233
  163.9 7.8 %backward.1 = (bf16[512,512]{1,0:T(8,128)(2,1)}, bf16[512,512]{1,0:T(8,128)(2,1)}, bf16[512,512]{1,0:T(8,128)(2,1)}) custom-call(bf16[512,512]{1,0:T(8,128)(2,1)S(1)} %copy-done.6, bf16[512,512]{1,0:T(8,128)(2,1)S(1)} %copy-done.13, bf16[512,512]{1,0:T(8,128)(2,1)S(1)} %copy-done.16, bf16[512,512]{1,0:T(8,128)(2,1)S(1)} %copy-done.19, ...), custom_call_target="tpu_custom_call" | custom-call | flops 2415919104 | bytes 4194304 | tf_op jit(solution)/shard_map/backward/pallas_call | solution.py:41
  (76 shorter events, 32.9 us)
Async XLA Ops:
  0.6 69.1 %copy-start.6 = (bf16[512,512]{1,0:T(8,128)(2,1)S(1)}, bf16[512,512]{1,0:T(8,128)(2,1)}, u32[]{:S(2)}) copy-start(bf16[512,512]{1,0:T(8,128)(2,1)} %q.5) | copy-start | bytes 1572868
  0.6 17.4 %collective-permute-start.9 = (bf16[512,512]{1,0:T(8,128)(2,1)}, bf16[512,512]{1,0:T(8,128)(2,1)S(1)}, u32[]{:S(2)}, u32[]{:S(2)}) collective-permute-start(bf16[512,512]{1,0:T(8,128)(2,1)} %rest_0_.3), channel_id=1, source_target_pairs={{0,7},{1,0},{2,1},{3,2},{4,3},{5,4},{6,5},{7,6},{8,15},{9,8},{10,9... | collective-permute-start | bytes 1572872 | tf_op jit(solution)/shard_map/ppermute | solution.py:233
  7.1 14.2 %collective-permute-start.8 = (bf16[512,512]{1,0:T(8,128)(2,1)}, bf16[512,512]{1,0:T(8,128)(2,1)S(1)}, u32[]{:S(2)}, u32[]{:S(2)}) collective-permute-start(bf16[512,512]{1,0:T(8,128)(2,1)} %rest_0_.3), channel_id=1, source_target_pairs={{0,1},{1,2},{2,3},{3,4},{4,5},{5,6},{6,7},{7,0},{8,9},{9,10},{10,1... | collective-permute-start | bytes 1572872 | tf_op jit(solution)/shard_map/ppermute | solution.py:233
  18.0 13.0 %collective-permute-start.11 = (bf16[512,512]{1,0:T(8,128)(2,1)S(1)}, bf16[512,512]{1,0:T(8,128)(2,1)S(1)}, u32[]{:S(2)}, u32[]{:S(2)}) collective-permute-start(bf16[512,512]{1,0:T(8,128)(2,1)S(1)} %collective-permute-done.9.rest_2_), channel_id=1, source_target_pairs={{0,7},{1,0},{2,1},{3,2},{4,3},{5,4},{6,5},{7,6},{8,15},{9,8},{10,9... | collective-permute-start | bytes 1572872 | tf_op jit(solution)/shard_map/ppermute | solution.py:233
  21.3 13.1 %collective-permute-start.10 = (bf16[512,512]{1,0:T(8,128)(2,1)S(1)}, bf16[512,512]{1,0:T(8,128)(2,1)}, u32[]{:S(2)}, u32[]{:S(2)}) collective-permute-start(bf16[512,512]{1,0:T(8,128)(2,1)S(1)} %collective-permute-done.8.rest_1_), channel_id=1, source_target_pairs={{0,1},{1,2},{2,3},{3,4},{4,5},{5,6},{6,7},{7,0},{8,9},{9,10},{10,1... | collective-permute-start | bytes 1572872 | tf_op jit(solution)/shard_map/ppermute | solution.py:233
  31.0 38.7 %copy-start.9 = (bf16[512,512]{1,0:T(8,128)(2,1)}, bf16[512,512]{1,0:T(8,128)(2,1)S(1)}, u32[]{:S(2)}) copy-start(bf16[512,512]{1,0:T(8,128)(2,1)S(1)} %collective-permute-done.11.rest_4_) | copy-start | bytes 1572868
  31.0 29.6 %collective-permute-start.13 = (bf16[512,512]{1,0:T(8,128)(2,1)S(1)}, bf16[512,512]{1,0:T(8,128)(2,1)S(1)}, u32[]{:S(2)}, u32[]{:S(2)}) collective-permute-start(bf16[512,512]{1,0:T(8,128)(2,1)S(1)} %collective-permute-done.11.rest_4_), channel_id=1, source_target_pairs={{0,7},{1,0},{2,1},{3,2},{4,3},{5,4},{6,5},{7,6},{8,15},{9,8},{10,9... | collective-permute-start | bytes 1572872 | tf_op jit(solution)/shard_map/ppermute | solution.py:233
  34.4 29.9 %collective-permute-start.12 = (bf16[512,512]{1,0:T(8,128)(2,1)}, bf16[512,512]{1,0:T(8,128)(2,1)S(1)}, u32[]{:S(2)}, u32[]{:S(2)}) collective-permute-start(bf16[512,512]{1,0:T(8,128)(2,1)} %collective-permute-done.10.rest_3_), channel_id=1, source_target_pairs={{0,1},{1,2},{2,3},{3,4},{4,5},{5,6},{6,7},{7,0},{8,9},{9,10},{10,1... | collective-permute-start | bytes 1572872 | tf_op jit(solution)/shard_map/ppermute | solution.py:233
  56.2 13.5 %all-to-all-start.1 = ((f32[32,16,128]{2,1,0:T(8,128)}), f32[32,16,128]{2,1,0:T(8,128)}, u32[]{:S(2)}, u32[]{:S(2)}) async-start(f32[32,16,128]{2,1,0:T(8,128)} %prefix.1), calls=%async_computation.1 | async-start | bytes 524288 | tf_op jit(solution)/shard_map/all_to_all | solution.py:244
  61.4 13.8 %collective-permute-start.15 = (bf16[256,512]{1,0:T(8,128)(2,1)}, bf16[256,512]{1,0:T(8,128)(2,1)S(1)}, u32[]{:S(2)}, u32[]{:S(2)}) collective-permute-start(bf16[256,512]{1,0:T(8,128)(2,1)} %slice.9), channel_id=1, source_target_pairs={{0,7},{1,0},{2,1},{3,2},{4,3},{5,4},{6,5},{7,6},{8,15},{9,8},{10,9... | collective-permute-start | bytes 786440 | tf_op jit(solution)/shard_map/ppermute | solution.py:233
  65.0 10.1 %collective-permute-start.14 = (bf16[256,512]{1,0:T(8,128)(2,1)}, bf16[256,512]{1,0:T(8,128)(2,1)}, u32[]{:S(2)}, u32[]{:S(2)}) collective-permute-start(bf16[256,512]{1,0:T(8,128)(2,1)} %slice.8), channel_id=1, source_target_pairs={{0,1},{1,2},{2,3},{3,4},{4,5},{5,6},{6,7},{7,0},{8,9},{9,10},{10,1... | collective-permute-start | bytes 786440 | tf_op jit(solution)/shard_map/ppermute | solution.py:233
  83.2 28.5 %collective-permute-start.16 = (bf16[16,512,128]{2,1,0:T(8,128)(2,1)}, bf16[16,512,128]{2,1,0:T(8,128)(2,1)}, u32[]{:S(2)}, u32[]{:S(2)}) collective-permute-start(bf16[16,512,128]{2,1,0:T(8,128)(2,1)} %get-tuple-element.40), channel_id=1, source_target_pairs={{0,8},{8,0},{16,24},{24,16},{32,40},{40,32},{48,56},{56,48},{64,72... | collective-permute-start | bytes 6291464 | tf_op jit(solution)/shard_map/ppermute | solution.py:327
  89.3 16.1 %all-to-all-start.2 = ((f32[32,16,128]{2,1,0:T(8,128)}), f32[32,16,128]{2,1,0:T(8,128)S(1)}, u32[]{:S(2)}, u32[]{:S(2)}) async-start(f32[32,16,128]{2,1,0:T(8,128)} %bitcast.8), calls=%async_computation.2 | async-start | bytes 524288 | tf_op jit(solution)/shard_map/all_to_all | solution.py:240
  100.3 24.1 %collective-permute-start = (bf16[256,512]{1,0:T(8,128)(2,1)}, bf16[256,512]{1,0:T(8,128)(2,1)}, u32[]{:S(2)}, u32[]{:S(2)}) collective-permute-start(bf16[256,512]{1,0:T(8,128)(2,1)} %get-tuple-element.24), channel_id=1, source_target_pairs={{0,1},{1,2},{2,3},{3,4},{4,5},{5,6},{6,7},{7,0},{8,9},{9,10},{10,1... | collective-permute-start | bytes 786440 | tf_op jit(solution)/shard_map/ppermute | solution.py:233
  100.3 24.1 %collective-permute-start.1 = (bf16[256,512]{1,0:T(8,128)(2,1)}, bf16[256,512]{1,0:T(8,128)(2,1)}, u32[]{:S(2)}, u32[]{:S(2)}) collective-permute-start(bf16[256,512]{1,0:T(8,128)(2,1)} %get-tuple-element.25), channel_id=1, source_target_pairs={{0,7},{1,0},{2,1},{3,2},{4,3},{5,4},{6,5},{7,6},{8,15},{9,8},{10,9... | collective-permute-start | bytes 786440 | tf_op jit(solution)/shard_map/ppermute | solution.py:233
  106.1 14.6 %all-to-all-start.3 = ((f32[32,16,128]{2,1,0:T(8,128)}), f32[32,16,128]{2,1,0:T(8,128)S(1)}, u32[]{:S(2)}, u32[]{:S(2)}) async-start(f32[32,16,128]{2,1,0:T(8,128)} %suffix.1), calls=%async_computation.3 | async-start | bytes 524288 | tf_op jit(solution)/shard_map/all_to_all | solution.py:244
  120.7 55.0 %all-to-all-start.4 = ((bf16[16,512,128]{2,1,0:T(8,128)(2,1)}), bf16[16,512,128]{2,1,0:T(8,128)(2,1)S(1)}, u32[]{:S(2)}, u32[]{:S(2)}) async-start(bf16[16,512,128]{2,1,0:T(8,128)(2,1)} %add_convert_fusion), calls=%async_computation.4 | async-start | bytes 4194304 | tf_op jit(solution)/shard_map/all_to_all | solution.py:330
  129.3 14.6 %collective-permute-start.2 = (bf16[512,512]{1,0:T(8,128)(2,1)S(1)}, bf16[512,512]{1,0:T(8,128)(2,1)S(1)}, u32[]{:S(2)}, u32[]{:S(2)}) collective-permute-start(bf16[512,512]{1,0:T(8,128)(2,1)S(1)} %get-tuple-element.26), channel_id=1, source_target_pairs={{0,1},{1,2},{2,3},{3,4},{4,5},{5,6},{6,7},{7,0},{8,9},{9,10},{10,1... | collective-permute-start | bytes 1572872 | tf_op jit(solution)/shard_map/ppermute | solution.py:233
  129.4 14.5 %collective-permute-start.3 = (bf16[512,512]{1,0:T(8,128)(2,1)S(1)}, bf16[512,512]{1,0:T(8,128)(2,1)S(1)}, u32[]{:S(2)}, u32[]{:S(2)}) collective-permute-start(bf16[512,512]{1,0:T(8,128)(2,1)S(1)} %get-tuple-element.27), channel_id=1, source_target_pairs={{0,7},{1,0},{2,1},{3,2},{4,3},{5,4},{6,5},{7,6},{8,15},{9,8},{10,9... | collective-permute-start | bytes 1572872 | tf_op jit(solution)/shard_map/ppermute | solution.py:233
  145.6 13.7 %collective-permute-start.4 = (bf16[512,512]{1,0:T(8,128)(2,1)S(1)}, bf16[512,512]{1,0:T(8,128)(2,1)S(1)}, u32[]{:S(2)}, u32[]{:S(2)}) collective-permute-start(bf16[512,512]{1,0:T(8,128)(2,1)S(1)} %get-tuple-element.28), channel_id=1, source_target_pairs={{0,1},{1,2},{2,3},{3,4},{4,5},{5,6},{6,7},{7,0},{8,9},{9,10},{10,1... | collective-permute-start | bytes 1572872 | tf_op jit(solution)/shard_map/ppermute | solution.py:233
  145.7 18.1 %copy-start.13 = (bf16[512,512]{1,0:T(8,128)(2,1)S(1)}, bf16[512,512]{1,0:T(8,128)(2,1)}, u32[]{:S(2)}) copy-start(bf16[512,512]{1,0:T(8,128)(2,1)} %k.3) | copy-start | bytes 1572868
  145.8 13.6 %collective-permute-start.5 = (bf16[512,512]{1,0:T(8,128)(2,1)S(1)}, bf16[512,512]{1,0:T(8,128)(2,1)S(1)}, u32[]{:S(2)}, u32[]{:S(2)}) collective-permute-start(bf16[512,512]{1,0:T(8,128)(2,1)S(1)} %get-tuple-element.29), channel_id=1, source_target_pairs={{0,7},{1,0},{2,1},{3,2},{4,3},{5,4},{6,5},{7,6},{8,15},{9,8},{10,9... | collective-permute-start | bytes 1572872 | tf_op jit(solution)/shard_map/ppermute | solution.py:233
  161.1 12.8 %collective-permute-start.6 = (bf16[512,512]{1,0:T(8,128)(2,1)S(1)}, bf16[512,512]{1,0:T(8,128)(2,1)S(1)}, u32[]{:S(2)}, u32[]{:S(2)}) collective-permute-start(bf16[512,512]{1,0:T(8,128)(2,1)S(1)} %get-tuple-element.30), channel_id=1, source_target_pairs={{0,1},{1,2},{2,3},{3,4},{4,5},{5,6},{6,7},{7,0},{8,9},{9,10},{10,1... | collective-permute-start | bytes 1572872 | tf_op jit(solution)/shard_map/ppermute | solution.py:233
  161.2 12.7 %collective-permute-start.7 = (bf16[512,512]{1,0:T(8,128)(2,1)S(1)}, bf16[512,512]{1,0:T(8,128)(2,1)S(1)}, u32[]{:S(2)}, u32[]{:S(2)}) collective-permute-start(bf16[512,512]{1,0:T(8,128)(2,1)S(1)} %get-tuple-element.31), channel_id=1, source_target_pairs={{0,7},{1,0},{2,1},{3,2},{4,3},{5,4},{6,5},{7,6},{8,15},{9,8},{10,9... | collective-permute-start | bytes 1572872 | tf_op jit(solution)/shard_map/ppermute | solution.py:233
  (17 other events, 85.2 us)

commit v2 on v1

v2 whole, which is shorter than its diff:
```python
import functools

import jax
import jax.numpy as jnp
from jax import lax
from jax.experimental import pallas as pl
from jax.experimental.pallas import tpu as pltpu
from jax.sharding import PartitionSpec as P

DH = 128
epsilon = 1e-06
VMEM = 63 << 20
bf16, f32 = jnp.bfloat16, jnp.float32


def dot(a, b, left, right):
    return lax.dot_general(a, b, (((left,), (right,)), ((), ())), preferred_element_type=f32)


def split(x):
    high = x.astype(bf16)
    return high, (x - high.astype(f32)).astype(bf16)


def dot2(parts, b, left, right):
    return dot(parts[0], b, left, right) + dot(parts[1], b, left, right)


def dot2r(a, parts, left, right):
    return dot(a, parts[0], left, right) + dot(a, parts[1], left, right)


def shape(dims, dtype):
    return jax.ShapeDtypeStruct(dims, dtype)


def call(body, outs, args, name, weight=1, scalars=0):
    in_specs = [pl.BlockSpec(memory_space=pltpu.SMEM)] * scalars
    in_specs += [pl.BlockSpec(memory_space=pltpu.VMEM)] * (len(args) - scalars)
    return pl.pallas_call(
        body,
        out_shape=tuple(outs),
        in_specs=in_specs,
        out_specs=tuple([pl.BlockSpec(memory_space=pltpu.VMEM)] * len(outs)),
        compiler_params=pltpu.CompilerParams(vmem_limit_bytes=VMEM),
        cost_estimate=pl.CostEstimate(flops=weight * 10**10, bytes_accessed=1000, transcendentals=0),
        name=name,
    )(*args)


def head(i):
    return slice(i * DH, (i + 1) * DH)


def state_body(left, right, out):
    for h in range(out.shape[0]):
        out[h] = dot(left[:, head(h)], right[:, head(h)], 0, 0)


def prefix_body(reverse, parts, out):
    count = parts.shape[0]
    state = jnp.zeros(parts.shape[1:], f32)
    for step in range(count):
        i = count - 1 - step if reverse else step
        out[i] = state
        state = state + parts[i]


def lower_mask(rows):
    return lax.broadcasted_iota(jnp.int32, (rows, rows), 0) >= lax.broadcasted_iota(
        jnp.int32, (rows, rows), 1
    )


def forward_body(q, k, v, prefix, attn, attn_t, mixed_out):
    rows = q.shape[0]
    mask = lower_mask(rows)
    for h in range(prefix.shape[0]):
        qh, kh, vh = q[:, head(h)], k[:, head(h)], v[:, head(h)]
        scores = split(jnp.where(mask, dot(qh, kh, 1, 1), 0.0))
        mixed = dot2(scores, vh, 1, 0) + dot2r(qh, split(prefix[h]), 1, 0)
        inverse = lax.rsqrt(jnp.mean(mixed * mixed, axis=-1, keepdims=True) + epsilon)
        normed = mixed * inverse
        mixed_out[:, head(h)] = mixed
        attn[:, head(h)] = normed.astype(bf16)
        attn_t[head(h), :] = normed.T.astype(bf16)


def block_term(block, place, weight):
    rows = block[...] if block.shape[0] == place.stop - place.start else block[place, :]
    return dot(rows, weight, 1, 0)


def add_blocks(offsets, me, w, blocks, place, start):
    wide = w.shape[1]
    ring = w.shape[0] // wide
    total = start
    for block, (offset, part) in zip(blocks, offsets):
        if part is not None and part != place:
            continue
        source = lax.rem(me[0] + offset, ring)
        weight = w[pl.ds(pl.multiple_of(source * wide, wide), wide), :]
        term = block_term(block, place, weight)
        total = term if total is None else total + term
    return total


def project_early_body(offsets, me, w, *rest):
    blocks, out = rest[:-1], rest[-1]
    place = slice(0, out.shape[0])
    out[...] = add_blocks(offsets, me, w, blocks, place, None)


def project_body(offsets, me, w, early, mixed, q, *rest):
    blocks, (d_mixed, grads) = rest[:-2], rest[-2:]
    half = q.shape[0] // 2
    totals = [None] * grads.shape[0]
    for place in (slice(0, half), slice(half, 2 * half)):
        d_part = add_blocks(offsets, me, w, blocks, place, early[place, :])
        for h in range(grads.shape[0]):
            d_attn = d_part[:, head(h)]
            m = mixed[place, head(h)]
            inverse = lax.rsqrt(jnp.mean(m * m, axis=-1, keepdims=True) + epsilon)
            normed = m * inverse
            d_m = inverse * (d_attn - normed * jnp.mean(d_attn * normed, axis=-1, keepdims=True))
            d_m = d_m.astype(bf16)
            d_mixed[place, head(h)] = d_m
            term = dot(q[place, head(h)], d_m, 0, 0)
            totals[h] = term if totals[h] is None else totals[h] + term
    for h in range(grads.shape[0]):
        grads[h] = totals[h]


def backward_body(q, k, v, d_mixed, prefix, grad_q, part_k, part_v):
    rows = q.shape[0]
    low = lower_mask(rows)
    high = lax.broadcasted_iota(jnp.int32, (rows, rows), 0) <= lax.broadcasted_iota(
        jnp.int32, (rows, rows), 1
    )
    for h in range(prefix.shape[0]):
        qh, kh, vh, dh = q[:, head(h)], k[:, head(h)], v[:, head(h)], d_mixed[:, head(h)]
        d_scores = split(jnp.where(low, dot(dh, vh, 1, 1), 0.0))
        grad_q[:, head(h)] = (
            dot2(d_scores, kh, 1, 0) + dot2r(dh, split(prefix[h]), 1, 1)
        ).astype(bf16)
        d_scores_t = split(jnp.where(high, dot(vh, dh, 1, 1), 0.0))
        part_k[:, head(h)] = dot2(d_scores_t, qh, 1, 0)
        scores_t = split(jnp.where(high, dot(kh, qh, 1, 1), 0.0))
        part_v[:, head(h)] = dot2(scores_t, dh, 1, 0)


def finish_body(k, v, part_k, part_v, later, grad_k, grad_v):
    for h in range(later.shape[0]):
        after = split(later[h])
        grad_k[:, head(h)] = (part_k[:, head(h)] + dot2r(v[:, head(h)], after, 1, 1)).astype(bf16)
        grad_v[:, head(h)] = (part_v[:, head(h)] + dot2r(k[:, head(h)], after, 1, 0)).astype(bf16)


def weight_body(me, attn_t, *rest):
    blocks, (keep, send) = rest[:-2], rest[-2:]
    wide = keep.shape[2]
    half = attn_t.shape[1] // 2
    first = me[1] == 0
    groups = blocks[0].shape[1] // (2 * wide)
    place = 0
    while blocks:
        if blocks[0].shape[0] == 2 * half:
            terms, blocks = dot(attn_t[...], blocks[0][...], 1, 0), blocks[1:]
        else:
            terms = dot(attn_t[:, 0:half], blocks[0][...], 1, 0)
            terms = terms + dot(attn_t[:, half:], blocks[1][...], 1, 0)
            blocks = blocks[2:]
        for j in range(groups):
            even = terms[:, 2 * j * wide : (2 * j + 1) * wide]
            odd = terms[:, (2 * j + 1) * wide : (2 * j + 2) * wide]
            keep[place] = jnp.where(first, even, odd)
            send[place] = jnp.where(first, odd, even).astype(bf16)
            place += 1


def pair_body(offsets, ring, me, *rest):
    sources, out = rest[:-1], rest[-1]
    groups = out.shape[0] // ring
    at = 0
    for keep, received in zip(sources[0::2], sources[1::2]):
        for i in range(keep.shape[0] // groups):
            source = lax.rem(me[0] + offsets[at], ring)
            for j in range(groups):
                term = keep[groups * i + j] + received[groups * i + j].astype(f32)
                out[source * groups + j] = term.astype(bf16)
            at += 1


def sum_body(parts, out):
    total = parts[0].astype(f32)
    for i in range(1, parts.shape[0]):
        total = total + parts[i].astype(f32)
    out[...] = total.T


def out_body(attn, w, out):
    out[...] = dot(attn[...], w[...], 1, 1).astype(bf16)


def out_call(attn, w):
    rows, features = attn.shape
    return pl.pallas_call(
        out_body,
        grid=(w.shape[0] // features,),
        in_specs=[
            pl.BlockSpec((rows, features), lambda i: (0, 0)),
            pl.BlockSpec((features, features), lambda i: (i, 0)),
        ],
        out_specs=pl.BlockSpec((rows, features), lambda i: (i, 0)),
        out_shape=shape((rows * w.shape[0] // features, features), bf16),
        compiler_params=pltpu.CompilerParams(vmem_limit_bytes=VMEM),
        cost_estimate=pl.CostEstimate(flops=1000, bytes_accessed=1000, transcendentals=0),
        name="out_terms",
    )(attn, w)


def shift(x, axis, amount):
    count = lax.axis_size(axis)
    return lax.ppermute(x, axis, [(i, (i + amount) % count) for i in range(count)])


def per_device(queries, keys, values, w_out, grad_out):
    length, features = queries.shape
    heads = features // DH
    half = length // 2
    ring = lax.axis_size("head")
    count = lax.axis_size("seq")
    me = jnp.stack([lax.axis_index("head"), lax.rem(lax.axis_index("seq"), 2)]).astype(jnp.int32)
    block = shape((length, features), bf16)
    wide_block = shape((length, features), f32)
    states = shape((heads, DH, DH), f32)
    tie = lax.optimization_barrier

    def exchange(parts):
        return lax.all_to_all(parts, "seq", 0, 0, tiled=True)

    def sums(parts, reverse, name):
        body = functools.partial(prefix_body, reverse)
        return call(body, [shape(parts.shape, f32)], [parts], name)[0]

    def pieces_of(state):
        return state.reshape(count, -1, DH)

    def swap(x):
        return lax.ppermute(x, "seq", [(i, i ^ 1) for i in range(count)])

    def weight(blocks, number, name):
        dims = (number * count // (2 * ring), features, w_out.shape[0] // count)
        outs = [shape(dims, f32), shape(dims, bf16)]
        keep, send = call(weight_body, outs, [me, attn_t] + blocks, name, scalars=1)
        return [keep, swap(send)]

    right, left = shift(grad_out, "head", 1), shift(grad_out, "head", -1)
    (local_state,) = call(state_body, [states], [keys, values], "state")
    parts = exchange(pieces_of(local_state))
    right, left, parts = tie((right, left, parts))
    blocks, offsets = [grad_out, right, left], [(0, None), (ring - 1, None), (1, None)]
    right, left = shift(right, "head", 1), shift(left, "head", -1)
    prefix = exchange(sums(parts, False, "prefix"))
    right, left, prefix = tie((right, left, prefix))
    prefix = prefix.reshape(states.shape)
    blocks += [right, left]
    offsets += [(ring - 2, None), (2, None)]
    right, left = shift(right, "head", 1), shift(left, "head", -1)
    attn, attn_t, mixed = call(
        forward_body,
        [block, shape((features, length), bf16), wide_block],
        [queries, keys, values, prefix],
        "forward",
    )
    terms = out_call(attn, w_out)
    layer_out = lax.psum_scatter(terms, "head", scatter_dimension=0, tiled=True)
    me, terms = tie((me, terms))
    early = call(
        functools.partial(project_early_body, offsets),
        [wide_block],
        [me, w_out] + blocks,
        "project_early",
        scalars=1,
    )[0]
    early, attn_t = tie((early, attn_t))
    pairs = weight(blocks, len(blocks), "weight_early")
    right, left, early, pairs[0] = tie((right, left, early, pairs[0]))
    top, bottom = shift(right[:half], "head", 1), shift(left[half:], "head", -1)
    last_blocks = [right, left, top, bottom]
    last_offsets = [
        (ring - 3, None),
        (3, None),
        (ring // 2, slice(0, half)),
        (ring // 2, slice(half, length)),
    ]
    pairs += weight(last_blocks, 3, "weight_late")
    early, pairs[2] = tie((early, pairs[2]))
    d_mixed, local_grads = call(
        functools.partial(project_body, last_offsets),
        [block, states],
        [me, w_out, early, mixed, queries] + last_blocks,
        "project",
        scalars=1,
    )
    parts = exchange(pieces_of(local_grads))
    order = [offset for offset, _ in (offsets + last_offsets)[:ring]]
    dims = (count // 2, features, w_out.shape[0] // count)
    both = call(
        functools.partial(pair_body, order, ring),
        [shape(dims, bf16)],
        [me] + pairs,
        "pair_add",
        scalars=1,
    )[0]
    parts, both = tie((parts, both))
    groups = [[2 * chip + core for chip in range(count // 2)] for core in range(2)]
    both = lax.all_to_all(both, "seq", 0, 0, axis_index_groups=groups, tiled=True)
    grad_q, part_k, part_v = call(
        backward_body,
        [block, wide_block, wide_block],
        [queries, keys, values, d_mixed, prefix],
        "backward",
    )
    parts, grad_q, part_k, part_v = tie((parts, grad_q, part_k, part_v))
    later = exchange(sums(parts, True, "suffix")).reshape(states.shape)
    grad_k, grad_v = call(
        finish_body, [block, block], [keys, values, part_k, part_v, later], "finish"
    )
    grad_w_out = call(sum_body, [shape((dims[2], dims[1]), f32)], [both], "weight_sum")[0]
    return layer_out, grad_q, grad_k, grad_v, grad_w_out


def solution(mesh):
    return jax.shard_map(
        per_device,
        mesh=mesh,
        in_specs=(
            P("seq", "head"),
            P("seq", "head"),
            P("seq", "head"),
            P(None, "head"),
            P("seq", "head"),
        ),
        out_specs=(
            P("seq", "head"),
            P("seq", "head"),
            P("seq", "head"),
            P("seq", "head"),
            P("seq", "head"),
        ),
        check_vma=False,
    )
```

time: 178 us -> 186 us (1.045)
  Pallas kernels: 33 us -> 58.5 us
  starting transfers between devices: 48.1 us -> 29.6 us
  blocking collectives: 18.6 us -> 33.5 us
  local copies, waits for them, and re-layouts: 15.3 us -> 1.87 us
  between operations: 0.91 us -> 14.1 us
  waiting for transfers between devices: 56 us -> 46.6 us
  other arithmetic: 4.87 us -> 0.62 us
    ppermute x16 -> x8, waiting for transfers between devices: 44.8 us -> 12.4 us  [shift(): lax.ppermute(x, axis, [(i, (i + amount) % count) for i in range(count)])]
    pallas_call x8 -> x12, Pallas kernels: 23.3 us -> 50.2 us  [call(): pl.pallas_call(body, out_shape=tuple(outs), in_specs=in_specs, out_specs=...]
    all_to_all x1, waiting for transfers between devices: 0.01 us -> 25.7 us  [per_device(): lax.all_to_all(both, 'seq', 0, 0, axis_index_groups=groups, tiled=True)]
    all_to_all x1 -> x2, blocking collectives: 18.6 us -> 33.5 us  [exchange(): return lax.all_to_all(parts, 'seq', 0, 0, tiled=True)]
    ppermute x16 -> x8, starting transfers between devices: 27.1 us -> 13.9 us  [shift(): lax.ppermute(x, axis, [(i, (i + amount) % count) for i in range(count)])]
    unnamed x40 -> x10, local copies, waits for them, and re-layouts: 13.9 us -> 0.72 us
    all_to_all x3 -> x2, starting transfers between devices: 17.1 us -> 9.57 us  [exchange(): return lax.all_to_all(parts, 'seq', 0, 0, tiled=True)]
    convert_element_type x1 -> x0, other arithmetic: 4.8 us -> none  [per_device(): both = (keep + received.astype(f32)).astype(bf16)]
  transfers between devices with their start and end apart: 21 -> 14, of which waited for: 8 -> 4; matrix products, arithmetic and copies ran while one was open for 4% -> 1% of each run, Pallas kernels for 15% -> 32%
where the time goes in v2:
time: 186 us; the launch traced here: 185 us
  Pallas kernels  58.5 us (31%)
  waiting for transfers between devices  46.6 us (25%)
  blocking collectives  33.5 us (18%)
  starting transfers between devices  29.6 us (16%)
  between operations  14.1 us (8%)
  local copies, waits for them, and re-layouts  1.87 us (1%)
    pallas_call x12, Pallas kernels, call(): pl.pallas_call(body, out_shape=tuple(outs), in_specs=in_specs, out_specs=...  50.2 us
    all_to_all x2, blocking collectives, exchange(): return lax.all_to_all(parts, 'seq', 0, 0, tiled=True)  33.5 us
    all_to_all x1, waiting for transfers between devices, per_device(): lax.all_to_all(both, 'seq', 0, 0, axis_index_groups=groups, tiled=True)  25.7 us
    ppermute x8, starting transfers between devices, shift(): lax.ppermute(x, axis, [(i, (i + amount) % count) for i in range(count)])  13.9 us
    ppermute x8, waiting for transfers between devices, shift(): lax.ppermute(x, axis, [(i, (i + amount) % count) for i in range(count)])  12.4 us
    all_to_all x2, starting transfers between devices, exchange(): return lax.all_to_all(parts, 'seq', 0, 0, tiled=True)  9.57 us
    all_to_all x2, waiting for transfers between devices, exchange(): return lax.all_to_all(parts, 'seq', 0, 0, tiled=True)  8.43 us
    pallas_call x1, Pallas kernels, out_call(): pl.pallas_call(out_body, grid=(w.shape[0] // features,), in_specs=[pl.Blo...  8.31 us
  transfers between devices with their start and end apart: 14, of which 4 were waited for; matrix products, arithmetic and copies ran while one was open for 1% of the time, Pallas kernels for 32%

profile of v2, /device:TPU:1, one launch (start us, length us, event | category | flops | bytes accessed | tf_op | source)
XLA Modules:
  0.0 184.8 jit_solution(9028699830282993303)
XLA Ops:
  7.2 6.5 %collective-permute-start.1 = (bf16[512,512]{1,0:T(8,128)(2,1)}, bf16[512,512]{1,0:T(8,128)(2,1)S(1)}, u32[]{:S(2)}, u32[]{:S(2)}) collective-permute-start(bf16[512,512]{1,0:T(8,128)(2,1)} %rest_0_.3), channel_id=1, source_target_pairs={{0,7},{1,0},{2,1},{3,2},{4,3},{5,4},{6,5},{7,6},{8,15},{9,8},{10,9... | collective-permute-start | bytes 1572872 | tf_op jit(solution)/shard_map/ppermute | solution.py:224
  13.7 2.3 %state.1 = f32[4,128,128]{2,1,0:T(8,128)} custom-call(bf16[512,512]{1,0:T(8,128)(2,1)} %k.5, bf16[512,512]{1,0:T(8,128)(2,1)} %v.5), custom_call_target="tpu_custom_call" | custom-call | flops 10000000000 | bytes 1000 | tf_op jit(solution)/shard_map/state/pallas_call | solution.py:40
  15.9 17.1 %all_to_all.25.parts = f32[32,16,128]{2,1,0:T(8,128)} all-to-all(f32[32,16,128]{2,1,0:T(8,128)} %bitcast.10), channel_id=1, replica_groups=mesh['seq'=32,'head'=8] {'seq'}, dimensions={0} | all-to-all | bytes 524288 | tf_op jit(solution)/shard_map/all_to_all | solution.py:240
  33.1 3.0 %collective-permute-start.3 = (bf16[512,512]{1,0:T(8,128)(2,1)S(1)}, bf16[512,512]{1,0:T(8,128)(2,1)}, u32[]{:S(2)}, u32[]{:S(2)}) collective-permute-start(bf16[512,512]{1,0:T(8,128)(2,1)S(1)} %collective-permute-done.1.rest_2_), channel_id=1, source_target_pairs={{0,7},{1,0},{2,1},{3,2},{4,3},{5,4},{6,5},{7,6},{8,15},{9,8},{10,9... | collective-permute-start | bytes 1572872 | tf_op jit(solution)/shard_map/ppermute | solution.py:224
  36.2 1.7 prefix.1
  37.9 4.0 %all-to-all-start.1 = ((f32[32,16,128]{2,1,0:T(8,128)}), f32[32,16,128]{2,1,0:T(8,128)S(1)}, u32[]{:S(2)}, u32[]{:S(2)}) async-start(f32[32,16,128]{2,1,0:T(8,128)} %prefix.1), calls=%async_computation.1 | async-start | bytes 524288 | tf_op jit(solution)/shard_map/all_to_all | solution.py:240
  42.5 8.4 %all-to-all-done.1 = f32[32,16,128]{2,1,0:T(8,128)S(1)} async-done(((f32[32,16,128]{2,1,0:T(8,128)}), f32[32,16,128]{2,1,0:T(8,128)S(1)}, u32[]{:S(2)}, u32[]{:S(2)}) %all-to-all-start.1) | async-done | bytes 262176 | tf_op jit(solution)/shard_map/all_to_all | solution.py:240
  51.1 2.7 %collective-permute-start.5 = (bf16[512,512]{1,0:T(8,128)(2,1)}, bf16[512,512]{1,0:T(8,128)(2,1)}, u32[]{:S(2)}, u32[]{:S(2)}) collective-permute-start(bf16[512,512]{1,0:T(8,128)(2,1)} %collective-permute-done.3.rest_4_), channel_id=1, source_target_pairs={{0,7},{1,0},{2,1},{3,2},{4,3},{5,4},{6,5},{7,6},{8,15},{9,8},{10,9... | collective-permute-start | bytes 1572872 | tf_op jit(solution)/shard_map/ppermute | solution.py:224
  53.7 5.0 %forward.1 = (bf16[512,512]{1,0:T(8,128)(2,1)}, bf16[512,512]{1,0:T(8,128)(2,1)}, f32[512,512]{1,0:T(8,128)}) custom-call(bf16[512,512]{1,0:T(8,128)(2,1)} %q.5, bf16[512,512]{1,0:T(8,128)(2,1)} %k.5, bf16[512,512]{1,0:T(8,128)(2,1)} %v.5, f32[4,128,128]{2,1,0:T(8,128)} %bitcast.6), custom_call_target="tpu_custom_call" | custom-call | flops 10000000000 | bytes 1000 | tf_op jit(solution)/shard_map/forward/pallas_call | solution.py:40
  58.7 8.3 %out_terms.1 = bf16[4096,512]{1,0:T(8,128)(2,1)} custom-call(bf16[512,512]{1,0:T(8,128)(2,1)} %get-tuple-element.44.attn, bf16[4096,512]{1,0:T(8,128)(2,1)} %w.5), custom_call_target="tpu_custom_call" | custom-call | flops 1000 | bytes 1000 | tf_op jit(solution)/shard_map/out_terms/pallas_call | solution.py:207
  67.0 5.4 %project_early.1.early = f32[512,512]{1,0:T(8,128)} custom-call(s32[2]{0:T(128)} %pad_add_fusion.me, bf16[4096,512]{1,0:T(8,128)(2,1)} %w.5, bf16[512,512]{1,0:T(8,128)(2,1)} %rest_0_.3, bf16[512,512]{1,0:T(8,128)(2,1)} %collective-permute-done.rest_1_, bf16[512,512]{1,0:T(8,128)(2,1)} %copy-done.3, bf16[512,512]{1,0:T(8,128)(2,1)} %collective-permute-done.2.rest_3_, ...), custom_call_target="tpu_custom_call" | custom-call | flops 10000000000 | bytes 1000 | tf_op jit(solution)/shard_map/project_early/pallas_call | solution.py:40
  72.5 5.3 %weight_early.1 = (f32[10,512,128]{2,1,0:T(8,128)}, bf16[10,512,128]{2,1,0:T(8,128)(2,1)}) custom-call(s32[2]{0:T(128)} %pad_add_fusion.me, bf16[512,512]{1,0:T(8,128)(2,1)} %get-tuple-element.50.attn_t, bf16[512,512]{1,0:T(8,128)(2,1)} %rest_0_.3, bf16[512,512]{1,0:T(8,128)(2,1)} %collective-permute-done.rest_1_, bf16[512,512]{1,0:T(8,128)(2,1)} %copy-done.3, ...), custom_call_target="tpu_custom_call" | custom-call | flops 10000000000 | bytes 1000 | tf_op jit(solution)/shard_map/weight_early/pallas_call | solution.py:40
  81.8 10.9 %collective-permute-done.7.rest_3_ = bf16[256,512]{1,0:T(8,128)(2,1)S(1)} collective-permute-done((bf16[256,512]{1,0:T(8,128)(2,1)S(1)}, bf16[256,512]{1,0:T(8,128)(2,1)S(1)}, u32[]{:S(2)}, u32[]{:S(2)}) %collective-permute-start.7) | collective-permute-done | bytes 262176 | tf_op jit(solution)/shard_map/ppermute | solution.py:224
  94.2 4.0 %weight_late.1 = (f32[6,512,128]{2,1,0:T(8,128)}, bf16[6,512,128]{2,1,0:T(8,128)(2,1)}) custom-call(s32[2]{0:T(128)} %pad_add_fusion.me, bf16[512,512]{1,0:T(8,128)(2,1)} %get-tuple-element.50.attn_t, bf16[512,512]{1,0:T(8,128)(2,1)} %copy-done.2, bf16[512,512]{1,0:T(8,128)(2,1)} %collective-permute-done.5.rest_1_, ...), custom_call_target="tpu_custom_call" | custom-call | flops 10000000000 | bytes 1000 | tf_op jit(solution)/shard_map/weight_late/pallas_call | solution.py:40
  98.2 5.7 %project.1 = (bf16[512,512]{1,0:T(8,128)(2,1)}, f32[4,128,128]{2,1,0:T(8,128)}) custom-call(s32[2]{0:T(128)} %pad_add_fusion.me, bf16[4096,512]{1,0:T(8,128)(2,1)} %w.5, f32[512,512]{1,0:T(8,128)} %project_early.1.early, f32[512,512]{1,0:T(8,128)} %get-tuple-element.57.mixed, bf16[512,512]{1,0:T(8,128)(2,1)} %q.5, bf16[512,512]{1,0:T(8,128)(2,1)} %copy-done.2, ...), custom_call_target="tpu_custom_call" | custom-call | flops 10000000000 | bytes 1000 | tf_op jit(solution)/shard_map/project/pallas_call | solution.py:40
  103.9 5.6 %all-to-all-start.2 = ((f32[32,16,128]{2,1,0:T(8,128)}), f32[32,16,128]{2,1,0:T(8,128)S(1)}, u32[]{:S(2)}, u32[]{:S(2)}) async-start(f32[32,16,128]{2,1,0:T(8,128)} %bitcast.8), calls=%async_computation.3 | async-start | bytes 524288 | tf_op jit(solution)/shard_map/all_to_all | solution.py:240
  109.9 8.3 %backward.1 = (bf16[512,512]{1,0:T(8,128)(2,1)}, f32[512,512]{1,0:T(8,128)}, f32[512,512]{1,0:T(8,128)}) custom-call(bf16[512,512]{1,0:T(8,128)(2,1)} %q.5, bf16[512,512]{1,0:T(8,128)(2,1)} %k.5, bf16[512,512]{1,0:T(8,128)(2,1)} %v.5, bf16[512,512]{1,0:T(8,128)(2,1)} %get-tuple-element.64.d_mixed, f32[4,128,128]{2,1,0:T(8,128)} %bitcast.7), custom_call_target="tpu_custom_call" | custom-call | flops 10000000000 | bytes 1000 | tf_op jit(solution)/shard_map/backward/pallas_call | solution.py:40
  118.2 4.6 %pair_add.1 = bf16[16,512,128]{2,1,0:T(8,128)(2,1)} custom-call(s32[2]{0:T(128)} %pad_add_fusion.me, f32[10,512,128]{2,1,0:T(8,128)} %get-tuple-element.59.rest_0_, bf16[10,512,128]{2,1,0:T(8,128)(2,1)} %collective-permute-done.8.rest_1_, f32[6,512,128]{2,1,0:T(8,128)} %get-tuple-element.61.rest_2_, bf16[6,512,128]{2,1,0:T(8,128)(2,1)} %collective-permute-done.9.rest_3_), custom_call_target="tpu_custom_call" | custom-call | flops 10000000000 | bytes 1000 | tf_op jit(solution)/shard_map/pair_add/pallas_call | solution.py:40
  123.5 1.7 suffix.1
  125.2 16.4 %all_to_all.26 = f32[32,16,128]{2,1,0:T(8,128)} all-to-all(f32[32,16,128]{2,1,0:T(8,128)} %suffix.1), channel_id=1, replica_groups=mesh['seq'=32,'head'=8] {'seq'}, dimensions={0} | all-to-all | bytes 524288 | tf_op jit(solution)/shard_map/all_to_all | solution.py:240
  141.6 4.4 %all-to-all-start.4 = ((bf16[16,512,128]{2,1,0:T(8,128)(2,1)}), bf16[16,512,128]{2,1,0:T(8,128)(2,1)}, u32[]{:S(2)}, u32[]{:S(2)}) async-start(bf16[16,512,128]{2,1,0:T(8,128)(2,1)} %pair_add.1), calls=%async_computation.5 | async-start | bytes 4194304 | tf_op jit(solution)/shard_map/all_to_all | solution.py:318
  146.0 3.6 %finish.1 = (bf16[512,512]{1,0:T(8,128)(2,1)}, bf16[512,512]{1,0:T(8,128)(2,1)}) custom-call(bf16[512,512]{1,0:T(8,128)(2,1)} %k.5, bf16[512,512]{1,0:T(8,128)(2,1)} %v.5, f32[512,512]{1,0:T(8,128)} %get-tuple-element.69.part_k, f32[512,512]{1,0:T(8,128)} %get-tuple-element.70.part_v, f32[4,128,128]{2,1,0:T(8,128)} %bitcast.9), custom_call_target="tpu_custom_call" | custom-call | flops 10000000000 | bytes 1000 | tf_op jit(solution)/shard_map/finish/pallas_call | solution.py:40
  149.6 25.7 %all-to-all-done.4.parts = bf16[16,512,128]{2,1,0:T(8,128)(2,1)} async-done(((bf16[16,512,128]{2,1,0:T(8,128)(2,1)}), bf16[16,512,128]{2,1,0:T(8,128)(2,1)}, u32[]{:S(2)}, u32[]{:S(2)}) %all-to-all-start.4) | async-done | bytes 2097184 | tf_op jit(solution)/shard_map/all_to_all | solution.py:318
  175.4 2.6 %weight_sum.1 = f32[128,512]{1,0:T(8,128)} custom-call(bf16[16,512,128]{2,1,0:T(8,128)(2,1)} %all-to-all-done.4.parts), custom_call_target="tpu_custom_call" | custom-call | flops 10000000000 | bytes 1000 | tf_op jit(solution)/shard_map/weight_sum/pallas_call | solution.py:40
  (33 shorter events, 7.5 us)
Async XLA Ops:
  7.2 25.9 %collective-permute-start.1 = (bf16[512,512]{1,0:T(8,128)(2,1)}, bf16[512,512]{1,0:T(8,128)(2,1)S(1)}, u32[]{:S(2)}, u32[]{:S(2)}) collective-permute-start(bf16[512,512]{1,0:T(8,128)(2,1)} %rest_0_.3), channel_id=1, source_target_pairs={{0,7},{1,0},{2,1},{3,2},{4,3},{5,4},{6,5},{7,6},{8,15},{9,8},{10,9... | collective-permute-start | bytes 1572872 | tf_op jit(solution)/shard_map/ppermute | solution.py:224
  13.6 19.4 %collective-permute-start = (bf16[512,512]{1,0:T(8,128)(2,1)}, bf16[512,512]{1,0:T(8,128)(2,1)}, u32[]{:S(2)}, u32[]{:S(2)}) collective-permute-start(bf16[512,512]{1,0:T(8,128)(2,1)} %rest_0_.3), channel_id=1, source_target_pairs={{0,1},{1,2},{2,3},{3,4},{4,5},{5,6},{6,7},{7,0},{8,9},{9,10},{10,1... | collective-permute-start | bytes 1572872 | tf_op jit(solution)/shard_map/ppermute | solution.py:224
  33.0 4.8 %copy-start.3 = (bf16[512,512]{1,0:T(8,128)(2,1)}, bf16[512,512]{1,0:T(8,128)(2,1)S(1)}, u32[]{:S(2)}) copy-start(bf16[512,512]{1,0:T(8,128)(2,1)S(1)} %collective-permute-done.1.rest_2_) | copy-start | bytes 1572868
  33.0 17.9 %collective-permute-start.2 = (bf16[512,512]{1,0:T(8,128)(2,1)}, bf16[512,512]{1,0:T(8,128)(2,1)}, u32[]{:S(2)}, u32[]{:S(2)}) collective-permute-start(bf16[512,512]{1,0:T(8,128)(2,1)} %collective-permute-done.rest_1_), channel_id=1, source_target_pairs={{0,1},{1,2},{2,3},{3,4},{4,5},{5,6},{6,7},{7,0},{8,9},{9,10},{10,1... | collective-permute-start | bytes 1572872 | tf_op jit(solution)/shard_map/ppermute | solution.py:224
  33.1 17.8 %collective-permute-start.3 = (bf16[512,512]{1,0:T(8,128)(2,1)S(1)}, bf16[512,512]{1,0:T(8,128)(2,1)}, u32[]{:S(2)}, u32[]{:S(2)}) collective-permute-start(bf16[512,512]{1,0:T(8,128)(2,1)S(1)} %collective-permute-done.1.rest_2_), channel_id=1, source_target_pairs={{0,7},{1,0},{2,1},{3,2},{4,3},{5,4},{6,5},{7,6},{8,15},{9,8},{10,9... | collective-permute-start | bytes 1572872 | tf_op jit(solution)/shard_map/ppermute | solution.py:224
  37.9 13.1 %all-to-all-start.1 = ((f32[32,16,128]{2,1,0:T(8,128)}), f32[32,16,128]{2,1,0:T(8,128)S(1)}, u32[]{:S(2)}, u32[]{:S(2)}) async-start(f32[32,16,128]{2,1,0:T(8,128)} %prefix.1), calls=%async_computation.1 | async-start | bytes 524288 | tf_op jit(solution)/shard_map/all_to_all | solution.py:240
  41.9 136.1 %reduce-scatter.2.cloned.1.call-start = ((), (), s32[]{:S(2)}) async-start(), calls=%async_computation.6 | async-start | bytes 4718592 | tf_op jit(solution)/shard_map/reduce_scatter | solution.py:277
  51.0 2.8 %copy-start = (f32[32,16,128]{2,1,0:T(8,128)}, f32[32,16,128]{2,1,0:T(8,128)S(1)}, u32[]{:S(2)}) copy-start(f32[32,16,128]{2,1,0:T(8,128)S(1)} %all-to-all-done.1) | copy-start | bytes 786436
  51.0 26.8 %collective-permute-start.4 = (bf16[512,512]{1,0:T(8,128)(2,1)}, bf16[512,512]{1,0:T(8,128)(2,1)S(1)}, u32[]{:S(2)}, u32[]{:S(2)}) collective-permute-start(bf16[512,512]{1,0:T(8,128)(2,1)} %collective-permute-done.2.rest_3_), channel_id=1, source_target_pairs={{0,1},{1,2},{2,3},{3,4},{4,5},{5,6},{6,7},{7,0},{8,9},{9,10},{10,1... | collective-permute-start | bytes 1572872 | tf_op jit(solution)/shard_map/ppermute | solution.py:224
  51.1 26.8 %collective-permute-start.5 = (bf16[512,512]{1,0:T(8,128)(2,1)}, bf16[512,512]{1,0:T(8,128)(2,1)}, u32[]{:S(2)}, u32[]{:S(2)}) collective-permute-start(bf16[512,512]{1,0:T(8,128)(2,1)} %collective-permute-done.3.rest_4_), channel_id=1, source_target_pairs={{0,7},{1,0},{2,1},{3,2},{4,3},{5,4},{6,5},{7,6},{8,15},{9,8},{10,9... | collective-permute-start | bytes 1572872 | tf_op jit(solution)/shard_map/ppermute | solution.py:224
  77.8 16.4 %copy-start.2 = (bf16[512,512]{1,0:T(8,128)(2,1)}, bf16[512,512]{1,0:T(8,128)(2,1)S(1)}, u32[]{:S(2)}) copy-start(bf16[512,512]{1,0:T(8,128)(2,1)S(1)} %collective-permute-done.4.rest_0_) | copy-start | bytes 1572868
  79.0 13.7 %collective-permute-start.7 = (bf16[256,512]{1,0:T(8,128)(2,1)S(1)}, bf16[256,512]{1,0:T(8,128)(2,1)S(1)}, u32[]{:S(2)}, u32[]{:S(2)}) collective-permute-start(bf16[256,512]{1,0:T(8,128)(2,1)S(1)} %slice.7), channel_id=1, source_target_pairs={{0,7},{1,0},{2,1},{3,2},{4,3},{5,4},{6,5},{7,6},{8,15},{9,8},{10,9... | collective-permute-start | bytes 786440 | tf_op jit(solution)/shard_map/ppermute | solution.py:224
  79.5 14.7 %collective-permute-start.6 = (bf16[256,512]{1,0:T(8,128)(2,1)S(1)}, bf16[256,512]{1,0:T(8,128)(2,1)}, u32[]{:S(2)}, u32[]{:S(2)}) collective-permute-start(bf16[256,512]{1,0:T(8,128)(2,1)S(1)} %slice.6), channel_id=1, source_target_pairs={{0,1},{1,2},{2,3},{3,4},{4,5},{5,6},{6,7},{7,0},{8,9},{9,10},{10,1... | collective-permute-start | bytes 786440 | tf_op jit(solution)/shard_map/ppermute | solution.py:224
  80.5 37.7 %collective-permute-start.8 = (bf16[10,512,128]{2,1,0:T(8,128)(2,1)}, bf16[10,512,128]{2,1,0:T(8,128)(2,1)}, u32[]{:S(2)}, u32[]{:S(2)}) collective-permute-start(bf16[10,512,128]{2,1,0:T(8,128)(2,1)} %get-tuple-element.60), channel_id=1, source_target_pairs={{0,8},{8,0},{16,24},{24,16},{32,40},{40,32},{48,56},{56,48},{64,72... | collective-permute-start | bytes 3932168 | tf_op jit(solution)/shard_map/ppermute | solution.py:250
  92.7 1.5 copy-start.4
  103.9 18.9 %all-to-all-start.2 = ((f32[32,16,128]{2,1,0:T(8,128)}), f32[32,16,128]{2,1,0:T(8,128)S(1)}, u32[]{:S(2)}, u32[]{:S(2)}) async-start(f32[32,16,128]{2,1,0:T(8,128)} %bitcast.8), calls=%async_computation.3 | async-start | bytes 524288 | tf_op jit(solution)/shard_map/all_to_all | solution.py:240
  109.5 8.7 %collective-permute-start.9 = (bf16[6,512,128]{2,1,0:T(8,128)(2,1)}, bf16[6,512,128]{2,1,0:T(8,128)(2,1)}, u32[]{:S(2)}, u32[]{:S(2)}) collective-permute-start(bf16[6,512,128]{2,1,0:T(8,128)(2,1)} %get-tuple-element.62), channel_id=1, source_target_pairs={{0,8},{8,0},{16,24},{24,16},{32,40},{40,32},{48,56},{56,48},{64,72... | collective-permute-start | bytes 2359304 | tf_op jit(solution)/shard_map/ppermute | solution.py:250
  122.8 0.7 copy-start.1
  141.6 33.8 %all-to-all-start.4 = ((bf16[16,512,128]{2,1,0:T(8,128)(2,1)}), bf16[16,512,128]{2,1,0:T(8,128)(2,1)}, u32[]{:S(2)}, u32[]{:S(2)}) async-start(bf16[16,512,128]{2,1,0:T(8,128)(2,1)} %pair_add.1), calls=%async_computation.5 | async-start | bytes 4194304 | tf_op jit(solution)/shard_map/all_to_all | solution.py:318
Sparse Core Ops, SparseCore 0:
  67.2 56.4 reduce-scatter.1

commit v3 on v0

v3 whole, which is shorter than its diff:
```python
import functools

import jax
import jax.numpy as jnp
from jax import lax
from jax.experimental import pallas as pl
from jax.experimental.pallas import tpu as pltpu
from jax.sharding import PartitionSpec as P

DH = 128
epsilon = 1e-06
VMEM = 62 << 20
WORK = 10**9
LIGHT = 0
bf16, f32 = jnp.bfloat16, jnp.float32


def dot(a, b, left, right):
    return lax.dot_general(a, b, (((left,), (right,)), ((), ())), preferred_element_type=f32)


def split(x):
    high = x.astype(bf16)
    return high, (x - high.astype(f32)).astype(bf16)


def dot2(parts, b, left, right):
    return dot(parts[0], b, left, right) + dot(parts[1], b, left, right)


def dot2r(a, parts, left, right):
    return dot(a, parts[0], left, right) + dot(a, parts[1], left, right)


def shape(dims, dtype):
    return jax.ShapeDtypeStruct(dims, dtype)


def cost(weight=1):
    return pl.CostEstimate(flops=int(weight * WORK), bytes_accessed=1000, transcendentals=0)


def whole(dims):
    return pl.BlockSpec(tuple(dims), lambda *_: (0,) * len(dims))


def call(body, outs, args, name, grid=None, specs=None, scalars=0, scratch=(), weight=1):
    specs = specs or ([None] * (len(args) - scalars), [None] * len(outs))
    ins = [s or whole(a.shape) for s, a in zip(specs[0], args[scalars:])]
    outs_specs = tuple(s or whole(o.shape) for s, o in zip(specs[1], outs))
    return pl.pallas_call(
        body,
        grid_spec=pltpu.PrefetchScalarGridSpec(
            num_scalar_prefetch=scalars,
            grid=grid or (1,),
            in_specs=ins,
            out_specs=outs_specs,
            scratch_shapes=scratch,
        ),
        out_shape=tuple(outs),
        compiler_params=pltpu.CompilerParams(vmem_limit_bytes=VMEM),
        cost_estimate=cost(weight),
        name=name,
    )(*args)


def head(i):
    return slice(i * DH, (i + 1) * DH)


def columns(rows):
    return pl.BlockSpec((rows, DH), lambda h: (0, h))


def per_head():
    return pl.BlockSpec((1, DH, DH), lambda h: (h, 0, 0))


def state_body(left, right, out):
    out[0] = dot(left[...], right[...], 0, 0)


def prefix_body(reverse, parts, out):
    count = parts.shape[0]
    state = jnp.zeros(parts.shape[1:], f32)
    for step in range(count):
        i = count - 1 - step if reverse else step
        out[i] = state
        state = state + parts[i]


def place(rows):
    return (
        lax.broadcasted_iota(jnp.int32, (rows, rows), 0),
        lax.broadcasted_iota(jnp.int32, (rows, rows), 1),
    )


def forward_body(q, k, v, prefix, attn, attn_t, mixed_out):
    row, column = place(q.shape[0])
    scores = split(jnp.where(row >= column, dot(q[...], k[...], 1, 1), 0.0))
    mixed = dot2(scores, v[...], 1, 0) + dot2r(q[...], split(prefix[0]), 1, 0)
    inverse = lax.rsqrt(jnp.mean(mixed * mixed, axis=-1, keepdims=True) + epsilon)
    normed = mixed * inverse
    mixed_out[...] = mixed
    attn[...] = normed.astype(bf16)
    attn_t[...] = normed.T.astype(bf16)


def project_body(blocks, w, mixed, q, d_mixed, grads, total):
    step = pl.program_id(0)
    wide = w.shape[1]
    term = None
    for i in range(blocks.shape[0]):
        part = dot(blocks[i], w[i * wide : (i + 1) * wide, :], 1, 0)
        term = part if term is None else term + part

    @pl.when(step == 0)
    def _():
        total[...] = term

    @pl.when(step > 0)
    def _():
        total[...] += term

    @pl.when(step == pl.num_programs(0) - 1)
    def _():
        for h in range(grads.shape[0]):
            d_attn, m = total[:, head(h)], mixed[:, head(h)]
            inverse = lax.rsqrt(jnp.mean(m * m, axis=-1, keepdims=True) + epsilon)
            normed = m * inverse
            d_m = inverse * (d_attn - normed * jnp.mean(d_attn * normed, axis=-1, keepdims=True))
            d_m = d_m.astype(bf16)
            d_mixed[:, head(h)] = d_m
            grads[h] = dot(q[:, head(h)], d_m, 0, 0)


def backward_body(q, k, v, d_mixed, prefix, grad_q, part_k, part_v):
    row, column = place(q.shape[0])
    q, k, v, d = q[...], k[...], v[...], d_mixed[...]
    d_scores = split(jnp.where(row >= column, dot(d, v, 1, 1), 0.0))
    grad_q[...] = (dot2(d_scores, k, 1, 0) + dot2r(d, split(prefix[0]), 1, 1)).astype(bf16)
    d_scores_t = split(jnp.where(row <= column, dot(v, d, 1, 1), 0.0))
    part_k[...] = dot2(d_scores_t, q, 1, 0)
    scores_t = split(jnp.where(row <= column, dot(k, q, 1, 1), 0.0))
    part_v[...] = dot2(scores_t, d, 1, 0)


def finish_body(k, v, part_k, part_v, later, grad_k, grad_v):
    after = split(later[0])
    grad_k[...] = (part_k[...] + dot2r(v[...], after, 1, 1)).astype(bf16)
    grad_v[...] = (part_v[...] + dot2r(k[...], after, 1, 0)).astype(bf16)


def weight_body(me, attn_t, block, keep, send):
    wide = keep.shape[2]
    first = me[1] == 0
    terms = dot(attn_t[...], block[0], 1, 0)
    for j in range(keep.shape[0]):
        even = terms[:, 2 * j * wide : (2 * j + 1) * wide]
        odd = terms[:, (2 * j + 1) * wide : (2 * j + 2) * wide]
        keep[j] = jnp.where(first, even, odd)
        send[j] = jnp.where(first, odd, even).astype(bf16)


ORDER = (2, 1, 3, 0)


def pair_body(me, keep, received, *outs):
    far, near = outs[:4], outs[4:]
    side = keep.shape[1]
    half = keep.shape[2] // 2
    for step, dx in enumerate(ORDER):

        @pl.when(pl.program_id(0) == step)
        def _(dx=dx):
            for dy in range(side):
                source = lax.rem(me[3] + dy, side)
                term = (keep[0, source] + received[0, source].astype(f32)).astype(bf16)
                for kind, first, second, rows in (
                    (0, dx, dy, term[:half]),
                    (1, dy, dx, term[half:]),
                ):
                    if first == 2:
                        far[2 * kind + second // 2][second % 2] = rows
                    else:
                        near[3 * kind + (1, 3, 0).index(first)][second] = rows


def turn_body(*refs):
    count = len(refs) // 3
    near, got, outs = refs[:count], refs[count : 2 * count], refs[2 * count :]
    for i in range(count):
        half = got[i].shape[0]
        into, other = (slice(0, half), slice(half, 2 * half))[:: 1 if i % 2 == 0 else -1]
        term = near[i][into].astype(f32) + got[i][...].astype(f32)
        outs[i][into] = term.astype(outs[i].dtype)
        outs[i][other] = near[i][other]


def cross_body(own_a, own_b, *refs):
    got, outs = refs[:4], refs[4:]
    for kind, own in enumerate((own_a, own_b)):
        left, right = got[2 * kind], got[2 * kind + 1]
        far, near = outs[2 * kind : 2 * kind + 2], outs[4 + 3 * kind : 7 + 3 * kind]
        half = far[0].shape[0]
        for i in range(own.shape[0]):
            term = own[i].astype(f32) + left[i].astype(f32) + right[i].astype(f32)
            if i == 2:
                far[0][...] = term[:half]
                far[1][...] = term[half:]
            else:
                near[(1, 3, 0).index(i)][...] = term


def close_body(own_a, own_b, *refs):
    got, out = refs[:4], refs[4]
    half = own_a.shape[0]
    for kind, own in enumerate((own_a, own_b)):
        term = own[...] + got[2 * kind][...] + got[2 * kind + 1][...]
        out[:, kind * half : (kind + 1) * half] = term.T


def first_body(me, attn, w, top, bottom):
    half = attn.shape[0] // 2
    terms = dot(attn[...], w[...], 1, 1).astype(bf16)
    top[...] = terms[0:half]
    bottom[...] = terms[half:]


def step_body(me, attn, w, from_left, from_right, to_right, to_left):
    half = attn.shape[0] // 2
    terms = dot(attn[...], w[...], 1, 1)

    def put(source, target, top):
        if source.shape[0] == target.shape[0]:
            target[...] = (terms + source[...].astype(f32)).astype(bf16)
        else:
            place, other = slice(0, half), slice(half, 2 * half)
            if not top:
                place, other = other, place
            target[place, :] = (terms[place] + source[...].astype(f32)).astype(bf16)
            target[other, :] = terms[other].astype(bf16)

    @pl.when(pl.program_id(0) == 0)
    def _():
        put(from_left, to_right, True)

    @pl.when(pl.program_id(0) == 1)
    def _():
        put(from_right, to_left, False)


def last_body(me, attn, w, from_left, from_right, out):
    terms = dot(attn[...], w[...], 1, 1)
    out[...] = (terms + from_left[...].astype(f32) + from_right[...].astype(f32)).astype(bf16)


def ring_call(body, outs, me, attn, w, rest, offsets, name):
    ring = w.shape[0] // attn.shape[0]
    wide = w.shape[0] // ring

    def weight(i, me):
        offset = offsets[0] if len(offsets) == 1 else jnp.where(i == 0, offsets[0], offsets[1])
        return (lax.rem(me[0] + offset, ring), 0)

    specs = ([None, pl.BlockSpec((wide, w.shape[1]), weight)] + [None] * len(rest), [None] * len(outs))
    return call(body, outs, [me, attn, w] + rest, name, (len(offsets),), specs, 1)


def shift(x, axis, amount):
    count = lax.axis_size(axis)
    return lax.ppermute(x, axis, [(i, (i + amount) % count) for i in range(count)])


SIDE = 4


def torus(x, dx, dy):
    pairs = []
    for i in range(lax.axis_size("seq")):
        chip, core = i // 2, i % 2
        to = (chip // SIDE + dx) % SIDE * SIDE + (chip % SIDE + dy) % SIDE
        pairs.append((i, 2 * to + core))
    return lax.ppermute(x, "seq", pairs)


def ways(arrays, flip):
    moves = ((1, 0), (-1, 0), (0, 1), (0, -1))
    moves = moves[2:] + moves[:2] if flip else moves
    return [torus(x, *move) for x, move in zip(arrays, moves)]


tie = lax.optimization_barrier


def per_device(queries, keys, values, w_out, grad_out):
    length, features = queries.shape
    heads = features // DH
    half = length // 2
    ring = lax.axis_size("head")
    count = lax.axis_size("seq")
    at = lax.axis_index("seq")
    me = jnp.stack([lax.axis_index("head"), at % 2, at // 2 // SIDE, at // 2 % SIDE])
    me = me.astype(jnp.int32)
    block = shape((length, features), bf16)
    half_block = shape((half, features), bf16)
    wide_block = shape((length, features), f32)
    states = shape((heads, DH, DH), f32)
    tall = columns(length)

    def exchange(parts):
        return lax.all_to_all(parts, "seq", 0, 0, tiled=True)

    def sums(parts, reverse, name):
        return call(functools.partial(prefix_body, reverse), [shape(parts.shape, f32)], [parts], name)[0]

    def pieces_of(state):
        return state.reshape(count, -1, DH)

    gathered = lax.all_gather(grad_out, "head")

    (local_state,) = call(
        state_body, [states], [keys, values], "state", (heads,), ([tall, tall], [per_head()])
    )
    prefix = exchange(sums(exchange(pieces_of(local_state)), False, "prefix")).reshape(states.shape)
    attn, attn_t, mixed = call(
        forward_body,
        [block, shape((features, length), bf16), wide_block],
        [queries, keys, values, prefix],
        "forward",
        (heads,),
        (
            [tall, tall, tall, per_head()],
            [tall, pl.BlockSpec((DH, length), lambda h: (h, 0)), tall],
        ),
    )

    def hop(pair):
        return [shift(pair[0], "head", 1), shift(pair[1], "head", -1)]

    def out_step(pair, number):
        offsets = [number, ring - number]
        return ring_call(step_body, [block, block], me, attn, w_out, pair, offsets, "out_step")

    pair = ring_call(
        first_body, [half_block, half_block], me, attn, w_out, [], [ring // 2], "out_first"
    )
    pair = out_step(hop(pair), ring // 2 - 1)
    gathered, *pair = tie((gathered, *pair))
    pair_two = hop(pair)

    d_mixed, local_grads = call(
        project_body,
        [block, states],
        [gathered, w_out, mixed, queries],
        "project",
        (ring // 2,),
        (
            [
                pl.BlockSpec((2, length, features), lambda i: (i, 0, 0)),
                pl.BlockSpec((2 * features, features), lambda i: (i, 0)),
                None,
                None,
            ],
            [None, None],
        ),
        scratch=[pltpu.VMEM((length, features), f32)],
        weight=LIGHT,
    )
    wide = w_out.shape[0] // count
    dims = (count // 2, features, wide)
    chips = count // 2 // ring
    piece = pl.BlockSpec((chips, features, wide), lambda i, me: (i, 0, 0))
    gathered, d_mixed, local_grads = tie((gathered, d_mixed, local_grads))
    keep, send = call(
        weight_body,
        [shape(dims, f32), shape(dims, bf16)],
        [me, attn_t, gathered],
        "weight",
        (ring,),
        (
            [None, pl.BlockSpec((1, length, features), lambda i, me: (i, 0, 0))],
            [piece, piece],
        ),
        1,
        weight=LIGHT,
    )
    received = lax.ppermute(send, "seq", [(i, i ^ 1) for i in range(count)])
    parts = exchange(pieces_of(local_grads))

    grid_dims = (SIDE, SIDE, features, wide)

    def row(i, me):
        dx = jnp.where(i == 0, ORDER[0], jnp.where(i == 1, ORDER[1], jnp.where(i == 2, ORDER[2], 0)))
        return (lax.rem(me[2] + dx, SIDE), 0, 0, 0)

    strip = pl.BlockSpec((1,) + grid_dims[1:], row)
    far_dims = shape((SIDE // 2, features // 2, wide), bf16)
    near_dims = shape((SIDE, features // 2, wide), bf16)
    terms = call(
        pair_body,
        [far_dims] * 4 + [near_dims] * 6,
        [me, keep.reshape(grid_dims), received.reshape(grid_dims)],
        "pair_add",
        (SIDE,),
        ([strip, strip], [None] * 10),
        1,
    )
    pair = out_step(pair_two, ring // 2 - 2)
    parts, *rest = tie((parts, *pair, *terms))
    pair, terms = rest[:2], rest[2:]
    pair_three = hop(pair)
    later = exchange(sums(parts, True, "suffix")).reshape(states.shape)
    got = ways(terms[:4], False)
    near = [terms[4], terms[5], terms[7], terms[8]]
    turned = call(turn_body, [near_dims] * 4, near + got, "turn")
    pair = out_step(pair_three, ring // 2 - 3)
    later, *rest = tie((later, *pair, *turned))
    pair, turned = rest[:2], rest[2:]
    pair_four = hop(pair)
    got = ways(turned, False)
    small, large = shape((features // 4, wide), f32), shape((features // 2, wide), f32)
    terms = call(
        cross_body, [small] * 4 + [large] * 6, [terms[6], terms[9]] + got, "cross"
    )
    got = ways(terms[:4], True)
    near = [terms[4], terms[5], terms[7], terms[8]]
    got = ways(call(turn_body, [large] * 4, near + got, "turn_two"), True)
    (grad_w_out,) = call(
        close_body, [shape((wide, features), f32)], [terms[6], terms[9]] + got, "close"
    )

    grad_q, part_k, part_v = call(
        backward_body,
        [block, wide_block, wide_block],
        [queries, keys, values, d_mixed, prefix],
        "backward",
        (heads,),
        ([tall] * 4 + [per_head()], [tall] * 3),
    )
    (layer_out,) = ring_call(last_body, [block], me, attn, w_out, pair_four, [0], "out_last")
    grad_k, grad_v = call(
        finish_body,
        [block, block],
        [keys, values, part_k, part_v, later],
        "finish",
        (heads,),
        ([tall] * 4 + [per_head()], [tall] * 2),
    )
    return layer_out, grad_q, grad_k, grad_v, grad_w_out


def solution(mesh):
    return jax.shard_map(
        per_device,
        mesh=mesh,
        in_specs=(
            P("seq", "head"),
            P("seq", "head"),
            P("seq", "head"),
            P(None, "head"),
            P("seq", "head"),
        ),
        out_specs=(
            P("seq", "head"),
            P("seq", "head"),
            P("seq", "head"),
            P("seq", "head"),
            P("seq", "head"),
        ),
        check_vma=False,
    )
```

time: 409 us -> 211 us (0.52)
  waiting for transfers between devices: 302 us -> 41.9 us
  Pallas kernels: 0 us -> 77.1 us
  starting transfers between devices: 0.38 us -> 47 us
  matrix products: 43.6 us -> 0 us
  other arithmetic: 34 us -> 0.61 us
  blocking collectives: 0 us -> 17.7 us
    all_gather x3 -> x1, waiting for transfers between devices: 170 us -> 0.01 us  [per_device(): gathered = lax.all_gather(grad_out, 'head')]
    reduce_scatter x2 -> x0, waiting for transfers between devices: 131 us -> none  [the longest x1 76.6 us: per_device(): lax.psum_scatter(lax.dot_general(grad_full, attn, (((0,), (0,)), ((), ())...]
    pallas_call x0 -> x18, Pallas kernels: none -> 77.1 us  [call(): pl.pallas_call(body, grid_spec=pltpu.PrefetchScalarGridSpec(num_scalar_pr...]
    dot_general x15 -> x0, matrix products: 43.6 us -> none  [the longest x8 18.7 us: product(): return jnp.einsum(form, left, right, precision=lax.Precision.HIGHEST)]
    ppermute x0 -> x25, starting transfers between devices: none -> 33 us  [the longest x16 18.7 us: torus(): return lax.ppermute(x, 'seq', pairs)]
    ppermute x0 -> x25, waiting for transfers between devices: none -> 32.1 us  [the longest x8 20.8 us: shift(): lax.ppermute(x, axis, [(i, (i + amount) % count) for i in range(count)])]
    add x31 -> x0, other arithmetic: 31.5 us -> none  [combine_sum(): return earlier + later_part]
    all_to_all x0 -> x1, blocking collectives: none -> 17.7 us  [exchange(): return lax.all_to_all(parts, 'seq', 0, 0, tiled=True)]
  transfers between devices with their start and end apart: 5 -> 29, of which waited for: 5 -> 8; matrix products, arithmetic and copies ran while one was open for 17% -> 0% of each run, Pallas kernels for 0% -> 26%
where the time goes in v3:
time: 211 us; the launch traced here: 208 us
  Pallas kernels  77.1 us (37%)
  starting transfers between devices  47 us (22%)
  waiting for transfers between devices  41.9 us (20%)
  blocking collectives  17.7 us (8%)
  between operations  14.3 us (7%)
  local copies, waits for them, and re-layouts  9.66 us (5%)
    pallas_call x18, Pallas kernels, call(): pl.pallas_call(body, grid_spec=pltpu.PrefetchScalarGridSpec(num_scalar_pr...  77.1 us
    ppermute x8, waiting for transfers between devices, shift(): lax.ppermute(x, axis, [(i, (i + amount) % count) for i in range(count)])  20.8 us
    ppermute x16, starting transfers between devices, torus(): return lax.ppermute(x, 'seq', pairs)  18.7 us
    all_to_all x1, blocking collectives, exchange(): return lax.all_to_all(parts, 'seq', 0, 0, tiled=True)  17.7 us
    all_to_all x3, starting transfers between devices, exchange(): return lax.all_to_all(parts, 'seq', 0, 0, tiled=True)  13.9 us
    ppermute x8, starting transfers between devices, shift(): lax.ppermute(x, axis, [(i, (i + amount) % count) for i in range(count)])  13.7 us
    ppermute x16, waiting for transfers between devices, torus(): return lax.ppermute(x, 'seq', pairs)  11.3 us
    unnamed x56, local copies, waits for them, and re-layouts  9.66 us
  transfers between devices with their start and end apart: 29, of which 8 were waited for; matrix products, arithmetic and copies ran while one was open for 0% of the time, Pallas kernels for 26%

profile of v3, /device:TPU:1, one launch (start us, length us, event | category | flops | bytes accessed | tf_op | source)
XLA Modules:
  0.0 208.3 jit_solution(525996812573334925)
XLA Ops:
  7.9 3.7 %state.1 = f32[4,128,128]{2,1,0:T(8,128)} custom-call(bf16[512,512]{1,0:T(8,128)(2,1)} %k.5, bf16[512,512]{1,0:T(8,128)(2,1)} %v.5), custom_call_target="tpu_custom_call" | custom-call | flops 1000000000 | bytes 1000 | tf_op jit(solution)/shard_map/state/pallas_call | solution.py:51
  11.6 17.7 %all_to_all.20.parts = f32[32,16,128]{2,1,0:T(8,128)} all-to-all(f32[32,16,128]{2,1,0:T(8,128)} %bitcast.17), channel_id=1, replica_groups=mesh['seq'=32,'head'=8] {'seq'}, dimensions={0} | all-to-all | bytes 524288 | tf_op jit(solution)/shard_map/all_to_all | solution.py:313
  31.0 3.7 %all-to-all-start.1 = ((f32[32,16,128]{2,1,0:T(8,128)}), f32[32,16,128]{2,1,0:T(8,128)S(1)}, u32[]{:S(2)}, u32[]{:S(2)}) async-start(f32[32,16,128]{2,1,0:T(8,128)} %prefix.1), calls=%async_computation.1 | async-start | bytes 524288 | tf_op jit(solution)/shard_map/all_to_all | solution.py:313
  35.3 8.4 %all-to-all-done.1 = f32[32,16,128]{2,1,0:T(8,128)S(1)} async-done(((f32[32,16,128]{2,1,0:T(8,128)}), f32[32,16,128]{2,1,0:T(8,128)S(1)}, u32[]{:S(2)}, u32[]{:S(2)}) %all-to-all-start.1) | async-done | bytes 262176 | tf_op jit(solution)/shard_map/all_to_all | solution.py:313
  44.5 6.0 %forward.1 = (bf16[512,512]{1,0:T(8,128)(2,1)}, bf16[512,512]{1,0:T(8,128)(2,1)}, f32[512,512]{1,0:T(8,128)}) custom-call(bf16[512,512]{1,0:T(8,128)(2,1)} %q.5, bf16[512,512]{1,0:T(8,128)(2,1)} %k.5, bf16[512,512]{1,0:T(8,128)(2,1)} %v.5, f32[4,128,128]{2,1,0:T(8,128)} %bitcast.14), custom_call_target="tpu_custom_call" | custom-call | flops 1000000000 | bytes 1000 | tf_op jit(solution)/shard_map/forward/pallas_call | solution.py:51
  50.5 3.1 %out_first.1 = (bf16[256,512]{1,0:T(8,128)(2,1)}, bf16[256,512]{1,0:T(8,128)(2,1)}) custom-call(s32[4]{0:T(128)} %pad_add_fusion.me, bf16[512,512]{1,0:T(8,128)(2,1)} %get-tuple-element.79.attn, bf16[4096,512]{1,0:T(8,128)(2,1)} %w.11), custom_call_target="tpu_custom_call" | custom-call | flops 1000000000 | bytes 1000 | tf_op jit(solution)/shard_map/out_first/pallas_call | solution.py:51
  55.2 4.0 %collective-permute-start.1 = (bf16[256,512]{1,0:T(8,128)(2,1)}, bf16[256,512]{1,0:T(8,128)(2,1)S(1)}, u32[]{:S(2)}, u32[]{:S(2)}) collective-permute-start(bf16[256,512]{1,0:T(8,128)(2,1)} %get-tuple-element.81), channel_id=1, source_target_pairs={{0,7},{1,0},{2,1},{3,2},{4,3},{5,4},{6,5},{7,6},{8,15},{9,8},{10,9... | collective-permute-start | bytes 786440 | tf_op jit(solution)/shard_map/ppermute | solution.py:273
  59.2 12.6 %collective-permute-done.from_left = bf16[256,512]{1,0:T(8,128)(2,1)S(1)} collective-permute-done((bf16[256,512]{1,0:T(8,128)(2,1)}, bf16[256,512]{1,0:T(8,128)(2,1)S(1)}, u32[]{:S(2)}, u32[]{:S(2)}) %collective-permute-start) | collective-permute-done | bytes 262176 | tf_op jit(solution)/shard_map/ppermute | solution.py:273
  73.2 4.1 %out_step.3 = (bf16[512,512]{1,0:T(8,128)(2,1)}, bf16[512,512]{1,0:T(8,128)(2,1)}) custom-call(s32[4]{0:T(128)} %pad_add_fusion.me, bf16[512,512]{1,0:T(8,128)(2,1)} %get-tuple-element.79.attn, bf16[4096,512]{1,0:T(8,128)(2,1)} %w.11, bf16[256,512]{1,0:T(8,128)(2,1)} %copy-done.9, bf16[256,512]{1,0:T(8,128)(2,1)} %copy-done.10), custom_call_target="tpu_custom_call" | custom-call | flops 1000000000 | bytes 1000 | tf_op jit(solution)/shard_map/out_step/pallas_call | solution.py:51
  77.3 8.0 %project.1 = (bf16[512,512]{1,0:T(8,128)(2,1)}, f32[4,128,128]{2,1,0:T(8,128)}) custom-call(bf16[8,512,512]{2,1,0:T(8,128)(2,1)} %bitcast.11, bf16[4096,512]{1,0:T(8,128)(2,1)} %w.11, f32[512,512]{1,0:T(8,128)} %get-tuple-element.85.mixed, bf16[512,512]{1,0:T(8,128)(2,1)} %q.5), custom_call_target="tpu_custom_call" | custom-call | bytes 1000 | tf_op jit(solution)/shard_map/project/pallas_call | solution.py:51
  85.3 9.4 %weight.1 = (f32[16,512,128]{2,1,0:T(8,128)}, bf16[16,512,128]{2,1,0:T(8,128)(2,1)}) custom-call(s32[4]{0:T(128)} %pad_add_fusion.me, bf16[512,512]{1,0:T(8,128)(2,1)} %get-tuple-element.93.attn_t, bf16[8,512,512]{2,1,0:T(8,128)(2,1)} %bitcast.12), custom_call_target="tpu_custom_call" | custom-call | bytes 1000 | tf_op jit(solution)/shard_map/weight/pallas_call | solution.py:51
  98.0 4.2 %all-to-all-start.2 = ((f32[32,16,128]{2,1,0:T(8,128)}), f32[32,16,128]{2,1,0:T(8,128)S(1)}, u32[]{:S(2)}, u32[]{:S(2)}) async-start(f32[32,16,128]{2,1,0:T(8,128)} %bitcast.7), calls=%async_computation.2 | async-start | bytes 524288 | tf_op jit(solution)/shard_map/all_to_all | solution.py:313
  102.2 8.1 %collective-permute-done.2.from_left = bf16[512,512]{1,0:T(8,128)(2,1)S(1)} collective-permute-done((bf16[512,512]{1,0:T(8,128)(2,1)}, bf16[512,512]{1,0:T(8,128)(2,1)S(1)}, u32[]{:S(2)}, u32[]{:S(2)}) %collective-permute-start.2) | collective-permute-done | bytes 524320 | tf_op jit(solution)/shard_map/ppermute | solution.py:273
  111.9 4.3 %out_step.4 = (bf16[512,512]{1,0:T(8,128)(2,1)}, bf16[512,512]{1,0:T(8,128)(2,1)}) custom-call(s32[4]{0:T(128)} %pad_add_fusion.me, bf16[512,512]{1,0:T(8,128)(2,1)} %get-tuple-element.79.attn, bf16[4096,512]{1,0:T(8,128)(2,1)} %w.11, bf16[512,512]{1,0:T(8,128)(2,1)} %copy-done.4, bf16[512,512]{1,0:T(8,128)(2,1)} %copy-done.5), custom_call_target="tpu_custom_call" | custom-call | flops 1000000000 | bytes 1000 | tf_op jit(solution)/shard_map/out_step/pallas_call | solution.py:51
  116.2 5.6 %pair_add.1 = (bf16[2,256,128]{2,1,0:T(8,128)(2,1)}, bf16[2,256,128]{2,1,0:T(8,128)(2,1)}, bf16[2,256,128]{2,1,0:T(8,128)(2,1)}, bf16[2,256,128]{2,1,0:T(8,128)(...) custom-call(s32[4]{0:T(128)} %pad_add_fusion.me, ...), custom_call_target="tpu_custom_call" | custom-call | flops 1000000000 | bytes 1000 | tf_op jit(solution)/shard_map/pair_add/pallas_call | solution.py:51
  127.3 2.9 %collective-permute-done.7.refs_4_ = bf16[2,256,128]{2,1,0:T(8,128)(2,1)S(1)} collective-permute-done((bf16[2,256,128]{2,1,0:T(8,128)(2,1)}, bf16[2,256,128]{2,1,0:T(8,128)(2,1)S(1)}, u32[]{:S(2)}, u32[]{:S(2)}) %collective-permute-start.7) | collective-permute-done | bytes 131104 | tf_op jit(solution)/shard_map/ppermute | solution.py:285
  132.7 6.0 %all-to-all-start.3 = ((f32[32,16,128]{2,1,0:T(8,128)}), f32[32,16,128]{2,1,0:T(8,128)S(1)}, u32[]{:S(2)}, u32[]{:S(2)}) async-start(f32[32,16,128]{2,1,0:T(8,128)} %suffix.1), calls=%async_computation.3 | async-start | bytes 524288 | tf_op jit(solution)/shard_map/all_to_all | solution.py:313
  142.7 4.5 %out_step.5 = (bf16[512,512]{1,0:T(8,128)(2,1)}, bf16[512,512]{1,0:T(8,128)(2,1)}) custom-call(s32[4]{0:T(128)} %pad_add_fusion.me, bf16[512,512]{1,0:T(8,128)(2,1)} %get-tuple-element.79.attn, bf16[4096,512]{1,0:T(8,128)(2,1)} %w.11, bf16[512,512]{1,0:T(8,128)(2,1)} %copy-done.2, bf16[512,512]{1,0:T(8,128)(2,1)} %copy-done.3), custom_call_target="tpu_custom_call" | custom-call | flops 1000000000 | bytes 1000 | tf_op jit(solution)/shard_map/out_step/pallas_call | solution.py:51
  153.2 3.8 %collective-permute-done.13.refs_0_ = bf16[4,256,128]{2,1,0:T(8,128)(2,1)S(1)} collective-permute-done((bf16[4,256,128]{2,1,0:T(8,128)(2,1)}, bf16[4,256,128]{2,1,0:T(8,128)(2,1)S(1)}, u32[]{:S(2)}, u32[]{:S(2)}) %collective-permute-start.13) | collective-permute-done | bytes 262176 | tf_op jit(solution)/shard_map/ppermute | solution.py:285
  173.3 2.7 %collective-permute-start.22 = (f32[256,128]{1,0:T(8,128)}, f32[256,128]{1,0:T(8,128)S(1)}, u32[]{:S(2)}, u32[]{:S(2)}) collective-permute-start(f32[256,128]{1,0:T(8,128)} %get-tuple-element.150), channel_id=1, source_target_pairs={{0,48},{8,56},{16,0},{24,8},{32,16},{40,24},{48,32},{56,40},{64,11... | collective-permute-start | bytes 393224 | tf_op jit(solution)/shard_map/ppermute | solution.py:285
  176.0 2.9 %collective-permute-done.21.refs_0_ = f32[256,128]{1,0:T(8,128)S(1)} collective-permute-done((f32[256,128]{1,0:T(8,128)}, f32[256,128]{1,0:T(8,128)S(1)}, u32[]{:S(2)}, u32[]{:S(2)}) %collective-permute-start.21) | collective-permute-done | bytes 131104 | tf_op jit(solution)/shard_map/ppermute | solution.py:285
  180.6 8.5 %backward.1 = (bf16[512,512]{1,0:T(8,128)(2,1)}, f32[512,512]{1,0:T(8,128)}, f32[512,512]{1,0:T(8,128)}) custom-call(bf16[512,512]{1,0:T(8,128)(2,1)} %q.5, bf16[512,512]{1,0:T(8,128)(2,1)} %k.5, bf16[512,512]{1,0:T(8,128)(2,1)} %v.5, bf16[512,512]{1,0:T(8,128)(2,1)} %get-tuple-element.126.d_mixed, f32[4,128,128]{2,1,0:T(8,128)} %bitcast.15), custom_call_target="tpu_custom_call" | custom-call | flops 1000000000 | bytes 1000 | tf_op jit(solution)/shard_map/backward/pallas_call | solution.py:51
  189.1 4.3 %finish.1 = (bf16[512,512]{1,0:T(8,128)(2,1)}, bf16[512,512]{1,0:T(8,128)(2,1)}) custom-call(bf16[512,512]{1,0:T(8,128)(2,1)} %k.5, bf16[512,512]{1,0:T(8,128)(2,1)} %v.5, f32[512,512]{1,0:T(8,128)} %get-tuple-element.128.part_k, f32[512,512]{1,0:T(8,128)} %get-tuple-element.129.part_v, f32[4,128,128]{2,1,0:T(8,128)} %bitcast.16), custom_call_target="tpu_custom_call" | custom-call | flops 1000000000 | bytes 1000 | tf_op jit(solution)/shard_map/finish/pallas_call | solution.py:51
  197.9 3.5 %out_last.1 = bf16[512,512]{1,0:T(8,128)(2,1)} custom-call(s32[4]{0:T(128)} %pad_add_fusion.me, bf16[512,512]{1,0:T(8,128)(2,1)} %get-tuple-element.79.attn, bf16[4096,512]{1,0:T(8,128)(2,1)} %w.11, bf16[512,512]{1,0:T(8,128)(2,1)} %copy-done, bf16[512,512]{1,0:T(8,128)(2,1)} %copy-done.1), custom_call_target="tpu_custom_call" | custom-call | flops 1000000000 | bytes 1000 | tf_op jit(solution)/shard_map/out_last/pallas_call | solution.py:51
  (111 shorter events, 52.0 us)
Async XLA Ops:
  7.2 70.2 %all-gather.3.cloned.1.call-start = ((), (), s32[]{:S(2)}) async-start(), calls=%async_computation.4 | async-start | bytes 4718592 | tf_op jit(solution)/shard_map/all_gather | solution.py:321
  31.0 12.8 %all-to-all-start.1 = ((f32[32,16,128]{2,1,0:T(8,128)}), f32[32,16,128]{2,1,0:T(8,128)S(1)}, u32[]{:S(2)}, u32[]{:S(2)}) async-start(f32[32,16,128]{2,1,0:T(8,128)} %prefix.1), calls=%async_computation.1 | async-start | bytes 524288 | tf_op jit(solution)/shard_map/all_to_all | solution.py:313
  53.6 18.2 %collective-permute-start = (bf16[256,512]{1,0:T(8,128)(2,1)}, bf16[256,512]{1,0:T(8,128)(2,1)S(1)}, u32[]{:S(2)}, u32[]{:S(2)}) collective-permute-start(bf16[256,512]{1,0:T(8,128)(2,1)} %get-tuple-element.80), channel_id=1, source_target_pairs={{0,1},{1,2},{2,3},{3,4},{4,5},{5,6},{6,7},{7,0},{8,9},{9,10},{10,1... | collective-permute-start | bytes 786440 | tf_op jit(solution)/shard_map/ppermute | solution.py:273
  55.2 16.6 %collective-permute-start.1 = (bf16[256,512]{1,0:T(8,128)(2,1)}, bf16[256,512]{1,0:T(8,128)(2,1)S(1)}, u32[]{:S(2)}, u32[]{:S(2)}) collective-permute-start(bf16[256,512]{1,0:T(8,128)(2,1)} %get-tuple-element.81), channel_id=1, source_target_pairs={{0,7},{1,0},{2,1},{3,2},{4,3},{5,4},{6,5},{7,6},{8,15},{9,8},{10,9... | collective-permute-start | bytes 786440 | tf_op jit(solution)/shard_map/ppermute | solution.py:273
  94.7 21.5 %collective-permute-start.4 = (bf16[16,512,128]{2,1,0:T(8,128)(2,1)}, bf16[16,512,128]{2,1,0:T(8,128)(2,1)}, u32[]{:S(2)}, u32[]{:S(2)}) collective-permute-start(bf16[16,512,128]{2,1,0:T(8,128)(2,1)} %get-tuple-element.96), channel_id=1, source_target_pairs={{0,8},{8,0},{16,24},{24,16},{32,40},{40,32},{48,56},{56,48},{64,72... | collective-permute-start | bytes 6291464 | tf_op jit(solution)/shard_map/ppermute | solution.py:389
  95.4 15.0 %collective-permute-start.2 = (bf16[512,512]{1,0:T(8,128)(2,1)}, bf16[512,512]{1,0:T(8,128)(2,1)S(1)}, u32[]{:S(2)}, u32[]{:S(2)}) collective-permute-start(bf16[512,512]{1,0:T(8,128)(2,1)} %get-tuple-element.89), channel_id=1, source_target_pairs={{0,1},{1,2},{2,3},{3,4},{4,5},{5,6},{6,7},{7,0},{8,9},{9,10},{10,1... | collective-permute-start | bytes 1572872 | tf_op jit(solution)/shard_map/ppermute | solution.py:273
  95.4 15.0 %collective-permute-start.3 = (bf16[512,512]{1,0:T(8,128)(2,1)S(1)}, bf16[512,512]{1,0:T(8,128)(2,1)S(1)}, u32[]{:S(2)}, u32[]{:S(2)}) collective-permute-start(bf16[512,512]{1,0:T(8,128)(2,1)S(1)} %copy-done.12), channel_id=1, source_target_pairs={{0,7},{1,0},{2,1},{3,2},{4,3},{5,4},{6,5},{7,6},{8,15},{9,8},{10,9... | collective-permute-start | bytes 1572872 | tf_op jit(solution)/shard_map/ppermute | solution.py:273
  98.0 23.8 %all-to-all-start.2 = ((f32[32,16,128]{2,1,0:T(8,128)}), f32[32,16,128]{2,1,0:T(8,128)S(1)}, u32[]{:S(2)}, u32[]{:S(2)}) async-start(f32[32,16,128]{2,1,0:T(8,128)} %bitcast.7), calls=%async_computation.2 | async-start | bytes 524288 | tf_op jit(solution)/shard_map/all_to_all | solution.py:313
  121.9 19.2 %collective-permute-start.5 = (bf16[512,512]{1,0:T(8,128)(2,1)}, bf16[512,512]{1,0:T(8,128)(2,1)S(1)}, u32[]{:S(2)}, u32[]{:S(2)}) collective-permute-start(bf16[512,512]{1,0:T(8,128)(2,1)} %get-tuple-element.108), channel_id=1, source_target_pairs={{0,1},{1,2},{2,3},{3,4},{4,5},{5,6},{6,7},{7,0},{8,9},{9,10},{10,1... | collective-permute-start | bytes 1572872 | tf_op jit(solution)/shard_map/ppermute | solution.py:273
  122.5 18.6 %collective-permute-start.6 = (bf16[512,512]{1,0:T(8,128)(2,1)S(1)}, bf16[512,512]{1,0:T(8,128)(2,1)S(1)}, u32[]{:S(2)}, u32[]{:S(2)}) collective-permute-start(bf16[512,512]{1,0:T(8,128)(2,1)S(1)} %copy-done.11), channel_id=1, source_target_pairs={{0,7},{1,0},{2,1},{3,2},{4,3},{5,4},{6,5},{7,6},{8,15},{9,8},{10,9... | collective-permute-start | bytes 1572872 | tf_op jit(solution)/shard_map/ppermute | solution.py:273
  124.9 13.8 %collective-permute-start.8 = (bf16[2,256,128]{2,1,0:T(8,128)(2,1)}, bf16[2,256,128]{2,1,0:T(8,128)(2,1)}, u32[]{:S(2)}, u32[]{:S(2)}) collective-permute-start(bf16[2,256,128]{2,1,0:T(8,128)(2,1)} %get-tuple-element.117), channel_id=1, source_target_pairs={{0,192},{8,200},{16,208},{24,216},{32,224},{40,232},{48,240},{56,2... | collective-permute-start | bytes 393224 | tf_op jit(solution)/shard_map/ppermute | solution.py:285
  127.3 11.4 %collective-permute-start.9 = (bf16[2,256,128]{2,1,0:T(8,128)(2,1)}, bf16[2,256,128]{2,1,0:T(8,128)(2,1)}, u32[]{:S(2)}, u32[]{:S(2)}) collective-permute-start(bf16[2,256,128]{2,1,0:T(8,128)(2,1)} %get-tuple-element.118), channel_id=1, source_target_pairs={{0,16},{8,24},{16,32},{24,40},{32,48},{40,56},{48,0},{56,8},{64,80... | collective-permute-start | bytes 393224 | tf_op jit(solution)/shard_map/ppermute | solution.py:285
  130.2 8.6 %collective-permute-start.10 = (bf16[2,256,128]{2,1,0:T(8,128)(2,1)}, bf16[2,256,128]{2,1,0:T(8,128)(2,1)}, u32[]{:S(2)}, u32[]{:S(2)}) collective-permute-start(bf16[2,256,128]{2,1,0:T(8,128)(2,1)} %get-tuple-element.119), channel_id=1, source_target_pairs={{0,48},{8,56},{16,0},{24,8},{32,16},{40,24},{48,32},{56,40},{64,11... | collective-permute-start | bytes 393224 | tf_op jit(solution)/shard_map/ppermute | solution.py:285
  132.7 15.2 %all-to-all-start.3 = ((f32[32,16,128]{2,1,0:T(8,128)}), f32[32,16,128]{2,1,0:T(8,128)S(1)}, u32[]{:S(2)}, u32[]{:S(2)}) async-start(f32[32,16,128]{2,1,0:T(8,128)} %suffix.1), calls=%async_computation.3 | async-start | bytes 524288 | tf_op jit(solution)/shard_map/all_to_all | solution.py:313
  147.8 9.1 %collective-permute-start.13 = (bf16[4,256,128]{2,1,0:T(8,128)(2,1)}, bf16[4,256,128]{2,1,0:T(8,128)(2,1)S(1)}, u32[]{:S(2)}, u32[]{:S(2)}) collective-permute-start(bf16[4,256,128]{2,1,0:T(8,128)(2,1)} %get-tuple-element.135), channel_id=1, source_target_pairs={{0,64},{8,72},{16,80},{24,88},{32,96},{40,104},{48,112},{56,120},{... | collective-permute-start | bytes 786440 | tf_op jit(solution)/shard_map/ppermute | solution.py:285
  148.7 8.3 %collective-permute-start.14 = (bf16[4,256,128]{2,1,0:T(8,128)(2,1)}, bf16[4,256,128]{2,1,0:T(8,128)(2,1)S(1)}, u32[]{:S(2)}, u32[]{:S(2)}) collective-permute-start(bf16[4,256,128]{2,1,0:T(8,128)(2,1)} %get-tuple-element.136), channel_id=1, source_target_pairs={{0,192},{8,200},{16,208},{24,216},{32,224},{40,232},{48,240},{56,2... | collective-permute-start | bytes 786440 | tf_op jit(solution)/shard_map/ppermute | solution.py:285
  150.5 8.3 %collective-permute-start.15 = (bf16[4,256,128]{2,1,0:T(8,128)(2,1)S(1)}, bf16[4,256,128]{2,1,0:T(8,128)(2,1)S(1)}, u32[]{:S(2)}, u32[]{:S(2)}) collective-permute-start(bf16[4,256,128]{2,1,0:T(8,128)(2,1)S(1)} %copy-done.14), channel_id=1, source_target_pairs={{0,16},{8,24},{16,32},{24,40},{32,48},{40,56},{48,0},{56,8},{64,80... | collective-permute-start | bytes 786440 | tf_op jit(solution)/shard_map/ppermute | solution.py:285
  151.3 7.5 %collective-permute-start.16 = (bf16[4,256,128]{2,1,0:T(8,128)(2,1)S(1)}, bf16[4,256,128]{2,1,0:T(8,128)(2,1)S(1)}, u32[]{:S(2)}, u32[]{:S(2)}) collective-permute-start(bf16[4,256,128]{2,1,0:T(8,128)(2,1)S(1)} %copy-done.13), channel_id=1, source_target_pairs={{0,48},{8,56},{16,0},{24,8},{32,16},{40,24},{48,32},{56,40},{64,11... | collective-permute-start | bytes 786440 | tf_op jit(solution)/shard_map/ppermute | solution.py:285
  162.6 8.0 %collective-permute-start.18 = (f32[128,128]{1,0:T(8,128)}, f32[128,128]{1,0:T(8,128)S(1)}, u32[]{:S(2)}, u32[]{:S(2)}) collective-permute-start(f32[128,128]{1,0:T(8,128)} %get-tuple-element.146), channel_id=1, source_target_pairs={{0,48},{8,56},{16,0},{24,8},{32,16},{40,24},{48,32},{56,40},{64,11... | collective-permute-start | bytes 196616 | tf_op jit(solution)/shard_map/ppermute | solution.py:285
  168.0 28.3 %collective-permute-start.11 = (bf16[512,512]{1,0:T(8,128)(2,1)}, bf16[512,512]{1,0:T(8,128)(2,1)S(1)}, u32[]{:S(2)}, u32[]{:S(2)}) collective-permute-start(bf16[512,512]{1,0:T(8,128)(2,1)} %get-tuple-element.124), channel_id=1, source_target_pairs={{0,1},{1,2},{2,3},{3,4},{4,5},{5,6},{6,7},{7,0},{8,9},{9,10},{10,1... | collective-permute-start | bytes 1572872 | tf_op jit(solution)/shard_map/ppermute | solution.py:273
  168.0 28.3 %collective-permute-start.12 = (bf16[512,512]{1,0:T(8,128)(2,1)}, bf16[512,512]{1,0:T(8,128)(2,1)S(1)}, u32[]{:S(2)}, u32[]{:S(2)}) collective-permute-start(bf16[512,512]{1,0:T(8,128)(2,1)} %get-tuple-element.125), channel_id=1, source_target_pairs={{0,7},{1,0},{2,1},{3,2},{4,3},{5,4},{6,5},{7,6},{8,15},{9,8},{10,9... | collective-permute-start | bytes 1572872 | tf_op jit(solution)/shard_map/ppermute | solution.py:273
  173.3 20.2 %collective-permute-start.22 = (f32[256,128]{1,0:T(8,128)}, f32[256,128]{1,0:T(8,128)S(1)}, u32[]{:S(2)}, u32[]{:S(2)}) collective-permute-start(f32[256,128]{1,0:T(8,128)} %get-tuple-element.150), channel_id=1, source_target_pairs={{0,48},{8,56},{16,0},{24,8},{32,16},{40,24},{48,32},{56,40},{64,11... | collective-permute-start | bytes 393224 | tf_op jit(solution)/shard_map/ppermute | solution.py:285
  176.0 17.5 %collective-permute-start.23 = (f32[256,128]{1,0:T(8,128)}, f32[256,128]{1,0:T(8,128)S(1)}, u32[]{:S(2)}, u32[]{:S(2)}) collective-permute-start(f32[256,128]{1,0:T(8,128)} %get-tuple-element.151), channel_id=1, source_target_pairs={{0,64},{8,72},{16,80},{24,88},{32,96},{40,104},{48,112},{56,120},{... | collective-permute-start | bytes 393224 | tf_op jit(solution)/shard_map/ppermute | solution.py:285
  178.8 14.7 %collective-permute-start.24 = (f32[256,128]{1,0:T(8,128)}, f32[256,128]{1,0:T(8,128)S(1)}, u32[]{:S(2)}, u32[]{:S(2)}) collective-permute-start(f32[256,128]{1,0:T(8,128)} %get-tuple-element.152), channel_id=1, source_target_pairs={{0,192},{8,200},{16,208},{24,216},{32,224},{40,232},{48,240},{56,2... | collective-permute-start | bytes 393224 | tf_op jit(solution)/shard_map/ppermute | solution.py:285
  (33 other events, 152.4 us)
Sparse Core Ops, SparseCore 0:
  9.8 64.2 all-gather.2

commit v4 on v2

v4 whole, which is shorter than its diff:
```python
import functools

import jax
import jax.numpy as jnp
from jax import lax
from jax.experimental import pallas as pl
from jax.experimental.pallas import tpu as pltpu
from jax.sharding import PartitionSpec as P

DH = 128
epsilon = 1e-06
VMEM = 63 << 20
WORK = 10**9
bf16, f32 = jnp.bfloat16, jnp.float32


def dot(a, b, left, right):
    return lax.dot_general(a, b, (((left,), (right,)), ((), ())), preferred_element_type=f32)


def split(x):
    high = x.astype(bf16)
    return high, (x - high.astype(f32)).astype(bf16)


def dot2(parts, b, left, right):
    return dot(parts[0], b, left, right) + dot(parts[1], b, left, right)


def dot2r(a, parts, left, right):
    return dot(a, parts[0], left, right) + dot(a, parts[1], left, right)


def shape(dims, dtype):
    return jax.ShapeDtypeStruct(dims, dtype)


def call(body, outs, args, name, far=(), far_outs=(), scalars=0, scratch=(), weight=1):
    specs = [pl.BlockSpec(memory_space=pltpu.SMEM)] * scalars
    for i in range(scalars, len(args)):
        specs.append(pl.BlockSpec(memory_space=pltpu.HBM if i in far else pltpu.VMEM))
    return pl.pallas_call(
        body,
        out_shape=tuple(outs),
        in_specs=specs,
        out_specs=tuple(
            pl.BlockSpec(memory_space=pltpu.HBM if i in far_outs else pltpu.VMEM)
            for i in range(len(outs))
        ),
        scratch_shapes=scratch,
        compiler_params=pltpu.CompilerParams(vmem_limit_bytes=VMEM),
        cost_estimate=pl.CostEstimate(
            flops=int(weight * WORK), bytes_accessed=1000, transcendentals=0
        ),
        name=name,
    )(*args)


def head(i):
    return slice(i * DH, (i + 1) * DH)


def state_body(left, right, out):
    for h in range(out.shape[0]):
        out[h] = dot(left[:, head(h)], right[:, head(h)], 0, 0)


def prefix_body(reverse, parts, out):
    count = parts.shape[0]
    state = jnp.zeros(parts.shape[1:], f32)
    for step in range(count):
        i = count - 1 - step if reverse else step
        out[i] = state
        state = state + parts[i]


def lower_mask(rows):
    return lax.broadcasted_iota(jnp.int32, (rows, rows), 0) >= lax.broadcasted_iota(
        jnp.int32, (rows, rows), 1
    )


def forward_body(q, k, v, prefix, attn, attn_t, mixed_out):
    rows = q.shape[0]
    mask = lower_mask(rows)
    for h in range(prefix.shape[0]):
        qh, kh, vh = q[:, head(h)], k[:, head(h)], v[:, head(h)]
        scores = split(jnp.where(mask, dot(qh, kh, 1, 1), 0.0))
        mixed = dot2(scores, vh, 1, 0) + dot2r(qh, split(prefix[h]), 1, 0)
        inverse = lax.rsqrt(jnp.mean(mixed * mixed, axis=-1, keepdims=True) + epsilon)
        normed = mixed * inverse
        mixed_out[:, head(h)] = mixed
        attn[:, head(h)] = normed.astype(bf16)
        attn_t[head(h), :] = normed.T.astype(bf16)


def project_body(me, gathered, w, mixed, q, attn_t, d_mixed, grads, keep, send, *scratch):
    blocks, weights, keeps, sends, sems, out_sems = scratch
    count, _, wide = blocks.shape
    groups = keep.shape[0] // count
    lanes = keep.shape[2]
    first = me[1] == 0
    copies, results = [], []
    for i in range(count):
        rows = pl.ds(i * wide, wide)
        copies.append(
            (
                pltpu.make_async_copy(gathered.at[i], blocks.at[i], sems.at[0, i]),
                pltpu.make_async_copy(w.at[rows, :], weights.at[rows, :], sems.at[1, i]),
            )
        )
        span = pl.ds(groups * i, groups)
        results.append(pltpu.make_async_copy(keeps.at[span], keep.at[span], out_sems.at[0, i]))
        results.append(pltpu.make_async_copy(sends.at[span], send.at[span], out_sems.at[1, i]))
    for pair in copies:
        pair[0].start()
        pair[1].start()
    total = None
    for i in range(count):
        copies[i][0].wait()
        copies[i][1].wait()
        term = dot(blocks[i], weights[i * wide : (i + 1) * wide, :], 1, 0)
        total = term if total is None else total + term
        terms = dot(attn_t[...], blocks[i], 1, 0)
        for j in range(groups):
            even = terms[:, 2 * j * lanes : (2 * j + 1) * lanes]
            odd = terms[:, (2 * j + 1) * lanes : (2 * j + 2) * lanes]
            keeps[groups * i + j] = jnp.where(first, even, odd).astype(bf16)
            sends[groups * i + j] = jnp.where(first, odd, even).astype(bf16)
        results[2 * i].start()
        results[2 * i + 1].start()
    for h in range(grads.shape[0]):
        d_attn, m = total[:, head(h)], mixed[:, head(h)]
        inverse = lax.rsqrt(jnp.mean(m * m, axis=-1, keepdims=True) + epsilon)
        normed = m * inverse
        d_m = inverse * (d_attn - normed * jnp.mean(d_attn * normed, axis=-1, keepdims=True))
        d_m = d_m.astype(bf16)
        d_mixed[:, head(h)] = d_m
        grads[h] = dot(q[:, head(h)], d_m, 0, 0)
    for copy in results:
        copy.wait()


def backward_body(q, k, v, d_mixed, prefix, grad_q, part_k, part_v):
    rows = q.shape[0]
    low = lower_mask(rows)
    high = lax.broadcasted_iota(jnp.int32, (rows, rows), 0) <= lax.broadcasted_iota(
        jnp.int32, (rows, rows), 1
    )
    for h in range(prefix.shape[0]):
        qh, kh, vh, dh = q[:, head(h)], k[:, head(h)], v[:, head(h)], d_mixed[:, head(h)]
        d_scores = split(jnp.where(low, dot(dh, vh, 1, 1), 0.0))
        grad_q[:, head(h)] = (
            dot2(d_scores, kh, 1, 0) + dot2r(dh, split(prefix[h]), 1, 1)
        ).astype(bf16)
        d_scores_t = split(jnp.where(high, dot(vh, dh, 1, 1), 0.0))
        part_k[:, head(h)] = dot2(d_scores_t, qh, 1, 0)
        scores_t = split(jnp.where(high, dot(kh, qh, 1, 1), 0.0))
        part_v[:, head(h)] = dot2(scores_t, dh, 1, 0)


def finish_body(me, k, v, part_k, part_v, states, grad_k, grad_v, held, sems):
    count = held.shape[0]
    copies = [pltpu.make_async_copy(states.at[i], held.at[i], sems.at[i]) for i in range(count)]
    for copy in copies:
        copy.start()
    for copy in copies:
        copy.wait()
    for h in range(held.shape[1]):
        later = jnp.zeros(held.shape[2:], f32)
        for i in range(count - 1, 0, -1):
            later = later + jnp.where(me[2] < i, held[i, h].astype(f32), 0.0)
        after = split(later)
        grad_k[:, head(h)] = (part_k[:, head(h)] + dot2r(v[:, head(h)], after, 1, 1)).astype(bf16)
        grad_v[:, head(h)] = (part_v[:, head(h)] + dot2r(k[:, head(h)], after, 1, 0)).astype(bf16)


def pair_body(keep, received, out):
    for i in range(keep.shape[0]):
        out[i] = (keep[i].astype(f32) + received[i].astype(f32)).astype(bf16)


def sum_body(parts, out):
    total = parts[0].astype(f32)
    for i in range(1, parts.shape[0]):
        total = total + parts[i].astype(f32)
    out[...] = total.T


def rows_of(me, w, offsets, weights, sems):
    ring = w.shape[0] // w.shape[1]
    wide = w.shape[1]
    copies = []
    for i, offset in enumerate(offsets):
        start = pl.multiple_of(lax.rem(me[0] + offset, ring) * wide, wide)
        copies.append(
            pltpu.make_async_copy(w.at[pl.ds(start, wide), :], weights.at[i], sems.at[i])
        )
    for copy in copies:
        copy.start()
    return copies


def out_body(me, attn, w, terms, top, bottom, low, high, weights, sems):
    ring = weights.shape[0]
    half = attn.shape[0] // 2
    copies = rows_of(me, w, range(ring), weights, sems)
    for i in range(ring):
        copies[i].wait()
        term = dot(attn[...], weights[i], 1, 1)
        if i == ring // 2:
            top[...] = term[:half].astype(bf16)
            bottom[...] = term[half:].astype(bf16)
        else:
            terms[i] = term
        if i == ring // 2 - 1:
            low[...] = term[half:].astype(bf16)
        if i == ring // 2 + 1:
            high[...] = term[:half].astype(bf16)


def shift(x, axis, amount):
    count = lax.axis_size(axis)
    return lax.ppermute(x, axis, [(i, (i + amount) % count) for i in range(count)])


tie = lax.optimization_barrier


def per_device(queries, keys, values, w_out, grad_out):
    length, features = queries.shape
    heads = features // DH
    half = length // 2
    ring = lax.axis_size("head")
    count = lax.axis_size("seq")
    me = jnp.stack([lax.axis_index("head"), lax.axis_index("seq") % 2, lax.axis_index("seq")])
    me = me.astype(jnp.int32)
    block = shape((length, features), bf16)
    half_block = shape((half, features), bf16)
    wide_block = shape((length, features), f32)
    states = shape((heads, DH, DH), f32)

    def exchange(parts):
        return lax.all_to_all(parts, "seq", 0, 0, tiled=True)

    def sums(parts, reverse, name):
        body = functools.partial(prefix_body, reverse)
        return call(body, [shape(parts.shape, f32)], [parts], name)[0]

    def pieces_of(state):
        return state.reshape(count, -1, DH)

    def hop(pair):
        pair = tie(tuple(pair))
        return tie((shift(pair[0], "head", 1), shift(pair[1], "head", -1)))

    def out_step(pair, number):
        outs = []
        for i, term in enumerate((terms_out[number], terms_out[ring - number])):
            got = pair[i].astype(f32)
            if got.shape[0] == half and i == 0:
                parts = [(term[:half] + got).astype(bf16), low]
                outs.append(jnp.concatenate(parts, axis=0))
            elif got.shape[0] == half:
                parts = [high, (term[half:] + got).astype(bf16)]
                outs.append(jnp.concatenate(parts, axis=0))
            else:
                outs.append((term + got).astype(bf16))
        return outs

    gathered = lax.all_gather(grad_out, "head")
    (local_state,) = call(state_body, [states], [keys, values], "state")
    prefix = exchange(sums(exchange(pieces_of(local_state)), False, "prefix")).reshape(states.shape)
    attn, attn_t, mixed = call(
        forward_body,
        [block, shape((features, length), bf16), wide_block],
        [queries, keys, values, prefix],
        "forward",
    )
    wide_terms = shape((ring, length, features), f32)
    terms_out, top, bottom, low, high = call(
        out_body,
        [wide_terms] + [half_block] * 4,
        [me, attn, w_out],
        "out_terms",
        far=(2,),
        scalars=1,
        scratch=[pltpu.VMEM((ring, features, features), bf16), pltpu.SemaphoreType.DMA((ring,))],
    )
    gathered, *pair = tie((gathered, top, bottom))
    pair = hop(pair)
    dims = (count // 2, features, w_out.shape[0] // count)
    d_mixed, local_grads, keep, send = call(
        project_body,
        [block, states, shape(dims, bf16), shape(dims, bf16)],
        [me, gathered, w_out, mixed, queries, attn_t],
        "project",
        far=(1, 2),
        far_outs=(2, 3),
        scalars=1,
        scratch=[
            pltpu.VMEM((ring, length, features), bf16),
            pltpu.VMEM(w_out.shape, bf16),
            pltpu.VMEM(dims, bf16),
            pltpu.VMEM(dims, bf16),
            pltpu.SemaphoreType.DMA((2, ring)),
            pltpu.SemaphoreType.DMA((2, ring)),
        ],
    )
    state_all = lax.all_gather(local_grads.astype(bf16), "seq")
    received = lax.ppermute(send, "seq", [(i, i ^ 1) for i in range(count)])
    (terms,) = call(pair_body, [shape(dims, bf16)], [keep, received], "pair_add")
    pair = tie((*pair, terms))[:2]
    pair = out_step(pair, ring // 2 - 1)
    after_one = tie((d_mixed, *pair))[0]
    pair = hop(pair)
    grad_q, part_k, part_v = call(
        backward_body,
        [block, wide_block, wide_block],
        [queries, keys, values, after_one, prefix],
        "backward",
    )
    terms = tie((terms, grad_q))[0]
    groups = [[2 * chip + core for chip in range(count // 2)] for core in range(2)]
    terms = lax.all_to_all(terms, "seq", 0, 0, axis_index_groups=groups, tiled=True)
    pair = tie((*pair, grad_q))[:2]
    pair = out_step(pair, ring // 2 - 2)
    pair = out_step(hop(pair), ring // 2 - 3)
    terms = tie((terms, *pair))[0]
    state_all = tie((state_all, *pair))[0]
    pair = hop(pair)
    (grad_w_out,) = call(sum_body, [shape((dims[2], dims[1]), f32)], [terms], "weight_sum")
    grad_k, grad_v = call(
        finish_body,
        [block, block],
        [me, keys, values, part_k, part_v, state_all],
        "finish",
        far=(5,),
        scalars=1,
        scratch=[pltpu.VMEM(state_all.shape, bf16), pltpu.SemaphoreType.DMA((count,))],
    )
    pair = tie((*pair, grad_k))[:2]
    layer_out = (terms_out[0] + pair[0].astype(f32) + pair[1].astype(f32)).astype(bf16)
    return layer_out, grad_q, grad_k, grad_v, grad_w_out


def solution(mesh):
    return jax.shard_map(
        per_device,
        mesh=mesh,
        in_specs=(
            P("seq", "head"),
            P("seq", "head"),
            P("seq", "head"),
            P(None, "head"),
            P("seq", "head"),
        ),
        out_specs=(
            P("seq", "head"),
            P("seq", "head"),
            P("seq", "head"),
            P("seq", "head"),
            P("seq", "head"),
        ),
        check_vma=False,
    )
```

time: 186 us -> 171 us (0.919)
  blocking collectives: 33.5 us -> 17.7 us
  other arithmetic: 0.62 us -> 11.9 us
  Pallas kernels: 58.5 us -> 50.5 us
  starting transfers between devices: 29.6 us -> 22 us
  waiting for transfers between devices: 46.6 us -> 53.4 us
    all_to_all x1, waiting for transfers between devices: 25.7 us -> 6.61 us  [per_device(): lax.all_to_all(terms, 'seq', 0, 0, axis_index_groups=groups, tiled=True)]
    all_to_all x2 -> x1, blocking collectives: 33.5 us -> 17.7 us  [exchange(): return lax.all_to_all(parts, 'seq', 0, 0, tiled=True)]
    ppermute x8, waiting for transfers between devices: 12.4 us -> 26.5 us  [shift(): lax.ppermute(x, axis, [(i, (i + amount) % count) for i in range(count)])]
    all_gather x0 -> x2, waiting for transfers between devices: none -> 11.1 us  [the longest x1 11.1 us: per_device(): gathered = lax.all_gather(grad_out, 'head')]
    convert_element_type x0 -> x5, other arithmetic: none -> 9.52 us  [the longest x2 4.14 us: out_step(): outs.append((term + got).astype(bf16))]
    pallas_call x13 -> x9, Pallas kernels: 58.5 us -> 50.5 us  [call(): pl.pallas_call(body, out_shape=tuple(outs), in_specs=specs, out_specs=tup...]
    all_to_all x2 -> x1, starting transfers between devices: 9.57 us -> 3.71 us  [exchange(): return lax.all_to_all(parts, 'seq', 0, 0, tiled=True)]
    ppermute x8, starting transfers between devices: 13.9 us -> 10.9 us  [shift(): lax.ppermute(x, axis, [(i, (i + amount) % count) for i in range(count)])]
  transfers between devices with their start and end apart: 14 -> 13, of which waited for: 4 -> 6; matrix products, arithmetic and copies ran while one was open for 1% -> 5% of each run, Pallas kernels for 32% -> 19%
where the time goes in v4:
time: 171 us; the launch traced here: 170 us
  waiting for transfers between devices  53.4 us (31%)
  Pallas kernels  50.5 us (30%)
  starting transfers between devices  22 us (13%)
  blocking collectives  17.7 us (10%)
  between operations  14.2 us (8%)
  other arithmetic  11.9 us (7%)
    pallas_call x9, Pallas kernels, call(): pl.pallas_call(body, out_shape=tuple(outs), in_specs=specs, out_specs=tup...  50.5 us
    ppermute x8, waiting for transfers between devices, shift(): lax.ppermute(x, axis, [(i, (i + amount) % count) for i in range(count)])  26.5 us
    all_to_all x1, blocking collectives, exchange(): return lax.all_to_all(parts, 'seq', 0, 0, tiled=True)  17.7 us
    all_gather x1, waiting for transfers between devices, per_device(): gathered = lax.all_gather(grad_out, 'head')  11.1 us
    ppermute x8, starting transfers between devices, shift(): lax.ppermute(x, axis, [(i, (i + amount) % count) for i in range(count)])  10.9 us
    all_to_all x1, waiting for transfers between devices, exchange(): return lax.all_to_all(parts, 'seq', 0, 0, tiled=True)  8.44 us
    all_to_all x1, waiting for transfers between devices, per_device(): lax.all_to_all(terms, 'seq', 0, 0, axis_index_groups=groups, tiled=True)  6.61 us
    all_to_all x1, starting transfers between devices, per_device(): lax.all_to_all(terms, 'seq', 0, 0, axis_index_groups=groups, tiled=True)  6.61 us
  transfers between devices with their start and end apart: 13, of which 6 were waited for; matrix products, arithmetic and copies ran while one was open for 5% of the time, Pallas kernels for 19%

profile of v4, /device:TPU:1, one launch (start us, length us, event | category | flops | bytes accessed | tf_op | source)
XLA Modules:
  0.0 170.4 jit_solution(7842321599091489799)
XLA Ops:
  7.9 2.3 %state.1 = f32[4,128,128]{2,1,0:T(8,128)} custom-call(bf16[512,512]{1,0:T(8,128)(2,1)} %k.5, bf16[512,512]{1,0:T(8,128)(2,1)} %v.5), custom_call_target="tpu_custom_call" | custom-call | flops 1000000000 | bytes 1000 | tf_op jit(solution)/shard_map/state/pallas_call | solution.py:42
  10.2 17.7 %all_to_all.15.parts = f32[32,16,128]{2,1,0:T(8,128)} all-to-all(f32[32,16,128]{2,1,0:T(8,128)} %bitcast.41), channel_id=1, replica_groups=mesh['seq'=32,'head'=8] {'seq'}, dimensions={0} | all-to-all | bytes 524288 | tf_op jit(solution)/shard_map/all_to_all | solution.py:244
  29.5 3.7 %all-to-all-start.1 = ((f32[32,16,128]{2,1,0:T(8,128)}), f32[32,16,128]{2,1,0:T(8,128)S(1)}, u32[]{:S(2)}, u32[]{:S(2)}) async-start(f32[32,16,128]{2,1,0:T(8,128)} %prefix.1), calls=%async_computation.1 | async-start | bytes 524288 | tf_op jit(solution)/shard_map/all_to_all | solution.py:244
  33.9 8.4 %all-to-all-done.1 = f32[32,16,128]{2,1,0:T(8,128)S(1)} async-done(((f32[32,16,128]{2,1,0:T(8,128)}), f32[32,16,128]{2,1,0:T(8,128)S(1)}, u32[]{:S(2)}, u32[]{:S(2)}) %all-to-all-start.1) | async-done | bytes 262176 | tf_op jit(solution)/shard_map/all_to_all | solution.py:244
  43.0 5.0 %forward.1 = (bf16[512,512]{1,0:T(8,128)(2,1)}, bf16[512,512]{1,0:T(8,128)(2,1)}, f32[512,512]{1,0:T(8,128)}) custom-call(bf16[512,512]{1,0:T(8,128)(2,1)} %q.5, bf16[512,512]{1,0:T(8,128)(2,1)} %k.5, bf16[512,512]{1,0:T(8,128)(2,1)} %v.5, f32[4,128,128]{2,1,0:T(8,128)} %bitcast.39), custom_call_target="tpu_custom_call" | custom-call | flops 1000000000 | bytes 1000 | tf_op jit(solution)/shard_map/forward/pallas_call | solution.py:42
  48.1 9.2 %out_terms.1 = (f32[8,512,512]{2,1,0:T(8,128)}, bf16[256,512]{1,0:T(8,128)(2,1)}, bf16[256,512]{1,0:T(8,128)(2,1)}, bf16[256,512]{1,0:T(8,128)(2,1)}, bf16[256,512]{1,0:T(8,128)(2,1)}) custom-call(s32[3]{0:T(128)} %pad_add_fusion.me, bf16[512,512]{1,0:T(8,128)(2,1)} %get-tuple-element.51.attn, bf16[4096,512]{1,0:T(8,128)(2,1)} %w.3), custom_call_target="tpu_custom_call" | custom-call | flops 1000000000 | bytes 1000 | tf_op jit(solution)/shard_map/out_terms/pallas_call | solution.py:42
  57.3 11.1 %all-gather.5.cloned.1.call-done = bf16[4096,512]{1,0:T(8,128)(2,1)} async-done(((bf16[512,512]{1,0:T(8,128)(2,1)}), bf16[4096,512]{1,0:T(8,128)(2,1)}) %all-gather.5.cloned.1.call-update) | async-done | bytes 4194320 | tf_op jit(solution)/shard_map/all_gather | solution.py:271
  68.4 10.6 %project.1 = (bf16[512,512]{1,0:T(8,128)(2,1)}, f32[4,128,128]{2,1,0:T(8,128)}, bf16[16,512,128]{2,1,0:T(8,128)(2,1)}, bf16[16,512,128]{2,1,0:T(8,128)(2,1)}) custom-call(s32[3]{0:T(128)} %pad_add_fusion.me, bf16[8,512,512]{2,1,0:T(8,128)(2,1)} %bitcast.38, bf16[4096,512]{1,0:T(8,128)(2,1)} %w.3, f32[512,512]{1,0:T(8,128)} %get-tuple-element.62.mixed, ...), custom_call_target="tpu_custom_call" | custom-call | flops 1000000000 | bytes 1000 | tf_op jit(solution)/shard_map/project/pallas_call | solution.py:42
  81.4 2.7 %collective-permute-start.1 = (bf16[256,512]{1,0:T(8,128)(2,1)S(1)}, bf16[256,512]{1,0:T(8,128)(2,1)S(1)}, u32[]{:S(2)}, u32[]{:S(2)}) collective-permute-start(bf16[256,512]{1,0:T(8,128)(2,1)S(1)} %copy-done.2), channel_id=1, source_target_pairs={{0,7},{1,0},{2,1},{3,2},{4,3},{5,4},{6,5},{7,6},{8,15},{9,8},{10,9... | collective-permute-start | bytes 786440 | tf_op jit(solution)/shard_map/ppermute | solution.py:224
  84.1 6.6 %collective-permute-done = bf16[256,512]{1,0:T(8,128)(2,1)S(1)} collective-permute-done((bf16[256,512]{1,0:T(8,128)(2,1)}, bf16[256,512]{1,0:T(8,128)(2,1)S(1)}, u32[]{:S(2)}, u32[]{:S(2)}) %collective-permute-start) | collective-permute-done | bytes 262176 | tf_op jit(solution)/shard_map/ppermute | solution.py:224
  90.7 4.1 %pair_add.1 = bf16[16,512,128]{2,1,0:T(8,128)(2,1)} custom-call(bf16[16,512,128]{2,1,0:T(8,128)(2,1)} %get-tuple-element.64.keep, bf16[16,512,128]{2,1,0:T(8,128)(2,1)} %collective-permute-done.2.received), custom_call_target="tpu_custom_call" | custom-call | flops 1000000000 | bytes 1000 | tf_op jit(solution)/shard_map/pair_add/pallas_call | solution.py:42
  98.4 2.4 %collective-permute-start.4 = (bf16[512,512]{1,0:T(8,128)(2,1)S(1)}, bf16[512,512]{1,0:T(8,128)(2,1)}, u32[]{:S(2)}, u32[]{:S(2)}) collective-permute-start(bf16[512,512]{1,0:T(8,128)(2,1)S(1)} %get-tuple-element.71), channel_id=1, source_target_pairs={{0,7},{1,0},{2,1},{3,2},{4,3},{5,4},{6,5},{7,6},{8,15},{9,8},{10,9... | collective-permute-start | bytes 1572872 | tf_op jit(solution)/shard_map/ppermute | solution.py:224
  100.7 8.3 %backward.1 = (bf16[512,512]{1,0:T(8,128)(2,1)}, f32[512,512]{1,0:T(8,128)}, f32[512,512]{1,0:T(8,128)}) custom-call(bf16[512,512]{1,0:T(8,128)(2,1)} %q.5, bf16[512,512]{1,0:T(8,128)(2,1)} %k.5, bf16[512,512]{1,0:T(8,128)(2,1)} %v.5, bf16[512,512]{1,0:T(8,128)(2,1)} %get-tuple-element.75.d_mixed, f32[4,128,128]{2,1,0:T(8,128)} %bitcast.40), custom_call_target="tpu_custom_call" | custom-call | flops 1000000000 | bytes 1000 | tf_op jit(solution)/shard_map/backward/pallas_call | solution.py:42
  109.0 6.6 %all-to-all-start.2 = ((bf16[16,512,128]{2,1,0:T(8,128)(2,1)}), bf16[16,512,128]{2,1,0:T(8,128)(2,1)}, u32[]{:S(2)}, u32[]{:S(2)}) async-start(bf16[16,512,128]{2,1,0:T(8,128)(2,1)} %pair_add.1), calls=%async_computation.2 | async-start | bytes 4194304 | tf_op jit(solution)/shard_map/all_to_all | solution.py:325
  115.6 2.2 %fusion.1 = (bf16[512,512]{1,0:T(8,128)(2,1)S(1)}, bf16[512,512]{1,0:T(8,128)(2,1)S(1)}) fusion(bf16[512,512]{1,0:T(8,128)(2,1)} %collective-permute-done.4, f32[8,512,512]{2,1,0:T(8,128)} %get-tuple-element.52, bf16[512,512]{1,0:T(8,128)(2,1)} %collective-permute-done.3), kind=kLoop, calls=%fused_computation.3 | loop fusion | flops 1572864 | bytes 4194304 | tf_op jit(solution)/shard_map/convert_element_type | solution.py:268
  117.9 2.7 %collective-permute-start.6 = (bf16[512,512]{1,0:T(8,128)(2,1)S(1)}, bf16[512,512]{1,0:T(8,128)(2,1)S(1)}, u32[]{:S(2)}, u32[]{:S(2)}) collective-permute-start(bf16[512,512]{1,0:T(8,128)(2,1)S(1)} %get-tuple-element.80), channel_id=1, source_target_pairs={{0,7},{1,0},{2,1},{3,2},{4,3},{5,4},{6,5},{7,6},{8,15},{9,8},{10,9... | collective-permute-start | bytes 1572872 | tf_op jit(solution)/shard_map/ppermute | solution.py:224
  120.6 10.3 %collective-permute-done.5 = bf16[512,512]{1,0:T(8,128)(2,1)S(1)} collective-permute-done((bf16[512,512]{1,0:T(8,128)(2,1)S(1)}, bf16[512,512]{1,0:T(8,128)(2,1)S(1)}, u32[]{:S(2)}, u32[]{:S(2)}) %collective-permute-start.5) | collective-permute-done | bytes 524320 | tf_op jit(solution)/shard_map/ppermute | solution.py:224
  130.9 2.0 %fusion = (bf16[512,512]{1,0:T(8,128)(2,1)S(1)}, bf16[512,512]{1,0:T(8,128)(2,1)S(1)}) fusion(bf16[512,512]{1,0:T(8,128)(2,1)S(1)} %collective-permute-done.6, f32[8,512,512]{2,1,0:T(8,128)} %get-tuple-element.52, bf16[512,512]{1,0:T(8,128)(2,1)S(1)} %collective-permute-done.5), kind=kLoop, calls=%fused_computation.1 | loop fusion | flops 1572864 | bytes 4194304 | tf_op jit(solution)/shard_map/convert_element_type | solution.py:268
  133.0 2.7 %collective-permute-start.8 = (bf16[512,512]{1,0:T(8,128)(2,1)S(1)}, bf16[512,512]{1,0:T(8,128)(2,1)}, u32[]{:S(2)}, u32[]{:S(2)}) collective-permute-start(bf16[512,512]{1,0:T(8,128)(2,1)S(1)} %get-tuple-element.84), channel_id=1, source_target_pairs={{0,7},{1,0},{2,1},{3,2},{4,3},{5,4},{6,5},{7,6},{8,15},{9,8},{10,9... | collective-permute-start | bytes 1572872 | tf_op jit(solution)/shard_map/ppermute | solution.py:224
  135.6 9.5 %collective-permute-done.7 = bf16[512,512]{1,0:T(8,128)(2,1)S(1)} collective-permute-done((bf16[512,512]{1,0:T(8,128)(2,1)S(1)}, bf16[512,512]{1,0:T(8,128)(2,1)S(1)}, u32[]{:S(2)}, u32[]{:S(2)}) %collective-permute-start.7) | collective-permute-done | bytes 524320 | tf_op jit(solution)/shard_map/ppermute | solution.py:224
  145.2 6.6 %all-to-all-done.2.parts = bf16[16,512,128]{2,1,0:T(8,128)(2,1)} async-done(((bf16[16,512,128]{2,1,0:T(8,128)(2,1)}), bf16[16,512,128]{2,1,0:T(8,128)(2,1)}, u32[]{:S(2)}, u32[]{:S(2)}) %all-to-all-start.2) | async-done | bytes 2097184 | tf_op jit(solution)/shard_map/all_to_all | solution.py:325
  151.8 2.6 %weight_sum.1 = f32[128,512]{1,0:T(8,128)} custom-call(bf16[16,512,128]{2,1,0:T(8,128)(2,1)} %all-to-all-done.2.parts), custom_call_target="tpu_custom_call" | custom-call | flops 1000000000 | bytes 1000 | tf_op jit(solution)/shard_map/weight_sum/pallas_call | solution.py:42
  154.4 6.7 %finish.1 = (bf16[512,512]{1,0:T(8,128)(2,1)}, bf16[512,512]{1,0:T(8,128)(2,1)}) custom-call(s32[3]{0:T(128)} %pad_add_fusion.me, bf16[512,512]{1,0:T(8,128)(2,1)} %k.5, bf16[512,512]{1,0:T(8,128)(2,1)} %v.5, f32[512,512]{1,0:T(8,128)} %get-tuple-element.87.part_k, f32[512,512]{1,0:T(8,128)} %get-tuple-element.88.part_v, bf16[32,4,128,128]{3,2,1,0:T(8,128)(2,1)} %bitcast.37), custom_call_target="tpu_custom_call" | custom-call | flops 1000000000 | bytes 1000 | tf_op jit(solution)/shard_map/finish/pallas_call | solution.py:42
  161.2 2.4 %fusion.5 = bf16[512,512]{1,0:T(8,128)(2,1)} fusion(bf16[512,512]{1,0:T(8,128)(2,1)} %collective-permute-done.8, bf16[512,512]{1,0:T(8,128)(2,1)S(1)} %collective-permute-done.7, f32[8,512,512]{2,1,0:T(8,128)} %get-tuple-element.52), kind=kLoop, calls=%fused_computation.10 | loop fusion | flops 1310720 | bytes 2621440 | tf_op jit(solution)/shard_map/convert_element_type | solution.py:343
  (27 shorter events, 9.8 us)
Async XLA Ops:
  7.2 61.3 %all-gather.5.cloned.1.call-start = ((), (), s32[]{:S(2)}) async-start(), calls=%async_computation.3 | async-start | bytes 4718592 | tf_op jit(solution)/shard_map/all_gather | solution.py:271
  29.5 12.8 %all-to-all-start.1 = ((f32[32,16,128]{2,1,0:T(8,128)}), f32[32,16,128]{2,1,0:T(8,128)S(1)}, u32[]{:S(2)}, u32[]{:S(2)}) async-start(f32[32,16,128]{2,1,0:T(8,128)} %prefix.1), calls=%async_computation.1 | async-start | bytes 524288 | tf_op jit(solution)/shard_map/all_to_all | solution.py:244
  33.2 121.2 %all-gather.7.cloned.1.call-start = ((), (), s32[]{:S(2)}) async-start(), calls=%async_computation.4 | async-start | bytes 4325376 | tf_op jit(solution)/shard_map/all_gather | solution.py:310
  42.3 0.7 copy-start
  68.4 13.0 %copy-start.2 = (bf16[256,512]{1,0:T(8,128)(2,1)S(1)}, bf16[256,512]{1,0:T(8,128)(2,1)}, u32[]{:S(2)}) copy-start(bf16[256,512]{1,0:T(8,128)(2,1)} %get-tuple-element.58) | copy-start | bytes 786436
  80.7 10.1 %collective-permute-start.2 = (bf16[16,512,128]{2,1,0:T(8,128)(2,1)}, bf16[16,512,128]{2,1,0:T(8,128)(2,1)}, u32[]{:S(2)}, u32[]{:S(2)}) collective-permute-start(bf16[16,512,128]{2,1,0:T(8,128)(2,1)} %get-tuple-element.65), channel_id=1, source_target_pairs={{0,8},{8,0},{16,24},{24,16},{32,40},{40,32},{48,56},{56,48},{64,72... | collective-permute-start | bytes 6291464 | tf_op jit(solution)/shard_map/ppermute | solution.py:311
  81.4 9.3 %collective-permute-start = (bf16[256,512]{1,0:T(8,128)(2,1)}, bf16[256,512]{1,0:T(8,128)(2,1)S(1)}, u32[]{:S(2)}, u32[]{:S(2)}) collective-permute-start(bf16[256,512]{1,0:T(8,128)(2,1)} %get-tuple-element.57), channel_id=1, source_target_pairs={{0,1},{1,2},{2,3},{3,4},{4,5},{5,6},{6,7},{7,0},{8,9},{9,10},{10,1... | collective-permute-start | bytes 786440 | tf_op jit(solution)/shard_map/ppermute | solution.py:224
  81.4 9.3 %collective-permute-start.1 = (bf16[256,512]{1,0:T(8,128)(2,1)S(1)}, bf16[256,512]{1,0:T(8,128)(2,1)S(1)}, u32[]{:S(2)}, u32[]{:S(2)}) collective-permute-start(bf16[256,512]{1,0:T(8,128)(2,1)S(1)} %copy-done.2), channel_id=1, source_target_pairs={{0,7},{1,0},{2,1},{3,2},{4,3},{5,4},{6,5},{7,6},{8,15},{9,8},{10,9... | collective-permute-start | bytes 786440 | tf_op jit(solution)/shard_map/ppermute | solution.py:224
  90.7 5.5 %copy-start.1 = (bf16[256,512]{1,0:T(8,128)(2,1)S(1)}, bf16[256,512]{1,0:T(8,128)(2,1)}, u32[]{:S(2)}) copy-start(bf16[256,512]{1,0:T(8,128)(2,1)} %get-tuple-element.67) | copy-start | bytes 786436
  98.1 17.6 %collective-permute-start.3 = (bf16[512,512]{1,0:T(8,128)(2,1)}, bf16[512,512]{1,0:T(8,128)(2,1)}, u32[]{:S(2)}, u32[]{:S(2)}) collective-permute-start(bf16[512,512]{1,0:T(8,128)(2,1)} %get-tuple-element.70), channel_id=1, source_target_pairs={{0,1},{1,2},{2,3},{3,4},{4,5},{5,6},{6,7},{7,0},{8,9},{9,10},{10,1... | collective-permute-start | bytes 1572872 | tf_op jit(solution)/shard_map/ppermute | solution.py:224
  98.4 17.3 %collective-permute-start.4 = (bf16[512,512]{1,0:T(8,128)(2,1)S(1)}, bf16[512,512]{1,0:T(8,128)(2,1)}, u32[]{:S(2)}, u32[]{:S(2)}) collective-permute-start(bf16[512,512]{1,0:T(8,128)(2,1)S(1)} %get-tuple-element.71), channel_id=1, source_target_pairs={{0,7},{1,0},{2,1},{3,2},{4,3},{5,4},{6,5},{7,6},{8,15},{9,8},{10,9... | collective-permute-start | bytes 1572872 | tf_op jit(solution)/shard_map/ppermute | solution.py:224
  109.0 42.8 %all-to-all-start.2 = ((bf16[16,512,128]{2,1,0:T(8,128)(2,1)}), bf16[16,512,128]{2,1,0:T(8,128)(2,1)}, u32[]{:S(2)}, u32[]{:S(2)}) async-start(bf16[16,512,128]{2,1,0:T(8,128)(2,1)} %pair_add.1), calls=%async_computation.2 | async-start | bytes 4194304 | tf_op jit(solution)/shard_map/all_to_all | solution.py:325
  117.8 13.1 %collective-permute-start.5 = (bf16[512,512]{1,0:T(8,128)(2,1)S(1)}, bf16[512,512]{1,0:T(8,128)(2,1)S(1)}, u32[]{:S(2)}, u32[]{:S(2)}) collective-permute-start(bf16[512,512]{1,0:T(8,128)(2,1)S(1)} %get-tuple-element.79), channel_id=1, source_target_pairs={{0,1},{1,2},{2,3},{3,4},{4,5},{5,6},{6,7},{7,0},{8,9},{9,10},{10,1... | collective-permute-start | bytes 1572872 | tf_op jit(solution)/shard_map/ppermute | solution.py:224
  117.9 13.0 %collective-permute-start.6 = (bf16[512,512]{1,0:T(8,128)(2,1)S(1)}, bf16[512,512]{1,0:T(8,128)(2,1)S(1)}, u32[]{:S(2)}, u32[]{:S(2)}) collective-permute-start(bf16[512,512]{1,0:T(8,128)(2,1)S(1)} %get-tuple-element.80), channel_id=1, source_target_pairs={{0,7},{1,0},{2,1},{3,2},{4,3},{5,4},{6,5},{7,6},{8,15},{9,8},{10,9... | collective-permute-start | bytes 1572872 | tf_op jit(solution)/shard_map/ppermute | solution.py:224
  132.9 12.3 %collective-permute-start.7 = (bf16[512,512]{1,0:T(8,128)(2,1)S(1)}, bf16[512,512]{1,0:T(8,128)(2,1)S(1)}, u32[]{:S(2)}, u32[]{:S(2)}) collective-permute-start(bf16[512,512]{1,0:T(8,128)(2,1)S(1)} %get-tuple-element.83), channel_id=1, source_target_pairs={{0,1},{1,2},{2,3},{3,4},{4,5},{5,6},{6,7},{7,0},{8,9},{9,10},{10,1... | collective-permute-start | bytes 1572872 | tf_op jit(solution)/shard_map/ppermute | solution.py:224
  133.0 12.2 %collective-permute-start.8 = (bf16[512,512]{1,0:T(8,128)(2,1)S(1)}, bf16[512,512]{1,0:T(8,128)(2,1)}, u32[]{:S(2)}, u32[]{:S(2)}) collective-permute-start(bf16[512,512]{1,0:T(8,128)(2,1)S(1)} %get-tuple-element.84), channel_id=1, source_target_pairs={{0,7},{1,0},{2,1},{3,2},{4,3},{5,4},{6,5},{7,6},{8,15},{9,8},{10,9... | collective-permute-start | bytes 1572872 | tf_op jit(solution)/shard_map/ppermute | solution.py:224
Sparse Core Ops, SparseCore 0:
  9.8 58.6 all-gather.4
  80.8 70.5 all-gather.6

commit v5 on v4

--- a/solution.py
+++ b/solution.py
@@ -320,7 +320,6 @@
         [queries, keys, values, after_one, prefix],
         "backward",
     )
-    terms = tie((terms, grad_q))[0]
     groups = [[2 * chip + core for chip in range(count // 2)] for core in range(2)]
     terms = lax.all_to_all(terms, "seq", 0, 0, axis_index_groups=groups, tiled=True)
     pair = tie((*pair, grad_q))[:2]
@@ -339,7 +338,6 @@
         scalars=1,
         scratch=[pltpu.VMEM(state_all.shape, bf16), pltpu.SemaphoreType.DMA((count,))],
     )
-    pair = tie((*pair, grad_k))[:2]
     layer_out = (terms_out[0] + pair[0].astype(f32) + pair[1].astype(f32)).astype(bf16)
     return layer_out, grad_q, grad_k, grad_v, grad_w_out
 

time: 171 us -> 166 us (0.971); the launches traced: 170 us -> 164 us
  waiting for transfers between devices: 53.4 us -> 46.7 us
    all_to_all x1, waiting for transfers between devices: 6.61 us -> 0.01 us  [per_device(): lax.all_to_all(terms, 'seq', 0, 0, axis_index_groups=groups, tiled=True)]
  transfers between devices with their start and end apart: 13 -> 13, of which waited for: 6 -> 5; matrix products, arithmetic and copies ran while one was open for 5% -> 6% of each run, Pallas kernels for 19% -> 20%
where the time goes in v5:
time: 166 us; the launch traced here: 164 us
  Pallas kernels  50.5 us (30%)
  waiting for transfers between devices  46.7 us (28%)
  starting transfers between devices  22 us (13%)
  blocking collectives  17.7 us (11%)
  between operations  14.2 us (9%)
  other arithmetic  11.8 us (7%)
    pallas_call x9, Pallas kernels, call(): pl.pallas_call(body, out_shape=tuple(outs), in_specs=specs, out_specs=tup...  50.5 us
    ppermute x8, waiting for transfers between devices, shift(): lax.ppermute(x, axis, [(i, (i + amount) % count) for i in range(count)])  26.4 us
    all_to_all x1, blocking collectives, exchange(): return lax.all_to_all(parts, 'seq', 0, 0, tiled=True)  17.7 us
    all_gather x1, waiting for transfers between devices, per_device(): gathered = lax.all_gather(grad_out, 'head')  11.1 us
    ppermute x8, starting transfers between devices, shift(): lax.ppermute(x, axis, [(i, (i + amount) % count) for i in range(count)])  10.9 us
    all_to_all x1, waiting for transfers between devices, exchange(): return lax.all_to_all(parts, 'seq', 0, 0, tiled=True)  8.44 us
    all_to_all x1, starting transfers between devices, per_device(): lax.all_to_all(terms, 'seq', 0, 0, axis_index_groups=groups, tiled=True)  6.61 us
    convert_element_type x2, other arithmetic, out_step(): outs.append((term + got).astype(bf16))  4.14 us
  transfers between devices with their start and end apart: 13, of which 5 were waited for; matrix products, arithmetic and copies ran while one was open for 6% of the time, Pallas kernels for 20%

profile of v5, /device:TPU:1, one launch (start us, length us, event | category | flops | bytes accessed | tf_op | source)
XLA Modules:
  0.0 163.5 jit_solution(11343641887180410730)
XLA Ops:
  7.9 2.3 %state.1 = f32[4,128,128]{2,1,0:T(8,128)} custom-call(bf16[512,512]{1,0:T(8,128)(2,1)} %k.5, bf16[512,512]{1,0:T(8,128)(2,1)} %v.5), custom_call_target="tpu_custom_call" | custom-call | flops 1000000000 | bytes 1000 | tf_op jit(solution)/shard_map/state/pallas_call | solution.py:42
  10.2 17.7 %all_to_all.15.parts = f32[32,16,128]{2,1,0:T(8,128)} all-to-all(f32[32,16,128]{2,1,0:T(8,128)} %bitcast.41), channel_id=1, replica_groups=mesh['seq'=32,'head'=8] {'seq'}, dimensions={0} | all-to-all | bytes 524288 | tf_op jit(solution)/shard_map/all_to_all | solution.py:244
  29.5 3.7 %all-to-all-start.1 = ((f32[32,16,128]{2,1,0:T(8,128)}), f32[32,16,128]{2,1,0:T(8,128)S(1)}, u32[]{:S(2)}, u32[]{:S(2)}) async-start(f32[32,16,128]{2,1,0:T(8,128)} %prefix.1), calls=%async_computation.1 | async-start | bytes 524288 | tf_op jit(solution)/shard_map/all_to_all | solution.py:244
  33.9 8.4 %all-to-all-done.1 = f32[32,16,128]{2,1,0:T(8,128)S(1)} async-done(((f32[32,16,128]{2,1,0:T(8,128)}), f32[32,16,128]{2,1,0:T(8,128)S(1)}, u32[]{:S(2)}, u32[]{:S(2)}) %all-to-all-start.1) | async-done | bytes 262176 | tf_op jit(solution)/shard_map/all_to_all | solution.py:244
  43.0 5.0 %forward.1 = (bf16[512,512]{1,0:T(8,128)(2,1)}, bf16[512,512]{1,0:T(8,128)(2,1)}, f32[512,512]{1,0:T(8,128)}) custom-call(bf16[512,512]{1,0:T(8,128)(2,1)} %q.5, bf16[512,512]{1,0:T(8,128)(2,1)} %k.5, bf16[512,512]{1,0:T(8,128)(2,1)} %v.5, f32[4,128,128]{2,1,0:T(8,128)} %bitcast.39), custom_call_target="tpu_custom_call" | custom-call | flops 1000000000 | bytes 1000 | tf_op jit(solution)/shard_map/forward/pallas_call | solution.py:42
  48.1 9.2 %out_terms.1 = (f32[8,512,512]{2,1,0:T(8,128)}, bf16[256,512]{1,0:T(8,128)(2,1)}, bf16[256,512]{1,0:T(8,128)(2,1)}, bf16[256,512]{1,0:T(8,128)(2,1)}, bf16[256,512]{1,0:T(8,128)(2,1)}) custom-call(s32[3]{0:T(128)} %pad_add_fusion.me, bf16[512,512]{1,0:T(8,128)(2,1)} %get-tuple-element.48.attn, bf16[4096,512]{1,0:T(8,128)(2,1)} %w.3), custom_call_target="tpu_custom_call" | custom-call | flops 1000000000 | bytes 1000 | tf_op jit(solution)/shard_map/out_terms/pallas_call | solution.py:42
  57.3 11.1 %all-gather.5.cloned.1.call-done = bf16[4096,512]{1,0:T(8,128)(2,1)} async-done(((bf16[512,512]{1,0:T(8,128)(2,1)}), bf16[4096,512]{1,0:T(8,128)(2,1)}) %all-gather.5.cloned.1.call-update) | async-done | bytes 4194320 | tf_op jit(solution)/shard_map/all_gather | solution.py:271
  68.4 10.6 %project.1 = (bf16[512,512]{1,0:T(8,128)(2,1)}, f32[4,128,128]{2,1,0:T(8,128)}, bf16[16,512,128]{2,1,0:T(8,128)(2,1)}, bf16[16,512,128]{2,1,0:T(8,128)(2,1)}) custom-call(s32[3]{0:T(128)} %pad_add_fusion.me, bf16[8,512,512]{2,1,0:T(8,128)(2,1)} %bitcast.38, bf16[4096,512]{1,0:T(8,128)(2,1)} %w.3, f32[512,512]{1,0:T(8,128)} %get-tuple-element.59.mixed, ...), custom_call_target="tpu_custom_call" | custom-call | flops 1000000000 | bytes 1000 | tf_op jit(solution)/shard_map/project/pallas_call | solution.py:42
  81.4 2.7 %collective-permute-start.1 = (bf16[256,512]{1,0:T(8,128)(2,1)S(1)}, bf16[256,512]{1,0:T(8,128)(2,1)S(1)}, u32[]{:S(2)}, u32[]{:S(2)}) collective-permute-start(bf16[256,512]{1,0:T(8,128)(2,1)S(1)} %copy-done.2), channel_id=1, source_target_pairs={{0,7},{1,0},{2,1},{3,2},{4,3},{5,4},{6,5},{7,6},{8,15},{9,8},{10,9... | collective-permute-start | bytes 786440 | tf_op jit(solution)/shard_map/ppermute | solution.py:224
  84.1 6.6 %collective-permute-done = bf16[256,512]{1,0:T(8,128)(2,1)S(1)} collective-permute-done((bf16[256,512]{1,0:T(8,128)(2,1)}, bf16[256,512]{1,0:T(8,128)(2,1)S(1)}, u32[]{:S(2)}, u32[]{:S(2)}) %collective-permute-start) | collective-permute-done | bytes 262176 | tf_op jit(solution)/shard_map/ppermute | solution.py:224
  90.7 4.1 %pair_add.1 = bf16[16,512,128]{2,1,0:T(8,128)(2,1)} custom-call(bf16[16,512,128]{2,1,0:T(8,128)(2,1)} %get-tuple-element.61.keep, bf16[16,512,128]{2,1,0:T(8,128)(2,1)} %collective-permute-done.2.received), custom_call_target="tpu_custom_call" | custom-call | flops 1000000000 | bytes 1000 | tf_op jit(solution)/shard_map/pair_add/pallas_call | solution.py:42
  96.2 1.8 %pad_maximum_fusion = (bf16[512,512]{1,0:T(8,128)(2,1)}, bf16[512,512]{1,0:T(8,128)(2,1)S(1)}) fusion(bf16[256,512]{1,0:T(8,128)(2,1)S(1)} %copy-done.1, bf16[256,512]{1,0:T(8,128)(2,1)S(1)} %get-tuple-element.96, bf16[256,512]{1,0:T(8,128)(2,1)S(1)} %get-tuple-element.95, bf16[256,512]{1,0:T(8,128)(2,1)} %get-tuple-element.65), kind=kLoop, calls=%fused_computation.11 | loop fusion | flops 2097152 | bytes 2097152 | tf_op jit(solution)/shard_map/concatenate | solution.py:263
  98.4 2.4 %collective-permute-start.4 = (bf16[512,512]{1,0:T(8,128)(2,1)S(1)}, bf16[512,512]{1,0:T(8,128)(2,1)}, u32[]{:S(2)}, u32[]{:S(2)}) collective-permute-start(bf16[512,512]{1,0:T(8,128)(2,1)S(1)} %get-tuple-element.68), channel_id=1, source_target_pairs={{0,7},{1,0},{2,1},{3,2},{4,3},{5,4},{6,5},{7,6},{8,15},{9,8},{10,9... | collective-permute-start | bytes 1572872 | tf_op jit(solution)/shard_map/ppermute | solution.py:224
  100.7 6.6 %all-to-all-start.2 = ((bf16[16,512,128]{2,1,0:T(8,128)(2,1)}), bf16[16,512,128]{2,1,0:T(8,128)(2,1)}, u32[]{:S(2)}, u32[]{:S(2)}) async-start(bf16[16,512,128]{2,1,0:T(8,128)(2,1)} %pair_add.1), calls=%async_computation.2 | async-start | bytes 4194304 | tf_op jit(solution)/shard_map/all_to_all | solution.py:324
  107.3 8.3 %backward.1 = (bf16[512,512]{1,0:T(8,128)(2,1)}, f32[512,512]{1,0:T(8,128)}, f32[512,512]{1,0:T(8,128)}) custom-call(bf16[512,512]{1,0:T(8,128)(2,1)} %q.5, bf16[512,512]{1,0:T(8,128)(2,1)} %k.5, bf16[512,512]{1,0:T(8,128)(2,1)} %v.5, bf16[512,512]{1,0:T(8,128)(2,1)} %get-tuple-element.72.d_mixed, f32[4,128,128]{2,1,0:T(8,128)} %bitcast.40), custom_call_target="tpu_custom_call" | custom-call | flops 1000000000 | bytes 1000 | tf_op jit(solution)/shard_map/backward/pallas_call | solution.py:42
  115.6 2.2 %fusion.1 = (bf16[512,512]{1,0:T(8,128)(2,1)S(1)}, bf16[512,512]{1,0:T(8,128)(2,1)S(1)}) fusion(bf16[512,512]{1,0:T(8,128)(2,1)} %collective-permute-done.4, f32[8,512,512]{2,1,0:T(8,128)} %get-tuple-element.49, bf16[512,512]{1,0:T(8,128)(2,1)} %collective-permute-done.3), kind=kLoop, calls=%fused_computation.3 | loop fusion | flops 1572864 | bytes 4194304 | tf_op jit(solution)/shard_map/convert_element_type | solution.py:268
  117.9 2.7 %collective-permute-start.6 = (bf16[512,512]{1,0:T(8,128)(2,1)S(1)}, bf16[512,512]{1,0:T(8,128)(2,1)S(1)}, u32[]{:S(2)}, u32[]{:S(2)}) collective-permute-start(bf16[512,512]{1,0:T(8,128)(2,1)S(1)} %get-tuple-element.77), channel_id=1, source_target_pairs={{0,7},{1,0},{2,1},{3,2},{4,3},{5,4},{6,5},{7,6},{8,15},{9,8},{10,9... | collective-permute-start | bytes 1572872 | tf_op jit(solution)/shard_map/ppermute | solution.py:224
  120.6 10.3 %collective-permute-done.5 = bf16[512,512]{1,0:T(8,128)(2,1)S(1)} collective-permute-done((bf16[512,512]{1,0:T(8,128)(2,1)S(1)}, bf16[512,512]{1,0:T(8,128)(2,1)S(1)}, u32[]{:S(2)}, u32[]{:S(2)}) %collective-permute-start.5) | collective-permute-done | bytes 524320 | tf_op jit(solution)/shard_map/ppermute | solution.py:224
  130.9 2.0 %fusion = (bf16[512,512]{1,0:T(8,128)(2,1)S(1)}, bf16[512,512]{1,0:T(8,128)(2,1)S(1)}) fusion(bf16[512,512]{1,0:T(8,128)(2,1)S(1)} %collective-permute-done.6, f32[8,512,512]{2,1,0:T(8,128)} %get-tuple-element.49, bf16[512,512]{1,0:T(8,128)(2,1)S(1)} %collective-permute-done.5), kind=kLoop, calls=%fused_computation.1 | loop fusion | flops 1572864 | bytes 4194304 | tf_op jit(solution)/shard_map/convert_element_type | solution.py:268
  133.0 2.7 %collective-permute-start.8 = (bf16[512,512]{1,0:T(8,128)(2,1)S(1)}, bf16[512,512]{1,0:T(8,128)(2,1)S(1)}, u32[]{:S(2)}, u32[]{:S(2)}) collective-permute-start(bf16[512,512]{1,0:T(8,128)(2,1)S(1)} %get-tuple-element.81), channel_id=1, source_target_pairs={{0,7},{1,0},{2,1},{3,2},{4,3},{5,4},{6,5},{7,6},{8,15},{9,8},{10,9... | collective-permute-start | bytes 1572872 | tf_op jit(solution)/shard_map/ppermute | solution.py:224
  135.6 9.4 %collective-permute-done.7 = bf16[512,512]{1,0:T(8,128)(2,1)S(1)} collective-permute-done((bf16[512,512]{1,0:T(8,128)(2,1)S(1)}, bf16[512,512]{1,0:T(8,128)(2,1)S(1)}, u32[]{:S(2)}, u32[]{:S(2)}) %collective-permute-start.7) | collective-permute-done | bytes 524320 | tf_op jit(solution)/shard_map/ppermute | solution.py:224
  145.0 2.2 %fusion.5 = bf16[512,512]{1,0:T(8,128)(2,1)} fusion(bf16[512,512]{1,0:T(8,128)(2,1)S(1)} %collective-permute-done.8, bf16[512,512]{1,0:T(8,128)(2,1)S(1)} %collective-permute-done.7, f32[8,512,512]{2,1,0:T(8,128)} %get-tuple-element.49), kind=kLoop, calls=%fused_computation.10 | loop fusion | flops 1310720 | bytes 2621440 | tf_op jit(solution)/shard_map/convert_element_type | solution.py:341
  147.3 2.6 %weight_sum.1 = f32[128,512]{1,0:T(8,128)} custom-call(bf16[16,512,128]{2,1,0:T(8,128)(2,1)} %all-to-all-done.2.parts), custom_call_target="tpu_custom_call" | custom-call | flops 1000000000 | bytes 1000 | tf_op jit(solution)/shard_map/weight_sum/pallas_call | solution.py:42
  149.9 6.7 %finish.1 = (bf16[512,512]{1,0:T(8,128)(2,1)}, bf16[512,512]{1,0:T(8,128)(2,1)}) custom-call(s32[3]{0:T(128)} %pad_add_fusion.me, bf16[512,512]{1,0:T(8,128)(2,1)} %k.5, bf16[512,512]{1,0:T(8,128)(2,1)} %v.5, f32[512,512]{1,0:T(8,128)} %get-tuple-element.84.part_k, f32[512,512]{1,0:T(8,128)} %get-tuple-element.85.part_v, bf16[32,4,128,128]{3,2,1,0:T(8,128)(2,1)} %bitcast.37), custom_call_target="tpu_custom_call" | custom-call | flops 1000000000 | bytes 1000 | tf_op jit(solution)/shard_map/finish/pallas_call | solution.py:42
  (27 shorter events, 8.0 us)
Async XLA Ops:
  7.2 61.3 %all-gather.5.cloned.1.call-start = ((), (), s32[]{:S(2)}) async-start(), calls=%async_computation.3 | async-start | bytes 4718592 | tf_op jit(solution)/shard_map/all_gather | solution.py:271
  29.5 12.8 %all-to-all-start.1 = ((f32[32,16,128]{2,1,0:T(8,128)}), f32[32,16,128]{2,1,0:T(8,128)S(1)}, u32[]{:S(2)}, u32[]{:S(2)}) async-start(f32[32,16,128]{2,1,0:T(8,128)} %prefix.1), calls=%async_computation.1 | async-start | bytes 524288 | tf_op jit(solution)/shard_map/all_to_all | solution.py:244
  33.2 116.7 %all-gather.7.cloned.1.call-start = ((), (), s32[]{:S(2)}) async-start(), calls=%async_computation.4 | async-start | bytes 4325376 | tf_op jit(solution)/shard_map/all_gather | solution.py:310
  42.3 0.7 copy-start
  68.4 13.0 %copy-start.2 = (bf16[256,512]{1,0:T(8,128)(2,1)S(1)}, bf16[256,512]{1,0:T(8,128)(2,1)}, u32[]{:S(2)}) copy-start(bf16[256,512]{1,0:T(8,128)(2,1)} %get-tuple-element.55) | copy-start | bytes 786436
  80.7 10.1 %collective-permute-start.2 = (bf16[16,512,128]{2,1,0:T(8,128)(2,1)}, bf16[16,512,128]{2,1,0:T(8,128)(2,1)}, u32[]{:S(2)}, u32[]{:S(2)}) collective-permute-start(bf16[16,512,128]{2,1,0:T(8,128)(2,1)} %get-tuple-element.62), channel_id=1, source_target_pairs={{0,8},{8,0},{16,24},{24,16},{32,40},{40,32},{48,56},{56,48},{64,72... | collective-permute-start | bytes 6291464 | tf_op jit(solution)/shard_map/ppermute | solution.py:311
  81.4 9.3 %collective-permute-start = (bf16[256,512]{1,0:T(8,128)(2,1)}, bf16[256,512]{1,0:T(8,128)(2,1)S(1)}, u32[]{:S(2)}, u32[]{:S(2)}) collective-permute-start(bf16[256,512]{1,0:T(8,128)(2,1)} %get-tuple-element.54), channel_id=1, source_target_pairs={{0,1},{1,2},{2,3},{3,4},{4,5},{5,6},{6,7},{7,0},{8,9},{9,10},{10,1... | collective-permute-start | bytes 786440 | tf_op jit(solution)/shard_map/ppermute | solution.py:224
  81.4 9.3 %collective-permute-start.1 = (bf16[256,512]{1,0:T(8,128)(2,1)S(1)}, bf16[256,512]{1,0:T(8,128)(2,1)S(1)}, u32[]{:S(2)}, u32[]{:S(2)}) collective-permute-start(bf16[256,512]{1,0:T(8,128)(2,1)S(1)} %copy-done.2), channel_id=1, source_target_pairs={{0,7},{1,0},{2,1},{3,2},{4,3},{5,4},{6,5},{7,6},{8,15},{9,8},{10,9... | collective-permute-start | bytes 786440 | tf_op jit(solution)/shard_map/ppermute | solution.py:224
  90.7 5.5 %copy-start.1 = (bf16[256,512]{1,0:T(8,128)(2,1)S(1)}, bf16[256,512]{1,0:T(8,128)(2,1)}, u32[]{:S(2)}) copy-start(bf16[256,512]{1,0:T(8,128)(2,1)} %get-tuple-element.64) | copy-start | bytes 786436
  98.1 17.6 %collective-permute-start.3 = (bf16[512,512]{1,0:T(8,128)(2,1)}, bf16[512,512]{1,0:T(8,128)(2,1)}, u32[]{:S(2)}, u32[]{:S(2)}) collective-permute-start(bf16[512,512]{1,0:T(8,128)(2,1)} %get-tuple-element.67), channel_id=1, source_target_pairs={{0,1},{1,2},{2,3},{3,4},{4,5},{5,6},{6,7},{7,0},{8,9},{9,10},{10,1... | collective-permute-start | bytes 1572872 | tf_op jit(solution)/shard_map/ppermute | solution.py:224
  98.4 17.3 %collective-permute-start.4 = (bf16[512,512]{1,0:T(8,128)(2,1)S(1)}, bf16[512,512]{1,0:T(8,128)(2,1)}, u32[]{:S(2)}, u32[]{:S(2)}) collective-permute-start(bf16[512,512]{1,0:T(8,128)(2,1)S(1)} %get-tuple-element.68), channel_id=1, source_target_pairs={{0,7},{1,0},{2,1},{3,2},{4,3},{5,4},{6,5},{7,6},{8,15},{9,8},{10,9... | collective-permute-start | bytes 1572872 | tf_op jit(solution)/shard_map/ppermute | solution.py:224
  100.7 46.5 %all-to-all-start.2 = ((bf16[16,512,128]{2,1,0:T(8,128)(2,1)}), bf16[16,512,128]{2,1,0:T(8,128)(2,1)}, u32[]{:S(2)}, u32[]{:S(2)}) async-start(bf16[16,512,128]{2,1,0:T(8,128)(2,1)} %pair_add.1), calls=%async_computation.2 | async-start | bytes 4194304 | tf_op jit(solution)/shard_map/all_to_all | solution.py:324
  117.8 13.1 %collective-permute-start.5 = (bf16[512,512]{1,0:T(8,128)(2,1)S(1)}, bf16[512,512]{1,0:T(8,128)(2,1)S(1)}, u32[]{:S(2)}, u32[]{:S(2)}) collective-permute-start(bf16[512,512]{1,0:T(8,128)(2,1)S(1)} %get-tuple-element.76), channel_id=1, source_target_pairs={{0,1},{1,2},{2,3},{3,4},{4,5},{5,6},{6,7},{7,0},{8,9},{9,10},{10,1... | collective-permute-start | bytes 1572872 | tf_op jit(solution)/shard_map/ppermute | solution.py:224
  117.9 13.0 %collective-permute-start.6 = (bf16[512,512]{1,0:T(8,128)(2,1)S(1)}, bf16[512,512]{1,0:T(8,128)(2,1)S(1)}, u32[]{:S(2)}, u32[]{:S(2)}) collective-permute-start(bf16[512,512]{1,0:T(8,128)(2,1)S(1)} %get-tuple-element.77), channel_id=1, source_target_pairs={{0,7},{1,0},{2,1},{3,2},{4,3},{5,4},{6,5},{7,6},{8,15},{9,8},{10,9... | collective-permute-start | bytes 1572872 | tf_op jit(solution)/shard_map/ppermute | solution.py:224
  132.9 12.2 %collective-permute-start.7 = (bf16[512,512]{1,0:T(8,128)(2,1)S(1)}, bf16[512,512]{1,0:T(8,128)(2,1)S(1)}, u32[]{:S(2)}, u32[]{:S(2)}) collective-permute-start(bf16[512,512]{1,0:T(8,128)(2,1)S(1)} %get-tuple-element.80), channel_id=1, source_target_pairs={{0,1},{1,2},{2,3},{3,4},{4,5},{5,6},{6,7},{7,0},{8,9},{9,10},{10,1... | collective-permute-start | bytes 1572872 | tf_op jit(solution)/shard_map/ppermute | solution.py:224
  133.0 12.1 %collective-permute-start.8 = (bf16[512,512]{1,0:T(8,128)(2,1)S(1)}, bf16[512,512]{1,0:T(8,128)(2,1)S(1)}, u32[]{:S(2)}, u32[]{:S(2)}) collective-permute-start(bf16[512,512]{1,0:T(8,128)(2,1)S(1)} %get-tuple-element.81), channel_id=1, source_target_pairs={{0,7},{1,0},{2,1},{3,2},{4,3},{5,4},{6,5},{7,6},{8,15},{9,8},{10,9... | collective-permute-start | bytes 1572872 | tf_op jit(solution)/shard_map/ppermute | solution.py:224
Sparse Core Ops, SparseCore 0:
  9.8 58.6 all-gather.4
  80.8 64.4 all-gather.6

commit v6 on v5

--- a/solution.py
+++ b/solution.py
@@ -136,7 +136,7 @@
         d_m = inverse * (d_attn - normed * jnp.mean(d_attn * normed, axis=-1, keepdims=True))
         d_m = d_m.astype(bf16)
         d_mixed[:, head(h)] = d_m
-        grads[h] = dot(q[:, head(h)], d_m, 0, 0)
+        grads[h] = dot(q[:, head(h)], d_m, 0, 0).astype(bf16)
     for copy in results:
         copy.wait()
 
@@ -292,7 +292,7 @@
     dims = (count // 2, features, w_out.shape[0] // count)
     d_mixed, local_grads, keep, send = call(
         project_body,
-        [block, states, shape(dims, bf16), shape(dims, bf16)],
+        [block, shape(states.shape, bf16), shape(dims, bf16), shape(dims, bf16)],
         [me, gathered, w_out, mixed, queries, attn_t],
         "project",
         far=(1, 2),
@@ -307,24 +307,25 @@
             pltpu.SemaphoreType.DMA((2, ring)),
         ],
     )
-    state_all = lax.all_gather(local_grads.astype(bf16), "seq")
+    state_all = lax.all_gather(local_grads, "seq")
     received = lax.ppermute(send, "seq", [(i, i ^ 1) for i in range(count)])
     (terms,) = call(pair_body, [shape(dims, bf16)], [keep, received], "pair_add")
     pair = tie((*pair, terms))[:2]
     pair = out_step(pair, ring // 2 - 1)
-    after_one = tie((d_mixed, *pair))[0]
+    pair = hop(pair)
+    groups = [[2 * chip + core for chip in range(count // 2)] for core in range(2)]
+    terms = lax.all_to_all(terms, "seq", 0, 0, axis_index_groups=groups, tiled=True)
+    pair = out_step(pair, ring // 2 - 2)
+    after_two = tie((d_mixed, *pair))[0]
     pair = hop(pair)
     grad_q, part_k, part_v = call(
         backward_body,
         [block, wide_block, wide_block],
-        [queries, keys, values, after_one, prefix],
+        [queries, keys, values, after_two, prefix],
         "backward",
     )
-    groups = [[2 * chip + core for chip in range(count // 2)] for core in range(2)]
-    terms = lax.all_to_all(terms, "seq", 0, 0, axis_index_groups=groups, tiled=True)
     pair = tie((*pair, grad_q))[:2]
-    pair = out_step(pair, ring // 2 - 2)
-    pair = out_step(hop(pair), ring // 2 - 3)
+    pair = out_step(pair, ring // 2 - 3)
     terms = tie((terms, *pair))[0]
     state_all = tie((state_all, *pair))[0]
     pair = hop(pair)

time: 166 us -> 160 us (0.964)
  waiting for transfers between devices: 46.7 us -> 42.8 us
  other arithmetic: 11.8 us -> 9.24 us
    ppermute x8, waiting for transfers between devices: 26.4 us -> 22.5 us  [shift(): lax.ppermute(x, axis, [(i, (i + amount) % count) for i in range(count)])]
    concatenate x1, other arithmetic: 1.83 us -> 0.07 us  [out_step(): outs.append(jnp.concatenate(parts, axis=0))]
  transfers between devices with their start and end apart: 13 -> 13, of which waited for: 5 -> 6; matrix products, arithmetic and copies ran while one was open for 6% -> 6% of each run, Pallas kernels for 20% -> 21%
where the time goes in v6:
time: 160 us; the launch traced here: 158 us
  Pallas kernels  50.5 us (32%)
  waiting for transfers between devices  42.8 us (27%)
  starting transfers between devices  22 us (14%)
  blocking collectives  17.7 us (11%)
  between operations  14.2 us (9%)
  other arithmetic  9.24 us (6%)
    pallas_call x9, Pallas kernels, call(): pl.pallas_call(body, out_shape=tuple(outs), in_specs=specs, out_specs=tup...  50.5 us
    ppermute x8, waiting for transfers between devices, shift(): lax.ppermute(x, axis, [(i, (i + amount) % count) for i in range(count)])  22.5 us
    all_to_all x1, blocking collectives, exchange(): return lax.all_to_all(parts, 'seq', 0, 0, tiled=True)  17.7 us
    all_gather x1, waiting for transfers between devices, per_device(): gathered = lax.all_gather(grad_out, 'head')  11.2 us
    ppermute x8, starting transfers between devices, shift(): lax.ppermute(x, axis, [(i, (i + amount) % count) for i in range(count)])  10.9 us
    all_to_all x1, waiting for transfers between devices, exchange(): return lax.all_to_all(parts, 'seq', 0, 0, tiled=True)  8.44 us
    all_to_all x1, starting transfers between devices, per_device(): lax.all_to_all(terms, 'seq', 0, 0, axis_index_groups=groups, tiled=True)  6.57 us
    convert_element_type x2, other arithmetic, out_step(): outs.append((term + got).astype(bf16))  4.9 us
  transfers between devices with their start and end apart: 13, of which 6 were waited for; matrix products, arithmetic and copies ran while one was open for 6% of the time, Pallas kernels for 21%

profile of v6, /device:TPU:1, one launch (start us, length us, event | category | flops | bytes accessed | tf_op | source)
XLA Modules:
  0.0 157.8 jit_solution(3227131569301638900)
XLA Ops:
  7.9 2.3 %state.1 = f32[4,128,128]{2,1,0:T(8,128)} custom-call(bf16[512,512]{1,0:T(8,128)(2,1)} %k.5, bf16[512,512]{1,0:T(8,128)(2,1)} %v.5), custom_call_target="tpu_custom_call" | custom-call | flops 1000000000 | bytes 1000 | tf_op jit(solution)/shard_map/state/pallas_call | solution.py:42
  10.2 17.7 %all_to_all.15.parts = f32[32,16,128]{2,1,0:T(8,128)} all-to-all(f32[32,16,128]{2,1,0:T(8,128)} %bitcast.41), channel_id=1, replica_groups=mesh['seq'=32,'head'=8] {'seq'}, dimensions={0} | all-to-all | bytes 524288 | tf_op jit(solution)/shard_map/all_to_all | solution.py:244
  29.5 3.7 %all-to-all-start.1 = ((f32[32,16,128]{2,1,0:T(8,128)}), f32[32,16,128]{2,1,0:T(8,128)S(1)}, u32[]{:S(2)}, u32[]{:S(2)}) async-start(f32[32,16,128]{2,1,0:T(8,128)} %prefix.1), calls=%async_computation.1 | async-start | bytes 524288 | tf_op jit(solution)/shard_map/all_to_all | solution.py:244
  33.9 8.4 %all-to-all-done.1 = f32[32,16,128]{2,1,0:T(8,128)S(1)} async-done(((f32[32,16,128]{2,1,0:T(8,128)}), f32[32,16,128]{2,1,0:T(8,128)S(1)}, u32[]{:S(2)}, u32[]{:S(2)}) %all-to-all-start.1) | async-done | bytes 262176 | tf_op jit(solution)/shard_map/all_to_all | solution.py:244
  43.0 5.0 %forward.1 = (bf16[512,512]{1,0:T(8,128)(2,1)}, bf16[512,512]{1,0:T(8,128)(2,1)}, f32[512,512]{1,0:T(8,128)}) custom-call(bf16[512,512]{1,0:T(8,128)(2,1)} %q.5, bf16[512,512]{1,0:T(8,128)(2,1)} %k.5, bf16[512,512]{1,0:T(8,128)(2,1)} %v.5, f32[4,128,128]{2,1,0:T(8,128)} %bitcast.39), custom_call_target="tpu_custom_call" | custom-call | flops 1000000000 | bytes 1000 | tf_op jit(solution)/shard_map/forward/pallas_call | solution.py:42
  48.0 9.2 %out_terms.1 = (f32[8,512,512]{2,1,0:T(8,128)}, bf16[256,512]{1,0:T(8,128)(2,1)}, bf16[256,512]{1,0:T(8,128)(2,1)}, bf16[256,512]{1,0:T(8,128)(2,1)}, bf16[256,512]{1,0:T(8,128)(2,1)}) custom-call(s32[3]{0:T(128)} %pad_add_fusion.me, bf16[512,512]{1,0:T(8,128)(2,1)} %get-tuple-element.48.attn, bf16[4096,512]{1,0:T(8,128)(2,1)} %w.3), custom_call_target="tpu_custom_call" | custom-call | flops 1000000000 | bytes 1000 | tf_op jit(solution)/shard_map/out_terms/pallas_call | solution.py:42
  57.3 11.2 %all-gather.5.cloned.1.call-done = bf16[4096,512]{1,0:T(8,128)(2,1)} async-done(((bf16[512,512]{1,0:T(8,128)(2,1)}), bf16[4096,512]{1,0:T(8,128)(2,1)}) %all-gather.5.cloned.1.call-update) | async-done | bytes 4194320 | tf_op jit(solution)/shard_map/all_gather | solution.py:271
  68.4 10.5 %project.1 = (bf16[512,512]{1,0:T(8,128)(2,1)}, bf16[4,128,128]{2,1,0:T(8,128)(2,1)}, bf16[16,512,128]{2,1,0:T(8,128)(2,1)}, bf16[16,512,128]{2,1,0:T(8,128)(2,1)}) custom-call(s32[3]{0:T(128)} %pad_add_fusion.me, bf16[8,512,512]{2,1,0:T(8,128)(2,1)} %bitcast.38, bf16[4096,512]{1,0:T(8,128)(2,1)} %w.3, f32[512,512]{1,0:T(8,128)} %get-tuple-element.59.mixed, ...), custom_call_target="tpu_custom_call" | custom-call | flops 1000000000 | bytes 1000 | tf_op jit(solution)/shard_map/project/pallas_call | solution.py:42
  79.8 2.7 %collective-permute-start.1 = (bf16[256,512]{1,0:T(8,128)(2,1)S(1)}, bf16[256,512]{1,0:T(8,128)(2,1)S(1)}, u32[]{:S(2)}, u32[]{:S(2)}) collective-permute-start(bf16[256,512]{1,0:T(8,128)(2,1)S(1)} %copy-done.4), channel_id=1, source_target_pairs={{0,7},{1,0},{2,1},{3,2},{4,3},{5,4},{6,5},{7,6},{8,15},{9,8},{10,9... | collective-permute-start | bytes 786440 | tf_op jit(solution)/shard_map/ppermute | solution.py:224
  82.5 6.4 %collective-permute-done = bf16[256,512]{1,0:T(8,128)(2,1)S(1)} collective-permute-done((bf16[256,512]{1,0:T(8,128)(2,1)S(1)}, bf16[256,512]{1,0:T(8,128)(2,1)S(1)}, u32[]{:S(2)}, u32[]{:S(2)}) %collective-permute-start) | collective-permute-done | bytes 262176 | tf_op jit(solution)/shard_map/ppermute | solution.py:224
  89.5 4.2 %pair_add.1 = bf16[16,512,128]{2,1,0:T(8,128)(2,1)} custom-call(bf16[16,512,128]{2,1,0:T(8,128)(2,1)} %get-tuple-element.61.keep, bf16[16,512,128]{2,1,0:T(8,128)(2,1)} %collective-permute-done.2.received), custom_call_target="tpu_custom_call" | custom-call | flops 1000000000 | bytes 1000 | tf_op jit(solution)/shard_map/pair_add/pallas_call | solution.py:42
  95.9 2.1 %collective-permute-start.4 = (bf16[512,512]{1,0:T(8,128)(2,1)S(1)}, bf16[512,512]{1,0:T(8,128)(2,1)S(1)}, u32[]{:S(2)}, u32[]{:S(2)}) collective-permute-start(bf16[512,512]{1,0:T(8,128)(2,1)S(1)} %get-tuple-element.68), channel_id=1, source_target_pairs={{0,7},{1,0},{2,1},{3,2},{4,3},{5,4},{6,5},{7,6},{8,15},{9,8},{10,9... | collective-permute-start | bytes 1572872 | tf_op jit(solution)/shard_map/ppermute | solution.py:224
  98.0 6.6 %all-to-all-start.2 = ((bf16[16,512,128]{2,1,0:T(8,128)(2,1)}), bf16[16,512,128]{2,1,0:T(8,128)(2,1)}, u32[]{:S(2)}, u32[]{:S(2)}) async-start(bf16[16,512,128]{2,1,0:T(8,128)(2,1)} %pair_add.1), calls=%async_computation.2 | async-start | bytes 4194304 | tf_op jit(solution)/shard_map/all_to_all | solution.py:317
  104.6 4.5 %collective-permute-done.3 = bf16[512,512]{1,0:T(8,128)(2,1)S(1)} collective-permute-done((bf16[512,512]{1,0:T(8,128)(2,1)S(1)}, bf16[512,512]{1,0:T(8,128)(2,1)S(1)}, u32[]{:S(2)}, u32[]{:S(2)}) %collective-permute-start.3) | collective-permute-done | bytes 524320 | tf_op jit(solution)/shard_map/ppermute | solution.py:224
  109.1 2.7 %fusion.1 = (bf16[512,512]{1,0:T(8,128)(2,1)S(1)}, bf16[512,512]{1,0:T(8,128)(2,1)}) fusion(bf16[512,512]{1,0:T(8,128)(2,1)S(1)} %collective-permute-done.4, f32[8,512,512]{2,1,0:T(8,128)} %get-tuple-element.49, bf16[512,512]{1,0:T(8,128)(2,1)S(1)} %collective-permute-done.3), kind=kLoop, calls=%fused_computation.3 | loop fusion | flops 1572864 | bytes 4194304 | tf_op jit(solution)/shard_map/convert_element_type | solution.py:268
  112.0 2.5 %collective-permute-start.6 = (bf16[512,512]{1,0:T(8,128)(2,1)S(1)}, bf16[512,512]{1,0:T(8,128)(2,1)}, u32[]{:S(2)}, u32[]{:S(2)}) collective-permute-start(bf16[512,512]{1,0:T(8,128)(2,1)S(1)} %get-tuple-element.72), channel_id=1, source_target_pairs={{0,7},{1,0},{2,1},{3,2},{4,3},{5,4},{6,5},{7,6},{8,15},{9,8},{10,9... | collective-permute-start | bytes 1572872 | tf_op jit(solution)/shard_map/ppermute | solution.py:224
  114.5 8.3 %backward.1 = (bf16[512,512]{1,0:T(8,128)(2,1)}, f32[512,512]{1,0:T(8,128)}, f32[512,512]{1,0:T(8,128)}) custom-call(bf16[512,512]{1,0:T(8,128)(2,1)} %q.5, bf16[512,512]{1,0:T(8,128)(2,1)} %k.5, bf16[512,512]{1,0:T(8,128)(2,1)} %v.5, bf16[512,512]{1,0:T(8,128)(2,1)} %get-tuple-element.76.d_mixed, f32[4,128,128]{2,1,0:T(8,128)} %bitcast.40), custom_call_target="tpu_custom_call" | custom-call | flops 1000000000 | bytes 1000 | tf_op jit(solution)/shard_map/backward/pallas_call | solution.py:42
  122.7 2.2 %collective-permute-done.5 = bf16[512,512]{1,0:T(8,128)(2,1)} collective-permute-done((bf16[512,512]{1,0:T(8,128)(2,1)}, bf16[512,512]{1,0:T(8,128)(2,1)}, u32[]{:S(2)}, u32[]{:S(2)}) %collective-permute-start.5) | collective-permute-done | bytes 524320 | tf_op jit(solution)/shard_map/ppermute | solution.py:224
  125.0 2.2 %fusion = (bf16[512,512]{1,0:T(8,128)(2,1)S(1)}, bf16[512,512]{1,0:T(8,128)(2,1)S(1)}) fusion(bf16[512,512]{1,0:T(8,128)(2,1)} %collective-permute-done.6, f32[8,512,512]{2,1,0:T(8,128)} %get-tuple-element.49, bf16[512,512]{1,0:T(8,128)(2,1)} %collective-permute-done.5), kind=kLoop, calls=%fused_computation.1 | loop fusion | flops 1572864 | bytes 4194304 | tf_op jit(solution)/shard_map/convert_element_type | solution.py:268
  127.3 2.7 %collective-permute-start.8 = (bf16[512,512]{1,0:T(8,128)(2,1)S(1)}, bf16[512,512]{1,0:T(8,128)(2,1)S(1)}, u32[]{:S(2)}, u32[]{:S(2)}) collective-permute-start(bf16[512,512]{1,0:T(8,128)(2,1)S(1)} %get-tuple-element.81), channel_id=1, source_target_pairs={{0,7},{1,0},{2,1},{3,2},{4,3},{5,4},{6,5},{7,6},{8,15},{9,8},{10,9... | collective-permute-start | bytes 1572872 | tf_op jit(solution)/shard_map/ppermute | solution.py:224
  129.9 9.4 %collective-permute-done.7 = bf16[512,512]{1,0:T(8,128)(2,1)S(1)} collective-permute-done((bf16[512,512]{1,0:T(8,128)(2,1)S(1)}, bf16[512,512]{1,0:T(8,128)(2,1)S(1)}, u32[]{:S(2)}, u32[]{:S(2)}) %collective-permute-start.7) | collective-permute-done | bytes 524320 | tf_op jit(solution)/shard_map/ppermute | solution.py:224
  139.3 2.2 %fusion.5 = bf16[512,512]{1,0:T(8,128)(2,1)} fusion(bf16[512,512]{1,0:T(8,128)(2,1)S(1)} %collective-permute-done.8, bf16[512,512]{1,0:T(8,128)(2,1)S(1)} %collective-permute-done.7, f32[8,512,512]{2,1,0:T(8,128)} %get-tuple-element.49), kind=kLoop, calls=%fused_computation.10 | loop fusion | flops 1310720 | bytes 2621440 | tf_op jit(solution)/shard_map/convert_element_type | solution.py:342
  141.6 2.6 %weight_sum.1 = f32[128,512]{1,0:T(8,128)} custom-call(bf16[16,512,128]{2,1,0:T(8,128)(2,1)} %all-to-all-done.2.parts), custom_call_target="tpu_custom_call" | custom-call | flops 1000000000 | bytes 1000 | tf_op jit(solution)/shard_map/weight_sum/pallas_call | solution.py:42
  144.2 6.7 %finish.1 = (bf16[512,512]{1,0:T(8,128)(2,1)}, bf16[512,512]{1,0:T(8,128)(2,1)}) custom-call(s32[3]{0:T(128)} %pad_add_fusion.me, bf16[512,512]{1,0:T(8,128)(2,1)} %k.5, bf16[512,512]{1,0:T(8,128)(2,1)} %v.5, f32[512,512]{1,0:T(8,128)} %get-tuple-element.84.part_k, f32[512,512]{1,0:T(8,128)} %get-tuple-element.85.part_v, bf16[32,4,128,128]{3,2,1,0:T(8,128)(2,1)} %bitcast.37), custom_call_target="tpu_custom_call" | custom-call | flops 1000000000 | bytes 1000 | tf_op jit(solution)/shard_map/finish/pallas_call | solution.py:42
  (32 shorter events, 7.7 us)
Async XLA Ops:
  7.2 61.3 %all-gather.5.cloned.1.call-start = ((), (), s32[]{:S(2)}) async-start(), calls=%async_computation.3 | async-start | bytes 4718592 | tf_op jit(solution)/shard_map/all_gather | solution.py:271
  29.5 12.8 %all-to-all-start.1 = ((f32[32,16,128]{2,1,0:T(8,128)}), f32[32,16,128]{2,1,0:T(8,128)S(1)}, u32[]{:S(2)}, u32[]{:S(2)}) async-start(f32[32,16,128]{2,1,0:T(8,128)} %prefix.1), calls=%async_computation.1 | async-start | bytes 524288 | tf_op jit(solution)/shard_map/all_to_all | solution.py:244
  33.2 111.0 %all-gather.7.cloned.1.call-start = ((), (), s32[]{:S(2)}) async-start(), calls=%async_computation.4 | async-start | bytes 4325376 | tf_op jit(solution)/shard_map/all_gather | solution.py:310
  42.3 0.7 copy-start
  68.4 11.3 %copy-start.5 = (bf16[256,512]{1,0:T(8,128)(2,1)S(1)}, bf16[256,512]{1,0:T(8,128)(2,1)}, u32[]{:S(2)}) copy-start(bf16[256,512]{1,0:T(8,128)(2,1)} %get-tuple-element.54) | copy-start | bytes 786436
  68.4 11.3 %copy-start.4 = (bf16[256,512]{1,0:T(8,128)(2,1)S(1)}, bf16[256,512]{1,0:T(8,128)(2,1)}, u32[]{:S(2)}) copy-start(bf16[256,512]{1,0:T(8,128)(2,1)} %get-tuple-element.55) | copy-start | bytes 786436
  79.0 9.9 %collective-permute-start.2 = (bf16[16,512,128]{2,1,0:T(8,128)(2,1)}, bf16[16,512,128]{2,1,0:T(8,128)(2,1)}, u32[]{:S(2)}, u32[]{:S(2)}) collective-permute-start(bf16[16,512,128]{2,1,0:T(8,128)(2,1)} %get-tuple-element.62), channel_id=1, source_target_pairs={{0,8},{8,0},{16,24},{24,16},{32,40},{40,32},{48,56},{56,48},{64,72... | collective-permute-start | bytes 6291464 | tf_op jit(solution)/shard_map/ppermute | solution.py:311
  79.8 9.1 %collective-permute-start = (bf16[256,512]{1,0:T(8,128)(2,1)S(1)}, bf16[256,512]{1,0:T(8,128)(2,1)S(1)}, u32[]{:S(2)}, u32[]{:S(2)}) collective-permute-start(bf16[256,512]{1,0:T(8,128)(2,1)S(1)} %copy-done.5), channel_id=1, source_target_pairs={{0,1},{1,2},{2,3},{3,4},{4,5},{5,6},{6,7},{7,0},{8,9},{9,10},{10,1... | collective-permute-start | bytes 786440 | tf_op jit(solution)/shard_map/ppermute | solution.py:224
  79.8 9.1 %collective-permute-start.1 = (bf16[256,512]{1,0:T(8,128)(2,1)S(1)}, bf16[256,512]{1,0:T(8,128)(2,1)S(1)}, u32[]{:S(2)}, u32[]{:S(2)}) collective-permute-start(bf16[256,512]{1,0:T(8,128)(2,1)S(1)} %copy-done.4), channel_id=1, source_target_pairs={{0,7},{1,0},{2,1},{3,2},{4,3},{5,4},{6,5},{7,6},{8,15},{9,8},{10,9... | collective-permute-start | bytes 786440 | tf_op jit(solution)/shard_map/ppermute | solution.py:224
  88.8 0.7 copy-start.3
  89.5 5.6 %copy-start.1 = (bf16[256,512]{1,0:T(8,128)(2,1)S(1)}, bf16[256,512]{1,0:T(8,128)(2,1)}, u32[]{:S(2)}) copy-start(bf16[256,512]{1,0:T(8,128)(2,1)} %get-tuple-element.64) | copy-start | bytes 786436
  89.5 5.6 %copy-start.2 = (bf16[256,512]{1,0:T(8,128)(2,1)S(1)}, bf16[256,512]{1,0:T(8,128)(2,1)}, u32[]{:S(2)}) copy-start(bf16[256,512]{1,0:T(8,128)(2,1)} %get-tuple-element.65) | copy-start | bytes 786436
  95.3 13.9 %collective-permute-start.3 = (bf16[512,512]{1,0:T(8,128)(2,1)S(1)}, bf16[512,512]{1,0:T(8,128)(2,1)S(1)}, u32[]{:S(2)}, u32[]{:S(2)}) collective-permute-start(bf16[512,512]{1,0:T(8,128)(2,1)S(1)} %get-tuple-element.67), channel_id=1, source_target_pairs={{0,1},{1,2},{2,3},{3,4},{4,5},{5,6},{6,7},{7,0},{8,9},{9,10},{10,1... | collective-permute-start | bytes 1572872 | tf_op jit(solution)/shard_map/ppermute | solution.py:224
  95.9 13.2 %collective-permute-start.4 = (bf16[512,512]{1,0:T(8,128)(2,1)S(1)}, bf16[512,512]{1,0:T(8,128)(2,1)S(1)}, u32[]{:S(2)}, u32[]{:S(2)}) collective-permute-start(bf16[512,512]{1,0:T(8,128)(2,1)S(1)} %get-tuple-element.68), channel_id=1, source_target_pairs={{0,7},{1,0},{2,1},{3,2},{4,3},{5,4},{6,5},{7,6},{8,15},{9,8},{10,9... | collective-permute-start | bytes 1572872 | tf_op jit(solution)/shard_map/ppermute | solution.py:224
  98.0 43.6 %all-to-all-start.2 = ((bf16[16,512,128]{2,1,0:T(8,128)(2,1)}), bf16[16,512,128]{2,1,0:T(8,128)(2,1)}, u32[]{:S(2)}, u32[]{:S(2)}) async-start(bf16[16,512,128]{2,1,0:T(8,128)(2,1)} %pair_add.1), calls=%async_computation.2 | async-start | bytes 4194304 | tf_op jit(solution)/shard_map/all_to_all | solution.py:317
  111.8 13.2 %collective-permute-start.5 = (bf16[512,512]{1,0:T(8,128)(2,1)}, bf16[512,512]{1,0:T(8,128)(2,1)}, u32[]{:S(2)}, u32[]{:S(2)}) collective-permute-start(bf16[512,512]{1,0:T(8,128)(2,1)} %get-tuple-element.71), channel_id=1, source_target_pairs={{0,1},{1,2},{2,3},{3,4},{4,5},{5,6},{6,7},{7,0},{8,9},{9,10},{10,1... | collective-permute-start | bytes 1572872 | tf_op jit(solution)/shard_map/ppermute | solution.py:224
  112.0 13.0 %collective-permute-start.6 = (bf16[512,512]{1,0:T(8,128)(2,1)S(1)}, bf16[512,512]{1,0:T(8,128)(2,1)}, u32[]{:S(2)}, u32[]{:S(2)}) collective-permute-start(bf16[512,512]{1,0:T(8,128)(2,1)S(1)} %get-tuple-element.72), channel_id=1, source_target_pairs={{0,7},{1,0},{2,1},{3,2},{4,3},{5,4},{6,5},{7,6},{8,15},{9,8},{10,9... | collective-permute-start | bytes 1572872 | tf_op jit(solution)/shard_map/ppermute | solution.py:224
  127.2 12.1 %collective-permute-start.7 = (bf16[512,512]{1,0:T(8,128)(2,1)S(1)}, bf16[512,512]{1,0:T(8,128)(2,1)S(1)}, u32[]{:S(2)}, u32[]{:S(2)}) collective-permute-start(bf16[512,512]{1,0:T(8,128)(2,1)S(1)} %get-tuple-element.80), channel_id=1, source_target_pairs={{0,1},{1,2},{2,3},{3,4},{4,5},{5,6},{6,7},{7,0},{8,9},{9,10},{10,1... | collective-permute-start | bytes 1572872 | tf_op jit(solution)/shard_map/ppermute | solution.py:224
  127.3 12.0 %collective-permute-start.8 = (bf16[512,512]{1,0:T(8,128)(2,1)S(1)}, bf16[512,512]{1,0:T(8,128)(2,1)S(1)}, u32[]{:S(2)}, u32[]{:S(2)}) collective-permute-start(bf16[512,512]{1,0:T(8,128)(2,1)S(1)} %get-tuple-element.81), channel_id=1, source_target_pairs={{0,7},{1,0},{2,1},{3,2},{4,3},{5,4},{6,5},{7,6},{8,15},{9,8},{10,9... | collective-permute-start | bytes 1572872 | tf_op jit(solution)/shard_map/ppermute | solution.py:224
Sparse Core Ops, SparseCore 0:
  9.8 58.6 all-gather.4
  79.1 63.4 all-gather.6

commit v7 on v6

--- a/solution.py
+++ b/solution.py
@@ -309,9 +309,9 @@
     )
     state_all = lax.all_gather(local_grads, "seq")
     received = lax.ppermute(send, "seq", [(i, i ^ 1) for i in range(count)])
+    pair = out_step(pair, ring // 2 - 1)
+    keep = tie((keep, *pair))[0]
     (terms,) = call(pair_body, [shape(dims, bf16)], [keep, received], "pair_add")
-    pair = tie((*pair, terms))[:2]
-    pair = out_step(pair, ring // 2 - 1)
     pair = hop(pair)
     groups = [[2 * chip + core for chip in range(count // 2)] for core in range(2)]
     terms = lax.all_to_all(terms, "seq", 0, 0, axis_index_groups=groups, tiled=True)

time: 160 us -> 158 us (0.988)
  waiting for transfers between devices: 42.8 us -> 40.8 us
  other arithmetic: 9.24 us -> 11.2 us
    ppermute x8, waiting for transfers between devices: 22.5 us -> 18.6 us  [shift(): lax.ppermute(x, axis, [(i, (i + amount) % count) for i in range(count)])]
    all_gather x1, waiting for transfers between devices: 0.01 us -> 1.93 us  [per_device(): state_all = lax.all_gather(local_grads, 'seq')]
    concatenate x1, other arithmetic: 0.07 us -> 1.83 us  [out_step(): outs.append(jnp.concatenate(parts, axis=0))]
  transfers between devices with their start and end apart: 13 -> 13, of which waited for: 6 -> 7; matrix products, arithmetic and copies ran while one was open for 6% -> 7% of each run, Pallas kernels for 21% -> 21%
where the time goes in v7:
time: 158 us; the launch traced here: 157 us
  Pallas kernels  50.5 us (32%)
  waiting for transfers between devices  40.8 us (26%)
  starting transfers between devices  21.9 us (14%)
  blocking collectives  17.7 us (11%)
  between operations  14.1 us (9%)
  other arithmetic  11.2 us (7%)
    pallas_call x9, Pallas kernels, call(): pl.pallas_call(body, out_shape=tuple(outs), in_specs=specs, out_specs=tup...  50.5 us
    ppermute x8, waiting for transfers between devices, shift(): lax.ppermute(x, axis, [(i, (i + amount) % count) for i in range(count)])  18.6 us
    all_to_all x1, blocking collectives, exchange(): return lax.all_to_all(parts, 'seq', 0, 0, tiled=True)  17.7 us
    all_gather x1, waiting for transfers between devices, per_device(): gathered = lax.all_gather(grad_out, 'head')  11.2 us
    ppermute x8, starting transfers between devices, shift(): lax.ppermute(x, axis, [(i, (i + amount) % count) for i in range(count)])  10.8 us
    all_to_all x1, waiting for transfers between devices, exchange(): return lax.all_to_all(parts, 'seq', 0, 0, tiled=True)  8.44 us
    all_to_all x1, starting transfers between devices, per_device(): lax.all_to_all(terms, 'seq', 0, 0, axis_index_groups=groups, tiled=True)  6.58 us
    convert_element_type x2, other arithmetic, out_step(): outs.append((term + got).astype(bf16))  5.16 us
  transfers between devices with their start and end apart: 13, of which 7 were waited for; matrix products, arithmetic and copies ran while one was open for 7% of the time, Pallas kernels for 21%

profile of v7, /device:TPU:1, one launch (start us, length us, event | category | flops | bytes accessed | tf_op | source)
XLA Modules:
  0.0 156.9 jit_solution(942263055938316826)
XLA Ops:
  7.9 2.3 %state.1 = f32[4,128,128]{2,1,0:T(8,128)} custom-call(bf16[512,512]{1,0:T(8,128)(2,1)} %k.5, bf16[512,512]{1,0:T(8,128)(2,1)} %v.5), custom_call_target="tpu_custom_call" | custom-call | flops 1000000000 | bytes 1000 | tf_op jit(solution)/shard_map/state/pallas_call | solution.py:42
  10.2 17.7 %all_to_all.15.parts = f32[32,16,128]{2,1,0:T(8,128)} all-to-all(f32[32,16,128]{2,1,0:T(8,128)} %bitcast.41), channel_id=1, replica_groups=mesh['seq'=32,'head'=8] {'seq'}, dimensions={0} | all-to-all | bytes 524288 | tf_op jit(solution)/shard_map/all_to_all | solution.py:244
  29.5 3.7 %all-to-all-start.1 = ((f32[32,16,128]{2,1,0:T(8,128)}), f32[32,16,128]{2,1,0:T(8,128)S(1)}, u32[]{:S(2)}, u32[]{:S(2)}) async-start(f32[32,16,128]{2,1,0:T(8,128)} %prefix.1), calls=%async_computation.1 | async-start | bytes 524288 | tf_op jit(solution)/shard_map/all_to_all | solution.py:244
  33.9 8.4 %all-to-all-done.1 = f32[32,16,128]{2,1,0:T(8,128)S(1)} async-done(((f32[32,16,128]{2,1,0:T(8,128)}), f32[32,16,128]{2,1,0:T(8,128)S(1)}, u32[]{:S(2)}, u32[]{:S(2)}) %all-to-all-start.1) | async-done | bytes 262176 | tf_op jit(solution)/shard_map/all_to_all | solution.py:244
  43.0 5.0 %forward.1 = (bf16[512,512]{1,0:T(8,128)(2,1)}, bf16[512,512]{1,0:T(8,128)(2,1)}, f32[512,512]{1,0:T(8,128)}) custom-call(bf16[512,512]{1,0:T(8,128)(2,1)} %q.5, bf16[512,512]{1,0:T(8,128)(2,1)} %k.5, bf16[512,512]{1,0:T(8,128)(2,1)} %v.5, f32[4,128,128]{2,1,0:T(8,128)} %bitcast.39), custom_call_target="tpu_custom_call" | custom-call | flops 1000000000 | bytes 1000 | tf_op jit(solution)/shard_map/forward/pallas_call | solution.py:42
  48.0 9.2 %out_terms.1 = (f32[8,512,512]{2,1,0:T(8,128)}, bf16[256,512]{1,0:T(8,128)(2,1)}, bf16[256,512]{1,0:T(8,128)(2,1)}, bf16[256,512]{1,0:T(8,128)(2,1)}, bf16[256,512]{1,0:T(8,128)(2,1)}) custom-call(s32[3]{0:T(128)} %pad_add_fusion.me, bf16[512,512]{1,0:T(8,128)(2,1)} %get-tuple-element.47.attn, bf16[4096,512]{1,0:T(8,128)(2,1)} %w.3), custom_call_target="tpu_custom_call" | custom-call | flops 1000000000 | bytes 1000 | tf_op jit(solution)/shard_map/out_terms/pallas_call | solution.py:42
  57.3 11.2 %all-gather.5.cloned.1.call-done = bf16[4096,512]{1,0:T(8,128)(2,1)} async-done(((bf16[512,512]{1,0:T(8,128)(2,1)}), bf16[4096,512]{1,0:T(8,128)(2,1)}) %all-gather.5.cloned.1.call-update) | async-done | bytes 4194320 | tf_op jit(solution)/shard_map/all_gather | solution.py:271
  68.4 10.5 %project.1 = (bf16[512,512]{1,0:T(8,128)(2,1)}, bf16[4,128,128]{2,1,0:T(8,128)(2,1)}, bf16[16,512,128]{2,1,0:T(8,128)(2,1)}, bf16[16,512,128]{2,1,0:T(8,128)(2,1)}) custom-call(s32[3]{0:T(128)} %pad_add_fusion.me, bf16[8,512,512]{2,1,0:T(8,128)(2,1)} %bitcast.38, bf16[4096,512]{1,0:T(8,128)(2,1)} %w.3, f32[512,512]{1,0:T(8,128)} %get-tuple-element.68.mixed, ...), custom_call_target="tpu_custom_call" | custom-call | flops 1000000000 | bytes 1000 | tf_op jit(solution)/shard_map/project/pallas_call | solution.py:42
  79.8 2.7 %collective-permute-start.1 = (bf16[256,512]{1,0:T(8,128)(2,1)S(1)}, bf16[256,512]{1,0:T(8,128)(2,1)S(1)}, u32[]{:S(2)}, u32[]{:S(2)}) collective-permute-start(bf16[256,512]{1,0:T(8,128)(2,1)S(1)} %copy-done.2), channel_id=1, source_target_pairs={{0,7},{1,0},{2,1},{3,2},{4,3},{5,4},{6,5},{7,6},{8,15},{9,8},{10,9... | collective-permute-start | bytes 786440 | tf_op jit(solution)/shard_map/ppermute | solution.py:224
  82.5 6.4 %collective-permute-done = bf16[256,512]{1,0:T(8,128)(2,1)S(1)} collective-permute-done((bf16[256,512]{1,0:T(8,128)(2,1)S(1)}, bf16[256,512]{1,0:T(8,128)(2,1)S(1)}, u32[]{:S(2)}, u32[]{:S(2)}) %collective-permute-start) | collective-permute-done | bytes 262176 | tf_op jit(solution)/shard_map/ppermute | solution.py:224
  92.6 2.1 %collective-permute-start.3 = (bf16[512,512]{1,0:T(8,128)(2,1)S(1)}, bf16[512,512]{1,0:T(8,128)(2,1)}, u32[]{:S(2)}, u32[]{:S(2)}) collective-permute-start(bf16[512,512]{1,0:T(8,128)(2,1)S(1)} %get-tuple-element.60), channel_id=1, source_target_pairs={{0,7},{1,0},{2,1},{3,2},{4,3},{5,4},{6,5},{7,6},{8,15},{9,8},{10,9... | collective-permute-start | bytes 1572872 | tf_op jit(solution)/shard_map/ppermute | solution.py:224
  94.8 4.0 %pair_add.1 = bf16[16,512,128]{2,1,0:T(8,128)(2,1)} custom-call(bf16[16,512,128]{2,1,0:T(8,128)(2,1)} %get-tuple-element.86.keep, bf16[16,512,128]{2,1,0:T(8,128)(2,1)} %collective-permute-done.8.received), custom_call_target="tpu_custom_call" | custom-call | flops 1000000000 | bytes 1000 | tf_op jit(solution)/shard_map/pair_add/pallas_call | solution.py:42
  98.8 6.6 %all-to-all-start.2 = ((bf16[16,512,128]{2,1,0:T(8,128)(2,1)}), bf16[16,512,128]{2,1,0:T(8,128)(2,1)}, u32[]{:S(2)}, u32[]{:S(2)}) async-start(bf16[16,512,128]{2,1,0:T(8,128)(2,1)} %pair_add.1), calls=%async_computation.2 | async-start | bytes 4194304 | tf_op jit(solution)/shard_map/all_to_all | solution.py:317
  106.2 3.0 %fusion.1 = (bf16[512,512]{1,0:T(8,128)(2,1)S(1)}, bf16[512,512]{1,0:T(8,128)(2,1)}) fusion(bf16[512,512]{1,0:T(8,128)(2,1)} %collective-permute-done.3, f32[8,512,512]{2,1,0:T(8,128)} %get-tuple-element.48, bf16[512,512]{1,0:T(8,128)(2,1)} %collective-permute-done.2), kind=kLoop, calls=%fused_computation.3 | loop fusion | flops 1572864 | bytes 4194304 | tf_op jit(solution)/shard_map/convert_element_type | solution.py:268
  109.1 2.7 %collective-permute-start.5 = (bf16[512,512]{1,0:T(8,128)(2,1)S(1)}, bf16[512,512]{1,0:T(8,128)(2,1)}, u32[]{:S(2)}, u32[]{:S(2)}) collective-permute-start(bf16[512,512]{1,0:T(8,128)(2,1)S(1)} %get-tuple-element.64), channel_id=1, source_target_pairs={{0,7},{1,0},{2,1},{3,2},{4,3},{5,4},{6,5},{7,6},{8,15},{9,8},{10,9... | collective-permute-start | bytes 1572872 | tf_op jit(solution)/shard_map/ppermute | solution.py:224
  111.8 8.4 %backward.1 = (bf16[512,512]{1,0:T(8,128)(2,1)}, f32[512,512]{1,0:T(8,128)}, f32[512,512]{1,0:T(8,128)}) custom-call(bf16[512,512]{1,0:T(8,128)(2,1)} %q.5, bf16[512,512]{1,0:T(8,128)(2,1)} %k.5, bf16[512,512]{1,0:T(8,128)(2,1)} %v.5, bf16[512,512]{1,0:T(8,128)(2,1)} %get-tuple-element.71.d_mixed, f32[4,128,128]{2,1,0:T(8,128)} %bitcast.40), custom_call_target="tpu_custom_call" | custom-call | flops 1000000000 | bytes 1000 | tf_op jit(solution)/shard_map/backward/pallas_call | solution.py:42
  120.2 2.1 %collective-permute-done.4 = bf16[512,512]{1,0:T(8,128)(2,1)} collective-permute-done((bf16[512,512]{1,0:T(8,128)(2,1)}, bf16[512,512]{1,0:T(8,128)(2,1)}, u32[]{:S(2)}, u32[]{:S(2)}) %collective-permute-start.4) | collective-permute-done | bytes 524320 | tf_op jit(solution)/shard_map/ppermute | solution.py:224
  122.3 2.2 %fusion = (bf16[512,512]{1,0:T(8,128)(2,1)S(1)}, bf16[512,512]{1,0:T(8,128)(2,1)S(1)}) fusion(bf16[512,512]{1,0:T(8,128)(2,1)} %collective-permute-done.5, f32[8,512,512]{2,1,0:T(8,128)} %get-tuple-element.48, bf16[512,512]{1,0:T(8,128)(2,1)} %collective-permute-done.4), kind=kLoop, calls=%fused_computation.1 | loop fusion | flops 1572864 | bytes 4194304 | tf_op jit(solution)/shard_map/convert_element_type | solution.py:268
  124.6 2.7 %collective-permute-start.7 = (bf16[512,512]{1,0:T(8,128)(2,1)S(1)}, bf16[512,512]{1,0:T(8,128)(2,1)S(1)}, u32[]{:S(2)}, u32[]{:S(2)}) collective-permute-start(bf16[512,512]{1,0:T(8,128)(2,1)S(1)} %get-tuple-element.76), channel_id=1, source_target_pairs={{0,7},{1,0},{2,1},{3,2},{4,3},{5,4},{6,5},{7,6},{8,15},{9,8},{10,9... | collective-permute-start | bytes 1572872 | tf_op jit(solution)/shard_map/ppermute | solution.py:224
  127.3 9.3 %collective-permute-done.6 = bf16[512,512]{1,0:T(8,128)(2,1)S(1)} collective-permute-done((bf16[512,512]{1,0:T(8,128)(2,1)S(1)}, bf16[512,512]{1,0:T(8,128)(2,1)S(1)}, u32[]{:S(2)}, u32[]{:S(2)}) %collective-permute-start.6) | collective-permute-done | bytes 524320 | tf_op jit(solution)/shard_map/ppermute | solution.py:224
  136.6 2.2 %fusion.5 = bf16[512,512]{1,0:T(8,128)(2,1)} fusion(bf16[512,512]{1,0:T(8,128)(2,1)S(1)} %collective-permute-done.7, bf16[512,512]{1,0:T(8,128)(2,1)S(1)} %collective-permute-done.6, f32[8,512,512]{2,1,0:T(8,128)} %get-tuple-element.48), kind=kLoop, calls=%fused_computation.10 | loop fusion | flops 1310720 | bytes 2621440 | tf_op jit(solution)/shard_map/convert_element_type | solution.py:342
  138.8 2.6 %weight_sum.1 = f32[128,512]{1,0:T(8,128)} custom-call(bf16[16,512,128]{2,1,0:T(8,128)(2,1)} %all-to-all-done.2.parts), custom_call_target="tpu_custom_call" | custom-call | flops 1000000000 | bytes 1000 | tf_op jit(solution)/shard_map/weight_sum/pallas_call | solution.py:42
  141.4 1.9 %all-gather.7.cloned.1.call-done = bf16[128,128,128]{2,1,0:T(8,128)(2,1)} async-done(((bf16[4,128,128]{2,1,0:T(8,128)(2,1)}), bf16[128,128,128]{2,1,0:T(8,128)(2,1)}) %all-gather.7.cloned.1.call-update) | async-done | bytes 4194320 | tf_op jit(solution)/shard_map/all_gather | solution.py:310
  143.3 6.7 %finish.1 = (bf16[512,512]{1,0:T(8,128)(2,1)}, bf16[512,512]{1,0:T(8,128)(2,1)}) custom-call(s32[3]{0:T(128)} %pad_add_fusion.me, bf16[512,512]{1,0:T(8,128)(2,1)} %k.5, bf16[512,512]{1,0:T(8,128)(2,1)} %v.5, f32[512,512]{1,0:T(8,128)} %get-tuple-element.79.part_k, f32[512,512]{1,0:T(8,128)} %get-tuple-element.80.part_v, bf16[32,4,128,128]{3,2,1,0:T(8,128)(2,1)} %bitcast.37), custom_call_target="tpu_custom_call" | custom-call | flops 1000000000 | bytes 1000 | tf_op jit(solution)/shard_map/finish/pallas_call | solution.py:42
  (28 shorter events, 9.2 us)
Async XLA Ops:
  7.2 61.3 %all-gather.5.cloned.1.call-start = ((), (), s32[]{:S(2)}) async-start(), calls=%async_computation.3 | async-start | bytes 4718592 | tf_op jit(solution)/shard_map/all_gather | solution.py:271
  29.5 12.8 %all-to-all-start.1 = ((f32[32,16,128]{2,1,0:T(8,128)}), f32[32,16,128]{2,1,0:T(8,128)S(1)}, u32[]{:S(2)}, u32[]{:S(2)}) async-start(f32[32,16,128]{2,1,0:T(8,128)} %prefix.1), calls=%async_computation.1 | async-start | bytes 524288 | tf_op jit(solution)/shard_map/all_to_all | solution.py:244
  33.2 110.1 %all-gather.7.cloned.1.call-start = ((), (), s32[]{:S(2)}) async-start(), calls=%async_computation.4 | async-start | bytes 4325376 | tf_op jit(solution)/shard_map/all_gather | solution.py:310
  42.3 0.7 copy-start
  68.4 11.3 %copy-start.3 = (bf16[256,512]{1,0:T(8,128)(2,1)S(1)}, bf16[256,512]{1,0:T(8,128)(2,1)}, u32[]{:S(2)}) copy-start(bf16[256,512]{1,0:T(8,128)(2,1)} %get-tuple-element.53) | copy-start | bytes 786436
  68.4 11.3 %copy-start.2 = (bf16[256,512]{1,0:T(8,128)(2,1)S(1)}, bf16[256,512]{1,0:T(8,128)(2,1)}, u32[]{:S(2)}) copy-start(bf16[256,512]{1,0:T(8,128)(2,1)} %get-tuple-element.54) | copy-start | bytes 786436
  68.4 21.8 %copy-start.1 = (bf16[256,512]{1,0:T(8,128)(2,1)S(1)}, bf16[256,512]{1,0:T(8,128)(2,1)}, u32[]{:S(2)}) copy-start(bf16[256,512]{1,0:T(8,128)(2,1)} %get-tuple-element.56) | copy-start | bytes 786436
  79.0 15.8 %collective-permute-start.8 = (bf16[16,512,128]{2,1,0:T(8,128)(2,1)}, bf16[16,512,128]{2,1,0:T(8,128)(2,1)}, u32[]{:S(2)}, u32[]{:S(2)}) collective-permute-start(bf16[16,512,128]{2,1,0:T(8,128)(2,1)} %get-tuple-element.87), channel_id=1, source_target_pairs={{0,8},{8,0},{16,24},{24,16},{32,40},{40,32},{48,56},{56,48},{64,72... | collective-permute-start | bytes 6291464 | tf_op jit(solution)/shard_map/ppermute | solution.py:311
  79.8 9.1 %collective-permute-start = (bf16[256,512]{1,0:T(8,128)(2,1)S(1)}, bf16[256,512]{1,0:T(8,128)(2,1)S(1)}, u32[]{:S(2)}, u32[]{:S(2)}) collective-permute-start(bf16[256,512]{1,0:T(8,128)(2,1)S(1)} %copy-done.3), channel_id=1, source_target_pairs={{0,1},{1,2},{2,3},{3,4},{4,5},{5,6},{6,7},{7,0},{8,9},{9,10},{10,1... | collective-permute-start | bytes 786440 | tf_op jit(solution)/shard_map/ppermute | solution.py:224
  79.8 9.1 %collective-permute-start.1 = (bf16[256,512]{1,0:T(8,128)(2,1)S(1)}, bf16[256,512]{1,0:T(8,128)(2,1)S(1)}, u32[]{:S(2)}, u32[]{:S(2)}) collective-permute-start(bf16[256,512]{1,0:T(8,128)(2,1)S(1)} %copy-done.2), channel_id=1, source_target_pairs={{0,7},{1,0},{2,1},{3,2},{4,3},{5,4},{6,5},{7,6},{8,15},{9,8},{10,9... | collective-permute-start | bytes 786440 | tf_op jit(solution)/shard_map/ppermute | solution.py:224
  92.1 14.1 %collective-permute-start.2 = (bf16[512,512]{1,0:T(8,128)(2,1)}, bf16[512,512]{1,0:T(8,128)(2,1)}, u32[]{:S(2)}, u32[]{:S(2)}) collective-permute-start(bf16[512,512]{1,0:T(8,128)(2,1)} %get-tuple-element.59), channel_id=1, source_target_pairs={{0,1},{1,2},{2,3},{3,4},{4,5},{5,6},{6,7},{7,0},{8,9},{9,10},{10,1... | collective-permute-start | bytes 1572872 | tf_op jit(solution)/shard_map/ppermute | solution.py:224
  92.6 13.6 %collective-permute-start.3 = (bf16[512,512]{1,0:T(8,128)(2,1)S(1)}, bf16[512,512]{1,0:T(8,128)(2,1)}, u32[]{:S(2)}, u32[]{:S(2)}) collective-permute-start(bf16[512,512]{1,0:T(8,128)(2,1)S(1)} %get-tuple-element.60), channel_id=1, source_target_pairs={{0,7},{1,0},{2,1},{3,2},{4,3},{5,4},{6,5},{7,6},{8,15},{9,8},{10,9... | collective-permute-start | bytes 1572872 | tf_op jit(solution)/shard_map/ppermute | solution.py:224
  98.8 40.0 %all-to-all-start.2 = ((bf16[16,512,128]{2,1,0:T(8,128)(2,1)}), bf16[16,512,128]{2,1,0:T(8,128)(2,1)}, u32[]{:S(2)}, u32[]{:S(2)}) async-start(bf16[16,512,128]{2,1,0:T(8,128)(2,1)} %pair_add.1), calls=%async_computation.2 | async-start | bytes 4194304 | tf_op jit(solution)/shard_map/all_to_all | solution.py:317
  109.1 13.2 %collective-permute-start.4 = (bf16[512,512]{1,0:T(8,128)(2,1)}, bf16[512,512]{1,0:T(8,128)(2,1)}, u32[]{:S(2)}, u32[]{:S(2)}) collective-permute-start(bf16[512,512]{1,0:T(8,128)(2,1)} %get-tuple-element.63), channel_id=1, source_target_pairs={{0,1},{1,2},{2,3},{3,4},{4,5},{5,6},{6,7},{7,0},{8,9},{9,10},{10,1... | collective-permute-start | bytes 1572872 | tf_op jit(solution)/shard_map/ppermute | solution.py:224
  109.1 13.2 %collective-permute-start.5 = (bf16[512,512]{1,0:T(8,128)(2,1)S(1)}, bf16[512,512]{1,0:T(8,128)(2,1)}, u32[]{:S(2)}, u32[]{:S(2)}) collective-permute-start(bf16[512,512]{1,0:T(8,128)(2,1)S(1)} %get-tuple-element.64), channel_id=1, source_target_pairs={{0,7},{1,0},{2,1},{3,2},{4,3},{5,4},{6,5},{7,6},{8,15},{9,8},{10,9... | collective-permute-start | bytes 1572872 | tf_op jit(solution)/shard_map/ppermute | solution.py:224
  124.5 12.0 %collective-permute-start.6 = (bf16[512,512]{1,0:T(8,128)(2,1)S(1)}, bf16[512,512]{1,0:T(8,128)(2,1)S(1)}, u32[]{:S(2)}, u32[]{:S(2)}) collective-permute-start(bf16[512,512]{1,0:T(8,128)(2,1)S(1)} %get-tuple-element.75), channel_id=1, source_target_pairs={{0,1},{1,2},{2,3},{3,4},{4,5},{5,6},{6,7},{7,0},{8,9},{9,10},{10,1... | collective-permute-start | bytes 1572872 | tf_op jit(solution)/shard_map/ppermute | solution.py:224
  124.6 12.0 %collective-permute-start.7 = (bf16[512,512]{1,0:T(8,128)(2,1)S(1)}, bf16[512,512]{1,0:T(8,128)(2,1)S(1)}, u32[]{:S(2)}, u32[]{:S(2)}) collective-permute-start(bf16[512,512]{1,0:T(8,128)(2,1)S(1)} %get-tuple-element.76), channel_id=1, source_target_pairs={{0,7},{1,0},{2,1},{3,2},{4,3},{5,4},{6,5},{7,6},{8,15},{9,8},{10,9... | collective-permute-start | bytes 1572872 | tf_op jit(solution)/shard_map/ppermute | solution.py:224
Sparse Core Ops, SparseCore 0:
  9.8 58.6 all-gather.4
  79.1 64.1 all-gather.6
